TPU v7x, 256 devices: a whole 4x4x8 slice. The times are simulated.
256 devices in a mesh: pts: 256 (over y, z, x, core).
Axes of the slice: x: 4, y: 4, z: 8, core: 2. Of those that a mesh axis runs over, the one named last changes fastest.
Arguments:
- vectors: bfloat16 [4096, 8, 256], P('pts'), may hold values from -6 to 6
- leaf_basis: bfloat16 [4096, 64, 256], P('pts'), may hold values from -0.375 to 0.375
- leaf_transfer: bfloat16 [4096, 64, 64], P('pts'), may hold values from -0.1875 to 0.1875
- leaf_coupling: bfloat16 [4096, 64, 384], P('pts'), may hold values from -0.3125 to 0.3125
- near_tiles: bfloat16 [4096, 4, 256, 256], P('pts'), may hold values from -0.1875 to 0.1875
- tile_scale: float32 [4096, 4], P('pts'), may hold values from 0.3 to 3
- near_boxes: int32 [4096, 4], P('pts'), may hold values from 0 to 4095, as said below
- near_counts: int32 [4096], P('pts'), may hold values from 1 to 4, as said below
- far_boxes: int32 [4096, 6], P('pts'), may hold values from 0 to 4095, as said below
- level_up: float32 [256, 5, 64, 64], P('pts'), may hold values from -0.75 to 0.75
- level_coupling: float32 [256, 5, 64, 64], P('pts'), may hold values from -0.3125 to 0.3125
Outputs:
- product: float32 [4096, 8, 256], P('pts')
Inputs may be any that keep to these rules, and one draw needn't show every extreme that they name: Slot 0 of row b of near_boxes is b itself; every entry of a row on device d names a box on devices d - 7 to d + 7; all entries of slots 1 and up of near_boxes and all entries of far_boxes in the rows of one device d together name at most 4 distinct boxes of any one other device, and exactly 4 of some other device. `near_counts`: every device has a box with all 4 slots used. `far_boxes`: every entry of a row on device d names a box on devices d - 7 to d + 7.
All inputs are finite; a program needn't handle non-finite values.
Results may differ from a plain program's by a relative error of at most 0.009.
Values may be sent and summed in bfloat16 or wider, within the bound.
No kernel may reach another device: no remote copies, remote signals or barrier semaphores. Data moves between devices by JAX's collectives and lax.ppermute only.
A program may use at most 64 MiB of HBM per device.

v0:
```python
import jax
import jax.numpy as jnp
from jax import lax
from jax.sharding import PartitionSpec as P

UP = 5
REACH = 7


HIGH = lax.Precision.HIGHEST


def shifted(block, axis, distance):
    devices = range(lax.axis_size(axis))
    route = [(i - distance, i) for i in devices if i - distance in devices]
    return lax.ppermute(block, axis, route)


def swapped(block, axis, distance):
    count = lax.axis_size(axis)
    route = []
    for low in range(count):
        high = low | 1 << distance
        if high != low and high < count:
            route += [(low, high), (high, low)]
    return lax.ppermute(block, axis, route)


def per_device(
    vectors,
    leaf_basis,
    leaf_transfer,
    leaf_coupling,
    near_tiles,
    tile_scale,
    near_boxes,
    near_counts,
    far_boxes,
    level_up,
    level_coupling,
):
    box_count, rhs_count, leaf_size = vectors.shape
    rank_size = leaf_basis.shape[1]
    near_slots = near_tiles.shape[1]
    far_slots = far_boxes.shape[1]
    coefficients = jnp.einsum(
        "brj,bij->bri", vectors, leaf_basis, preferred_element_type=jnp.float32
    ).astype(jnp.bfloat16)
    flat_coeff = coefficients.reshape(box_count, rhs_count * rank_size)
    device = lax.axis_index("pts")
    own_pair = (vectors, flat_coeff)
    received = {}
    for offset in list(range(1, REACH + 1)) + list(range(-1, -REACH - 1, -1)):
        received[offset] = shifted((own_pair[0], own_pair[1]), "pts", offset)
    ordered = (
        [received[offset] for offset in range(REACH, 0, -1)]
        + [own_pair]
        + [received[-offset] for offset in range(1, REACH + 1)]
    )
    window_x = jnp.concatenate([member[0] for member in ordered], axis=0)
    window_q = jnp.concatenate([member[1] for member in ordered], axis=0)
    window_start = (device - REACH) * box_count
    gathered = jnp.take(window_x, near_boxes - window_start, axis=0)
    products = jnp.einsum(
        "bsrj,bsij->bsri", gathered, near_tiles, preferred_element_type=jnp.float32
    )
    in_use = (jnp.arange(near_slots, dtype=jnp.int32)[None, :] < near_counts[:, None]).astype(
        jnp.float32
    )
    near_part = jnp.einsum("bsri,bs->bri", products, tile_scale * in_use)
    far_coeff = jnp.take(window_q, far_boxes - window_start, axis=0).reshape(
        box_count, far_slots, rhs_count, rank_size
    )
    coupling = leaf_coupling.reshape(box_count, rank_size, far_slots, rank_size)
    leaf_far = jnp.einsum("bsrj,bisj->bri", far_coeff, coupling, preferred_element_type=jnp.float32)
    device_coeff = jnp.einsum(
        "brj,bjk->rk", coefficients, leaf_transfer, preferred_element_type=jnp.float32
    )
    lifted = jnp.einsum("rj,kjm->krm", device_coeff, level_up[0], precision=HIGH).reshape(
        UP, rhs_count * rank_size
    )
    far_field = jnp.zeros((rhs_count, rank_size), jnp.float32)
    running = lifted
    for bit_level in range(UP):
        partner_sums = swapped(running[bit_level:], "pts", bit_level)
        far_field = far_field + jnp.dot(
            partner_sums[0].reshape(rhs_count, rank_size),
            level_coupling[0, bit_level],
            precision=HIGH,
        )
        running = running.at[bit_level + 1 :].add(partner_sums[1:])
    far_rounded = far_field.astype(jnp.bfloat16)
    pushed = jnp.einsum(
        "rk,bjk->brj", far_rounded, leaf_transfer, preferred_element_type=jnp.float32
    )
    leaf_field = (leaf_far + pushed).astype(jnp.bfloat16)
    far_part = jnp.einsum(
        "bri,bij->brj", leaf_field, leaf_basis, preferred_element_type=jnp.float32
    )
    return far_part + near_part


def solution(mesh):
    placed = (
        P("pts", None, None),
        P("pts", None, None),
        P("pts", None, None),
        P("pts", None, None),
        P("pts", None, None, None),
        P("pts", None),
        P("pts", None),
        P("pts"),
        P("pts", None),
        P("pts", None, None, None),
        P("pts", None, None, None),
    )
    return jax.shard_map(
        per_device, mesh=mesh, in_specs=placed, out_specs=P("pts", None, None), check_vma=False
    )
```

profile of v0, /device:TPU:25, one launch (start us, length us, event | category | flops | bytes accessed | tf_op | source)
XLA Modules:
  0.0 140.0 jit_solution(2166714223844714472)
XLA Ops:
  0.0 1.0 copy-done
  1.0 1.1 convolution_convert_fusion
  2.2 4.1 %collective-permute-start = (bf16[16,512]{1,0:T(8,128)(2,1)S(1)}, bf16[16,512]{1,0:T(8,128)(2,1)S(1)}, u32[]{:S(2)}, u32[]{:S(2)}) collective-permute-start(bf16[16,512]{1,0:T(8,128)(2,1)S(1)} %reshape.120), channel_id=1, source_target_pairs={{0,7},{1,8},{2,9},{3,10},{4,11},{5,12},{6,13},{7,14},{8,15},{9,16}... | collective-permute-start | bytes 49160 | tf_op jit(solution)/shard_map/ppermute | solution.py:16
  6.3 4.4 %collective-permute-start.1 = (bf16[16,512]{1,0:T(8,128)(2,1)S(1)}, bf16[16,512]{1,0:T(8,128)(2,1)S(1)}, u32[]{:S(2)}, u32[]{:S(2)}) collective-permute-start(bf16[16,512]{1,0:T(8,128)(2,1)S(1)} %reshape.120), channel_id=1, source_target_pairs={{0,6},{1,7},{2,8},{3,9},{4,10},{5,11},{6,12},{7,13},{8,14},{9,15},... | collective-permute-start | bytes 49160 | tf_op jit(solution)/shard_map/ppermute | solution.py:16
  10.8 3.8 %collective-permute-start.2 = (bf16[16,512]{1,0:T(8,128)(2,1)S(1)}, bf16[16,512]{1,0:T(8,128)(2,1)S(1)}, u32[]{:S(2)}, u32[]{:S(2)}) collective-permute-start(bf16[16,512]{1,0:T(8,128)(2,1)S(1)} %reshape.120), channel_id=1, source_target_pairs={{0,5},{1,6},{2,7},{3,8},{4,9},{5,10},{6,11},{7,12},{8,13},{9,14},{... | collective-permute-start | bytes 49160 | tf_op jit(solution)/shard_map/ppermute | solution.py:16
  14.5 4.4 %collective-permute-start.3 = (bf16[16,512]{1,0:T(8,128)(2,1)S(1)}, bf16[16,512]{1,0:T(8,128)(2,1)S(1)}, u32[]{:S(2)}, u32[]{:S(2)}) collective-permute-start(bf16[16,512]{1,0:T(8,128)(2,1)S(1)} %reshape.120), channel_id=1, source_target_pairs={{0,4},{1,5},{2,6},{3,7},{4,8},{5,9},{6,10},{7,11},{8,12},{9,13},{1... | collective-permute-start | bytes 49160 | tf_op jit(solution)/shard_map/ppermute | solution.py:16
  18.9 1.2 fusion.33
  20.0 1.1 convolution_bitcast_fusion.2
  21.2 0.7 collective-permute-start.14
  24.5 1.8 %copy.25 = bf16[16,64,384]{1,2,0:T(8,128)(2,1)S(1)} copy(bf16[16,64,384]{2,1,0:T(8,128)(2,1)} %param.22) | data formatting | bytes 1572864 | tf_op jit(solution)/shard_map/reshape | solution.py:74
  26.6 3.7 %collective-permute-start.4 = (bf16[16,512]{1,0:T(8,128)(2,1)S(1)}, bf16[16,512]{1,0:T(8,128)(2,1)S(1)}, u32[]{:S(2)}, u32[]{:S(2)}) collective-permute-start(bf16[16,512]{1,0:T(8,128)(2,1)S(1)} %reshape.120), channel_id=1, source_target_pairs={{0,3},{1,4},{2,5},{3,6},{4,7},{5,8},{6,9},{7,10},{8,11},{9,12},{10... | collective-permute-start | bytes 49160 | tf_op jit(solution)/shard_map/ppermute | solution.py:16
  30.4 2.9 %collective-permute-start.5 = (bf16[16,512]{1,0:T(8,128)(2,1)S(1)}, bf16[16,512]{1,0:T(8,128)(2,1)S(1)}, u32[]{:S(2)}, u32[]{:S(2)}) collective-permute-start(bf16[16,512]{1,0:T(8,128)(2,1)S(1)} %reshape.120), channel_id=1, source_target_pairs={{0,2},{1,3},{2,4},{3,5},{4,6},{5,7},{6,8},{7,9},{8,10},{9,11},{10,... | collective-permute-start | bytes 49160 | tf_op jit(solution)/shard_map/ppermute | solution.py:16
  33.3 2.4 %collective-permute-start.6 = (bf16[16,512]{1,0:T(8,128)(2,1)S(1)}, bf16[16,512]{1,0:T(8,128)(2,1)S(1)}, u32[]{:S(2)}, u32[]{:S(2)}) collective-permute-start(bf16[16,512]{1,0:T(8,128)(2,1)S(1)} %reshape.120), channel_id=1, source_target_pairs={{0,1},{1,2},{2,3},{3,4},{4,5},{5,6},{6,7},{7,8},{8,9},{9,10},{10,1... | collective-permute-start | bytes 49160 | tf_op jit(solution)/shard_map/ppermute | solution.py:16
  35.8 1.9 %collective-permute-start.7 = (bf16[16,512]{1,0:T(8,128)(2,1)S(1)}, bf16[16,512]{1,0:T(8,128)(2,1)S(1)}, u32[]{:S(2)}, u32[]{:S(2)}) collective-permute-start(bf16[16,512]{1,0:T(8,128)(2,1)S(1)} %reshape.120), channel_id=1, source_target_pairs={{1,0},{2,1},{3,2},{4,3},{5,4},{6,5},{7,6},{8,7},{9,8},{10,9},{11,1... | collective-permute-start | bytes 49160 | tf_op jit(solution)/shard_map/ppermute | solution.py:16
  37.7 6.5 %collective-permute-start.8 = (bf16[16,512]{1,0:T(8,128)(2,1)S(1)}, bf16[16,512]{1,0:T(8,128)(2,1)S(1)}, u32[]{:S(2)}, u32[]{:S(2)}) collective-permute-start(bf16[16,512]{1,0:T(8,128)(2,1)S(1)} %reshape.120), channel_id=1, source_target_pairs={{2,0},{3,1},{4,2},{5,3},{6,4},{7,5},{8,6},{9,7},{10,8},{11,9},{12,... | collective-permute-start | bytes 49160 | tf_op jit(solution)/shard_map/ppermute | solution.py:16
  44.3 3.7 %collective-permute-start.9 = (bf16[16,512]{1,0:T(8,128)(2,1)S(1)}, bf16[16,512]{1,0:T(8,128)(2,1)S(1)}, u32[]{:S(2)}, u32[]{:S(2)}) collective-permute-start(bf16[16,512]{1,0:T(8,128)(2,1)S(1)} %reshape.120), channel_id=1, source_target_pairs={{3,0},{4,1},{5,2},{6,3},{7,4},{8,5},{9,6},{10,7},{11,8},{12,9},{13... | collective-permute-start | bytes 49160 | tf_op jit(solution)/shard_map/ppermute | solution.py:16
  48.0 3.3 %collective-permute-start.10 = (bf16[16,512]{1,0:T(8,128)(2,1)S(1)}, bf16[16,512]{1,0:T(8,128)(2,1)S(1)}, u32[]{:S(2)}, u32[]{:S(2)}) collective-permute-start(bf16[16,512]{1,0:T(8,128)(2,1)S(1)} %reshape.120), channel_id=1, source_target_pairs={{4,0},{5,1},{6,2},{7,3},{8,4},{9,5},{10,6},{11,7},{12,8},{13,9},{1... | collective-permute-start | bytes 49160 | tf_op jit(solution)/shard_map/ppermute | solution.py:16
  51.4 2.8 %collective-permute-start.11 = (bf16[16,512]{1,0:T(8,128)(2,1)S(1)}, bf16[16,512]{1,0:T(8,128)(2,1)S(1)}, u32[]{:S(2)}, u32[]{:S(2)}) collective-permute-start(bf16[16,512]{1,0:T(8,128)(2,1)S(1)} %reshape.120), channel_id=1, source_target_pairs={{5,0},{6,1},{7,2},{8,3},{9,4},{10,5},{11,6},{12,7},{13,8},{14,9},{... | collective-permute-start | bytes 49160 | tf_op jit(solution)/shard_map/ppermute | solution.py:16
  54.2 2.6 %collective-permute-start.12 = (bf16[16,512]{1,0:T(8,128)(2,1)S(1)}, bf16[16,512]{1,0:T(8,128)(2,1)S(1)}, u32[]{:S(2)}, u32[]{:S(2)}) collective-permute-start(bf16[16,512]{1,0:T(8,128)(2,1)S(1)} %reshape.120), channel_id=1, source_target_pairs={{6,0},{7,1},{8,2},{9,3},{10,4},{11,5},{12,6},{13,7},{14,8},{15,9},... | collective-permute-start | bytes 49160 | tf_op jit(solution)/shard_map/ppermute | solution.py:16
  56.8 5.0 %collective-permute-start.13 = (bf16[16,512]{1,0:T(8,128)(2,1)S(1)}, bf16[16,512]{1,0:T(8,128)(2,1)S(1)}, u32[]{:S(2)}, u32[]{:S(2)}) collective-permute-start(bf16[16,512]{1,0:T(8,128)(2,1)S(1)} %reshape.120), channel_id=1, source_target_pairs={{7,0},{8,1},{9,2},{10,3},{11,4},{12,5},{13,6},{14,7},{15,8},{16,9}... | collective-permute-start | bytes 49160 | tf_op jit(solution)/shard_map/ppermute | solution.py:16
  61.8 1.9 %collective-permute-start.19 = (bf16[16,8,256]{2,1,0:T(8,128)(2,1)}, bf16[16,8,256]{2,1,0:T(8,128)(2,1)S(1)}, u32[]{:S(2)}, u32[]{:S(2)}) collective-permute-start(bf16[16,8,256]{2,1,0:T(8,128)(2,1)} %param.19), channel_id=1, source_target_pairs={{0,7},{1,8},{2,9},{3,10},{4,11},{5,12},{6,13},{7,14},{8,15},{9,16}... | collective-permute-start | bytes 196616 | tf_op jit(solution)/shard_map/ppermute | solution.py:16
  63.8 2.6 %collective-permute-start.20 = (bf16[16,8,256]{2,1,0:T(8,128)(2,1)}, bf16[16,8,256]{2,1,0:T(8,128)(2,1)S(1)}, u32[]{:S(2)}, u32[]{:S(2)}) collective-permute-start(bf16[16,8,256]{2,1,0:T(8,128)(2,1)} %param.19), channel_id=1, source_target_pairs={{0,6},{1,7},{2,8},{3,9},{4,10},{5,11},{6,12},{7,13},{8,14},{9,15},... | collective-permute-start | bytes 196616 | tf_op jit(solution)/shard_map/ppermute | solution.py:16
  66.4 5.2 %collective-permute-start.21 = (bf16[16,8,256]{2,1,0:T(8,128)(2,1)}, bf16[16,8,256]{2,1,0:T(8,128)(2,1)S(1)}, u32[]{:S(2)}, u32[]{:S(2)}) collective-permute-start(bf16[16,8,256]{2,1,0:T(8,128)(2,1)} %param.19), channel_id=1, source_target_pairs={{0,5},{1,6},{2,7},{3,8},{4,9},{5,10},{6,11},{7,12},{8,13},{9,14},{... | collective-permute-start | bytes 196616 | tf_op jit(solution)/shard_map/ppermute | solution.py:16
  71.6 3.5 %collective-permute-start.22 = (bf16[16,8,256]{2,1,0:T(8,128)(2,1)}, bf16[16,8,256]{2,1,0:T(8,128)(2,1)S(1)}, u32[]{:S(2)}, u32[]{:S(2)}) collective-permute-start(bf16[16,8,256]{2,1,0:T(8,128)(2,1)} %param.19), channel_id=1, source_target_pairs={{0,4},{1,5},{2,6},{3,7},{4,8},{5,9},{6,10},{7,11},{8,12},{9,13},{1... | collective-permute-start | bytes 196616 | tf_op jit(solution)/shard_map/ppermute | solution.py:16
  75.2 0.8 gather_fusion
  76.1 0.7 convolution_bitcast_fusion.1
  76.8 0.9 collective-permute-done.15
  77.7 3.0 %collective-permute-start.16 = (f32[3,512]{1,0:T(4,128)S(1)}, f32[3,512]{1,0:T(4,128)S(1)}, u32[]{:S(2)}, u32[]{:S(2)}) collective-permute-start(f32[3,512]{1,0:T(4,128)S(1)} %slice_add_fusion), channel_id=1, source_target_pairs={{0,4},{4,0},{1,5},{5,1},{2,6},{6,2},{3,7},{7,3},{8,12},{12,8},{9,1... | collective-permute-start | bytes 18440 | tf_op jit(solution)/shard_map/ppermute | solution.py:26
  80.8 0.9 fusion.23
  81.8 1.7 %collective-permute-start.17 = (f32[2,512]{1,0:T(2,128)S(1)}, f32[2,512]{1,0:T(2,128)S(1)}, u32[]{:S(2)}, u32[]{:S(2)}) collective-permute-start(f32[2,512]{1,0:T(2,128)S(1)} %slice_add_fusion.2), channel_id=1, source_target_pairs={{0,8},{8,0},{1,9},{9,1},{2,10},{10,2},{3,11},{11,3},{4,12},{12,4},... | collective-permute-start | bytes 12296 | tf_op jit(solution)/shard_map/ppermute | solution.py:26
  83.6 0.9 fusion.21
  84.5 3.3 %collective-permute-start.18 = (f32[1,512]{1,0:T(1,128)S(1)}, f32[1,512]{1,0:T(1,128)S(1)}, u32[]{:S(2)}, u32[]{:S(2)}) collective-permute-start(f32[1,512]{1,0:T(1,128)S(1)} %get-tuple-element.58), channel_id=1, source_target_pairs={{0,16},{16,0},{1,17},{17,1},{2,18},{18,2},{3,19},{19,3},{4,20},{20... | collective-permute-start | bytes 6152 | tf_op jit(solution)/shard_map/ppermute | solution.py:26
  87.9 0.9 fusion.19
  88.8 7.6 %collective-permute-start.23 = (bf16[16,8,256]{2,1,0:T(8,128)(2,1)}, bf16[16,8,256]{2,1,0:T(8,128)(2,1)S(1)}, u32[]{:S(2)}, u32[]{:S(2)}) collective-permute-start(bf16[16,8,256]{2,1,0:T(8,128)(2,1)} %param.19), channel_id=1, source_target_pairs={{0,3},{1,4},{2,5},{3,6},{4,7},{5,8},{6,9},{7,10},{8,11},{9,12},{10... | collective-permute-start | bytes 196616 | tf_op jit(solution)/shard_map/ppermute | solution.py:16
  97.7 0.9 fusion.17
  98.6 0.9 fusion.6
  99.5 2.2 %collective-permute-start.24 = (bf16[16,8,256]{2,1,0:T(8,128)(2,1)}, bf16[16,8,256]{2,1,0:T(8,128)(2,1)S(1)}, u32[]{:S(2)}, u32[]{:S(2)}) collective-permute-start(bf16[16,8,256]{2,1,0:T(8,128)(2,1)} %param.19), channel_id=1, source_target_pairs={{0,2},{1,3},{2,4},{3,5},{4,6},{5,7},{6,8},{7,9},{8,10},{9,11},{10,... | collective-permute-start | bytes 196616 | tf_op jit(solution)/shard_map/ppermute | solution.py:16
  101.8 1.9 %collective-permute-start.25 = (bf16[16,8,256]{2,1,0:T(8,128)(2,1)}, bf16[16,8,256]{2,1,0:T(8,128)(2,1)S(1)}, u32[]{:S(2)}, u32[]{:S(2)}) collective-permute-start(bf16[16,8,256]{2,1,0:T(8,128)(2,1)} %param.19), channel_id=1, source_target_pairs={{0,1},{1,2},{2,3},{3,4},{4,5},{5,6},{6,7},{7,8},{8,9},{9,10},{10,1... | collective-permute-start | bytes 196616 | tf_op jit(solution)/shard_map/ppermute | solution.py:16
  103.7 2.4 %collective-permute-start.26 = (bf16[16,8,256]{2,1,0:T(8,128)(2,1)}, bf16[16,8,256]{2,1,0:T(8,128)(2,1)S(1)}, u32[]{:S(2)}, u32[]{:S(2)}) collective-permute-start(bf16[16,8,256]{2,1,0:T(8,128)(2,1)} %param.19), channel_id=1, source_target_pairs={{1,0},{2,1},{3,2},{4,3},{5,4},{6,5},{7,6},{8,7},{9,8},{10,9},{11,1... | collective-permute-start | bytes 196616 | tf_op jit(solution)/shard_map/ppermute | solution.py:16
  106.2 7.3 %collective-permute-start.27 = (bf16[16,8,256]{2,1,0:T(8,128)(2,1)}, bf16[16,8,256]{2,1,0:T(8,128)(2,1)S(1)}, u32[]{:S(2)}, u32[]{:S(2)}) collective-permute-start(bf16[16,8,256]{2,1,0:T(8,128)(2,1)} %param.19), channel_id=1, source_target_pairs={{2,0},{3,1},{4,2},{5,3},{6,4},{7,5},{8,6},{9,7},{10,8},{11,9},{12,... | collective-permute-start | bytes 196616 | tf_op jit(solution)/shard_map/ppermute | solution.py:16
  113.5 2.6 %collective-permute-start.28 = (bf16[16,8,256]{2,1,0:T(8,128)(2,1)S(1)}, bf16[16,8,256]{2,1,0:T(8,128)(2,1)S(1)}, u32[]{:S(2)}, u32[]{:S(2)}) collective-permute-start(bf16[16,8,256]{2,1,0:T(8,128)(2,1)S(1)} %copy-done.2), channel_id=1, source_target_pairs={{3,0},{4,1},{5,2},{6,3},{7,4},{8,5},{9,6},{10,7},{11,8},{12,9},{13... | collective-permute-start | bytes 196616 | tf_op jit(solution)/shard_map/ppermute | solution.py:16
  116.1 4.3 %collective-permute-start.29 = (bf16[16,8,256]{2,1,0:T(8,128)(2,1)S(1)}, bf16[16,8,256]{2,1,0:T(8,128)(2,1)S(1)}, u32[]{:S(2)}, u32[]{:S(2)}) collective-permute-start(bf16[16,8,256]{2,1,0:T(8,128)(2,1)S(1)} %copy-done.2), channel_id=1, source_target_pairs={{4,0},{5,1},{6,2},{7,3},{8,4},{9,5},{10,6},{11,7},{12,8},{13,9},{1... | collective-permute-start | bytes 196616 | tf_op jit(solution)/shard_map/ppermute | solution.py:16
  120.5 2.0 %collective-permute-start.30 = (bf16[16,8,256]{2,1,0:T(8,128)(2,1)S(1)}, bf16[16,8,256]{2,1,0:T(8,128)(2,1)S(1)}, u32[]{:S(2)}, u32[]{:S(2)}) collective-permute-start(bf16[16,8,256]{2,1,0:T(8,128)(2,1)S(1)} %copy-done.2), channel_id=1, source_target_pairs={{5,0},{6,1},{7,2},{8,3},{9,4},{10,5},{11,6},{12,7},{13,8},{14,9},{... | collective-permute-start | bytes 196616 | tf_op jit(solution)/shard_map/ppermute | solution.py:16
  122.5 3.6 %collective-permute-start.31 = (bf16[16,8,256]{2,1,0:T(8,128)(2,1)S(1)}, bf16[16,8,256]{2,1,0:T(8,128)(2,1)S(1)}, u32[]{:S(2)}, u32[]{:S(2)}) collective-permute-start(bf16[16,8,256]{2,1,0:T(8,128)(2,1)S(1)} %copy-done.2), channel_id=1, source_target_pairs={{6,0},{7,1},{8,2},{9,3},{10,4},{11,5},{12,6},{13,7},{14,8},{15,9},... | collective-permute-start | bytes 196616 | tf_op jit(solution)/shard_map/ppermute | solution.py:16
  126.1 3.3 %collective-permute-start.32 = (bf16[16,8,256]{2,1,0:T(8,128)(2,1)S(1)}, bf16[16,8,256]{2,1,0:T(8,128)(2,1)S(1)}, u32[]{:S(2)}, u32[]{:S(2)}) collective-permute-start(bf16[16,8,256]{2,1,0:T(8,128)(2,1)S(1)} %copy-done.2), channel_id=1, source_target_pairs={{7,0},{8,1},{9,2},{10,3},{11,4},{12,5},{13,6},{14,7},{15,8},{16,9}... | collective-permute-start | bytes 196616 | tf_op jit(solution)/shard_map/ppermute | solution.py:16
  129.6 2.7 %collective-permute-done.32 = bf16[16,8,256]{2,1,0:T(8,128)(2,1)S(1)} collective-permute-done((bf16[16,8,256]{2,1,0:T(8,128)(2,1)S(1)}, bf16[16,8,256]{2,1,0:T(8,128)(2,1)S(1)}, u32[]{:S(2)}, u32[]{:S(2)}) %collective-permute-start.32) | collective-permute-done | bytes 65568 | tf_op jit(solution)/shard_map/ppermute | solution.py:16
  132.9 5.7 %fusion.9 = bf16[16,4,8,256]{3,2,1,0:T(8,128)(2,1)S(1)} fusion(bf16[16,4,256,256]{3,2,1,0:T(8,128)(2,1)} %param.23, bf16[16,4,8,256]{3,2,1,0:T(8,128)(2,1)S(1)} %bitcast.57, pred[16,4]{1,0:T(8,128)(4,1)S(1)} %copy.18), kind=kOutput, calls=%fused_computation.17 | convolution fusion | flops 67239936 | bytes 8912960 | tf_op jit(solution)/shard_map/bsrj,bsij->bsri/dot_general | solution.py:64
  138.9 1.1 convolution_add_fusion
  (100 shorter events, 6.1 us)
Async XLA Ops:
  0.0 1.0 copy-start
  0.0 113.5 %copy-start.2 = (bf16[16,8,256]{2,1,0:T(8,128)(2,1)S(1)}, bf16[16,8,256]{2,1,0:T(8,128)(2,1)}, u32[]{:S(2)}) copy-start(bf16[16,8,256]{2,1,0:T(8,128)(2,1)} %param.19) | copy-start | bytes 196612
  2.2 28.2 %collective-permute-start = (bf16[16,512]{1,0:T(8,128)(2,1)S(1)}, bf16[16,512]{1,0:T(8,128)(2,1)S(1)}, u32[]{:S(2)}, u32[]{:S(2)}) collective-permute-start(bf16[16,512]{1,0:T(8,128)(2,1)S(1)} %reshape.120), channel_id=1, source_target_pairs={{0,7},{1,8},{2,9},{3,10},{4,11},{5,12},{6,13},{7,14},{8,15},{9,16}... | collective-permute-start | bytes 49160 | tf_op jit(solution)/shard_map/ppermute | solution.py:16
  6.3 27.0 %collective-permute-start.1 = (bf16[16,512]{1,0:T(8,128)(2,1)S(1)}, bf16[16,512]{1,0:T(8,128)(2,1)S(1)}, u32[]{:S(2)}, u32[]{:S(2)}) collective-permute-start(bf16[16,512]{1,0:T(8,128)(2,1)S(1)} %reshape.120), channel_id=1, source_target_pairs={{0,6},{1,7},{2,8},{3,9},{4,10},{5,11},{6,12},{7,13},{8,14},{9,15},... | collective-permute-start | bytes 49160 | tf_op jit(solution)/shard_map/ppermute | solution.py:16
  10.8 25.0 %collective-permute-start.2 = (bf16[16,512]{1,0:T(8,128)(2,1)S(1)}, bf16[16,512]{1,0:T(8,128)(2,1)S(1)}, u32[]{:S(2)}, u32[]{:S(2)}) collective-permute-start(bf16[16,512]{1,0:T(8,128)(2,1)S(1)} %reshape.120), channel_id=1, source_target_pairs={{0,5},{1,6},{2,7},{3,8},{4,9},{5,10},{6,11},{7,12},{8,13},{9,14},{... | collective-permute-start | bytes 49160 | tf_op jit(solution)/shard_map/ppermute | solution.py:16
  14.5 23.2 %collective-permute-start.3 = (bf16[16,512]{1,0:T(8,128)(2,1)S(1)}, bf16[16,512]{1,0:T(8,128)(2,1)S(1)}, u32[]{:S(2)}, u32[]{:S(2)}) collective-permute-start(bf16[16,512]{1,0:T(8,128)(2,1)S(1)} %reshape.120), channel_id=1, source_target_pairs={{0,4},{1,5},{2,6},{3,7},{4,8},{5,9},{6,10},{7,11},{8,12},{9,13},{1... | collective-permute-start | bytes 49160 | tf_op jit(solution)/shard_map/ppermute | solution.py:16
  21.2 5.4 %collective-permute-start.14 = (f32[5,512]{1,0:T(8,128)S(1)}, f32[5,512]{1,0:T(8,128)S(1)}, u32[]{:S(2)}, u32[]{:S(2)}) collective-permute-start(f32[5,512]{1,0:T(8,128)S(1)} %reshape.122), channel_id=1, source_target_pairs={{0,1},{1,0},{2,3},{3,2},{4,5},{5,4},{6,7},{7,6},{8,9},{9,8},{10,11... | collective-permute-start | bytes 30728 | tf_op jit(solution)/shard_map/ppermute | solution.py:26
  26.3 112.5 %copy-start.1 = (bf16[16,64,64]{2,1,0:T(8,128)(2,1)S(1)}, bf16[16,64,64]{2,1,0:T(8,128)(2,1)}, u32[]{:S(2)}) copy-start(bf16[16,64,64]{2,1,0:T(8,128)(2,1)} %param.21) | copy-start | bytes 393220
  26.6 17.7 %collective-permute-start.4 = (bf16[16,512]{1,0:T(8,128)(2,1)S(1)}, bf16[16,512]{1,0:T(8,128)(2,1)S(1)}, u32[]{:S(2)}, u32[]{:S(2)}) collective-permute-start(bf16[16,512]{1,0:T(8,128)(2,1)S(1)} %reshape.120), channel_id=1, source_target_pairs={{0,3},{1,4},{2,5},{3,6},{4,7},{5,8},{6,9},{7,10},{8,11},{9,12},{10... | collective-permute-start | bytes 49160 | tf_op jit(solution)/shard_map/ppermute | solution.py:16
  30.4 17.6 %collective-permute-start.5 = (bf16[16,512]{1,0:T(8,128)(2,1)S(1)}, bf16[16,512]{1,0:T(8,128)(2,1)S(1)}, u32[]{:S(2)}, u32[]{:S(2)}) collective-permute-start(bf16[16,512]{1,0:T(8,128)(2,1)S(1)} %reshape.120), channel_id=1, source_target_pairs={{0,2},{1,3},{2,4},{3,5},{4,6},{5,7},{6,8},{7,9},{8,10},{9,11},{10,... | collective-permute-start | bytes 49160 | tf_op jit(solution)/shard_map/ppermute | solution.py:16
  33.3 18.0 %collective-permute-start.6 = (bf16[16,512]{1,0:T(8,128)(2,1)S(1)}, bf16[16,512]{1,0:T(8,128)(2,1)S(1)}, u32[]{:S(2)}, u32[]{:S(2)}) collective-permute-start(bf16[16,512]{1,0:T(8,128)(2,1)S(1)} %reshape.120), channel_id=1, source_target_pairs={{0,1},{1,2},{2,3},{3,4},{4,5},{5,6},{6,7},{7,8},{8,9},{9,10},{10,1... | collective-permute-start | bytes 49160 | tf_op jit(solution)/shard_map/ppermute | solution.py:16
  35.8 18.4 %collective-permute-start.7 = (bf16[16,512]{1,0:T(8,128)(2,1)S(1)}, bf16[16,512]{1,0:T(8,128)(2,1)S(1)}, u32[]{:S(2)}, u32[]{:S(2)}) collective-permute-start(bf16[16,512]{1,0:T(8,128)(2,1)S(1)} %reshape.120), channel_id=1, source_target_pairs={{1,0},{2,1},{3,2},{4,3},{5,4},{6,5},{7,6},{8,7},{9,8},{10,9},{11,1... | collective-permute-start | bytes 49160 | tf_op jit(solution)/shard_map/ppermute | solution.py:16
  37.7 19.0 %collective-permute-start.8 = (bf16[16,512]{1,0:T(8,128)(2,1)S(1)}, bf16[16,512]{1,0:T(8,128)(2,1)S(1)}, u32[]{:S(2)}, u32[]{:S(2)}) collective-permute-start(bf16[16,512]{1,0:T(8,128)(2,1)S(1)} %reshape.120), channel_id=1, source_target_pairs={{2,0},{3,1},{4,2},{5,3},{6,4},{7,5},{8,6},{9,7},{10,8},{11,9},{12,... | collective-permute-start | bytes 49160 | tf_op jit(solution)/shard_map/ppermute | solution.py:16
  44.3 17.5 %collective-permute-start.9 = (bf16[16,512]{1,0:T(8,128)(2,1)S(1)}, bf16[16,512]{1,0:T(8,128)(2,1)S(1)}, u32[]{:S(2)}, u32[]{:S(2)}) collective-permute-start(bf16[16,512]{1,0:T(8,128)(2,1)S(1)} %reshape.120), channel_id=1, source_target_pairs={{3,0},{4,1},{5,2},{6,3},{7,4},{8,5},{9,6},{10,7},{11,8},{12,9},{13... | collective-permute-start | bytes 49160 | tf_op jit(solution)/shard_map/ppermute | solution.py:16
  48.0 15.7 %collective-permute-start.10 = (bf16[16,512]{1,0:T(8,128)(2,1)S(1)}, bf16[16,512]{1,0:T(8,128)(2,1)S(1)}, u32[]{:S(2)}, u32[]{:S(2)}) collective-permute-start(bf16[16,512]{1,0:T(8,128)(2,1)S(1)} %reshape.120), channel_id=1, source_target_pairs={{4,0},{5,1},{6,2},{7,3},{8,4},{9,5},{10,6},{11,7},{12,8},{13,9},{1... | collective-permute-start | bytes 49160 | tf_op jit(solution)/shard_map/ppermute | solution.py:16
  51.4 15.0 %collective-permute-start.11 = (bf16[16,512]{1,0:T(8,128)(2,1)S(1)}, bf16[16,512]{1,0:T(8,128)(2,1)S(1)}, u32[]{:S(2)}, u32[]{:S(2)}) collective-permute-start(bf16[16,512]{1,0:T(8,128)(2,1)S(1)} %reshape.120), channel_id=1, source_target_pairs={{5,0},{6,1},{7,2},{8,3},{9,4},{10,5},{11,6},{12,7},{13,8},{14,9},{... | collective-permute-start | bytes 49160 | tf_op jit(solution)/shard_map/ppermute | solution.py:16
  54.2 17.4 %collective-permute-start.12 = (bf16[16,512]{1,0:T(8,128)(2,1)S(1)}, bf16[16,512]{1,0:T(8,128)(2,1)S(1)}, u32[]{:S(2)}, u32[]{:S(2)}) collective-permute-start(bf16[16,512]{1,0:T(8,128)(2,1)S(1)} %reshape.120), channel_id=1, source_target_pairs={{6,0},{7,1},{8,2},{9,3},{10,4},{11,5},{12,6},{13,7},{14,8},{15,9},... | collective-permute-start | bytes 49160 | tf_op jit(solution)/shard_map/ppermute | solution.py:16
  56.8 18.3 %collective-permute-start.13 = (bf16[16,512]{1,0:T(8,128)(2,1)S(1)}, bf16[16,512]{1,0:T(8,128)(2,1)S(1)}, u32[]{:S(2)}, u32[]{:S(2)}) collective-permute-start(bf16[16,512]{1,0:T(8,128)(2,1)S(1)} %reshape.120), channel_id=1, source_target_pairs={{7,0},{8,1},{9,2},{10,3},{11,4},{12,5},{13,6},{14,7},{15,8},{16,9}... | collective-permute-start | bytes 49160 | tf_op jit(solution)/shard_map/ppermute | solution.py:16
  61.8 37.7 %collective-permute-start.19 = (bf16[16,8,256]{2,1,0:T(8,128)(2,1)}, bf16[16,8,256]{2,1,0:T(8,128)(2,1)S(1)}, u32[]{:S(2)}, u32[]{:S(2)}) collective-permute-start(bf16[16,8,256]{2,1,0:T(8,128)(2,1)} %param.19), channel_id=1, source_target_pairs={{0,7},{1,8},{2,9},{3,10},{4,11},{5,12},{6,13},{7,14},{8,15},{9,16}... | collective-permute-start | bytes 196616 | tf_op jit(solution)/shard_map/ppermute | solution.py:16
  63.8 38.0 %collective-permute-start.20 = (bf16[16,8,256]{2,1,0:T(8,128)(2,1)}, bf16[16,8,256]{2,1,0:T(8,128)(2,1)S(1)}, u32[]{:S(2)}, u32[]{:S(2)}) collective-permute-start(bf16[16,8,256]{2,1,0:T(8,128)(2,1)} %param.19), channel_id=1, source_target_pairs={{0,6},{1,7},{2,8},{3,9},{4,10},{5,11},{6,12},{7,13},{8,14},{9,15},... | collective-permute-start | bytes 196616 | tf_op jit(solution)/shard_map/ppermute | solution.py:16
  66.4 37.3 %collective-permute-start.21 = (bf16[16,8,256]{2,1,0:T(8,128)(2,1)}, bf16[16,8,256]{2,1,0:T(8,128)(2,1)S(1)}, u32[]{:S(2)}, u32[]{:S(2)}) collective-permute-start(bf16[16,8,256]{2,1,0:T(8,128)(2,1)} %param.19), channel_id=1, source_target_pairs={{0,5},{1,6},{2,7},{3,8},{4,9},{5,10},{6,11},{7,12},{8,13},{9,14},{... | collective-permute-start | bytes 196616 | tf_op jit(solution)/shard_map/ppermute | solution.py:16
  71.6 34.6 %collective-permute-start.22 = (bf16[16,8,256]{2,1,0:T(8,128)(2,1)}, bf16[16,8,256]{2,1,0:T(8,128)(2,1)S(1)}, u32[]{:S(2)}, u32[]{:S(2)}) collective-permute-start(bf16[16,8,256]{2,1,0:T(8,128)(2,1)} %param.19), channel_id=1, source_target_pairs={{0,4},{1,5},{2,6},{3,7},{4,8},{5,9},{6,10},{7,11},{8,12},{9,13},{1... | collective-permute-start | bytes 196616 | tf_op jit(solution)/shard_map/ppermute | solution.py:16
  75.1 2.6 %collective-permute-start.15 = (f32[4,512]{1,0:T(4,128)S(1)}, f32[4,512]{1,0:T(4,128)S(1)}, u32[]{:S(2)}, u32[]{:S(2)}) collective-permute-start(f32[4,512]{1,0:T(4,128)S(1)} %slice_add_fusion.1), channel_id=1, source_target_pairs={{0,2},{2,0},{1,3},{3,1},{4,6},{6,4},{5,7},{7,5},{8,10},{10,8},{9,1... | collective-permute-start | bytes 24584 | tf_op jit(solution)/shard_map/ppermute | solution.py:26
  77.7 4.1 %collective-permute-start.16 = (f32[3,512]{1,0:T(4,128)S(1)}, f32[3,512]{1,0:T(4,128)S(1)}, u32[]{:S(2)}, u32[]{:S(2)}) collective-permute-start(f32[3,512]{1,0:T(4,128)S(1)} %slice_add_fusion), channel_id=1, source_target_pairs={{0,4},{4,0},{1,5},{5,1},{2,6},{6,2},{3,7},{7,3},{8,12},{12,8},{9,1... | collective-permute-start | bytes 18440 | tf_op jit(solution)/shard_map/ppermute | solution.py:26
  81.8 2.7 %collective-permute-start.17 = (f32[2,512]{1,0:T(2,128)S(1)}, f32[2,512]{1,0:T(2,128)S(1)}, u32[]{:S(2)}, u32[]{:S(2)}) collective-permute-start(f32[2,512]{1,0:T(2,128)S(1)} %slice_add_fusion.2), channel_id=1, source_target_pairs={{0,8},{8,0},{1,9},{9,1},{2,10},{10,2},{3,11},{11,3},{4,12},{12,4},... | collective-permute-start | bytes 12296 | tf_op jit(solution)/shard_map/ppermute | solution.py:26
  84.5 4.3 %collective-permute-start.18 = (f32[1,512]{1,0:T(1,128)S(1)}, f32[1,512]{1,0:T(1,128)S(1)}, u32[]{:S(2)}, u32[]{:S(2)}) collective-permute-start(f32[1,512]{1,0:T(1,128)S(1)} %get-tuple-element.58), channel_id=1, source_target_pairs={{0,16},{16,0},{1,17},{17,1},{2,18},{18,2},{3,19},{19,3},{4,20},{20... | collective-permute-start | bytes 6152 | tf_op jit(solution)/shard_map/ppermute | solution.py:26
  88.8 24.6 %collective-permute-start.23 = (bf16[16,8,256]{2,1,0:T(8,128)(2,1)}, bf16[16,8,256]{2,1,0:T(8,128)(2,1)S(1)}, u32[]{:S(2)}, u32[]{:S(2)}) collective-permute-start(bf16[16,8,256]{2,1,0:T(8,128)(2,1)} %param.19), channel_id=1, source_target_pairs={{0,3},{1,4},{2,5},{3,6},{4,7},{5,8},{6,9},{7,10},{8,11},{9,12},{10... | collective-permute-start | bytes 196616 | tf_op jit(solution)/shard_map/ppermute | solution.py:16
  99.5 16.6 %collective-permute-start.24 = (bf16[16,8,256]{2,1,0:T(8,128)(2,1)}, bf16[16,8,256]{2,1,0:T(8,128)(2,1)S(1)}, u32[]{:S(2)}, u32[]{:S(2)}) collective-permute-start(bf16[16,8,256]{2,1,0:T(8,128)(2,1)} %param.19), channel_id=1, source_target_pairs={{0,2},{1,3},{2,4},{3,5},{4,6},{5,7},{6,8},{7,9},{8,10},{9,11},{10,... | collective-permute-start | bytes 196616 | tf_op jit(solution)/shard_map/ppermute | solution.py:16
  101.8 18.7 %collective-permute-start.25 = (bf16[16,8,256]{2,1,0:T(8,128)(2,1)}, bf16[16,8,256]{2,1,0:T(8,128)(2,1)S(1)}, u32[]{:S(2)}, u32[]{:S(2)}) collective-permute-start(bf16[16,8,256]{2,1,0:T(8,128)(2,1)} %param.19), channel_id=1, source_target_pairs={{0,1},{1,2},{2,3},{3,4},{4,5},{5,6},{6,7},{7,8},{8,9},{9,10},{10,1... | collective-permute-start | bytes 196616 | tf_op jit(solution)/shard_map/ppermute | solution.py:16
  103.7 18.8 %collective-permute-start.26 = (bf16[16,8,256]{2,1,0:T(8,128)(2,1)}, bf16[16,8,256]{2,1,0:T(8,128)(2,1)S(1)}, u32[]{:S(2)}, u32[]{:S(2)}) collective-permute-start(bf16[16,8,256]{2,1,0:T(8,128)(2,1)} %param.19), channel_id=1, source_target_pairs={{1,0},{2,1},{3,2},{4,3},{5,4},{6,5},{7,6},{8,7},{9,8},{10,9},{11,1... | collective-permute-start | bytes 196616 | tf_op jit(solution)/shard_map/ppermute | solution.py:16
  106.2 20.0 %collective-permute-start.27 = (bf16[16,8,256]{2,1,0:T(8,128)(2,1)}, bf16[16,8,256]{2,1,0:T(8,128)(2,1)S(1)}, u32[]{:S(2)}, u32[]{:S(2)}) collective-permute-start(bf16[16,8,256]{2,1,0:T(8,128)(2,1)} %param.19), channel_id=1, source_target_pairs={{2,0},{3,1},{4,2},{5,3},{6,4},{7,5},{8,6},{9,7},{10,8},{11,9},{12,... | collective-permute-start | bytes 196616 | tf_op jit(solution)/shard_map/ppermute | solution.py:16
  113.5 16.0 %collective-permute-start.28 = (bf16[16,8,256]{2,1,0:T(8,128)(2,1)S(1)}, bf16[16,8,256]{2,1,0:T(8,128)(2,1)S(1)}, u32[]{:S(2)}, u32[]{:S(2)}) collective-permute-start(bf16[16,8,256]{2,1,0:T(8,128)(2,1)S(1)} %copy-done.2), channel_id=1, source_target_pairs={{3,0},{4,1},{5,2},{6,3},{7,4},{8,5},{9,6},{10,7},{11,8},{12,9},{13... | collective-permute-start | bytes 196616 | tf_op jit(solution)/shard_map/ppermute | solution.py:16
  116.1 13.4 %collective-permute-start.29 = (bf16[16,8,256]{2,1,0:T(8,128)(2,1)S(1)}, bf16[16,8,256]{2,1,0:T(8,128)(2,1)S(1)}, u32[]{:S(2)}, u32[]{:S(2)}) collective-permute-start(bf16[16,8,256]{2,1,0:T(8,128)(2,1)S(1)} %copy-done.2), channel_id=1, source_target_pairs={{4,0},{5,1},{6,2},{7,3},{8,4},{9,5},{10,6},{11,7},{12,8},{13,9},{1... | collective-permute-start | bytes 196616 | tf_op jit(solution)/shard_map/ppermute | solution.py:16
  120.5 9.1 %collective-permute-start.30 = (bf16[16,8,256]{2,1,0:T(8,128)(2,1)S(1)}, bf16[16,8,256]{2,1,0:T(8,128)(2,1)S(1)}, u32[]{:S(2)}, u32[]{:S(2)}) collective-permute-start(bf16[16,8,256]{2,1,0:T(8,128)(2,1)S(1)} %copy-done.2), channel_id=1, source_target_pairs={{5,0},{6,1},{7,2},{8,3},{9,4},{10,5},{11,6},{12,7},{13,8},{14,9},{... | collective-permute-start | bytes 196616 | tf_op jit(solution)/shard_map/ppermute | solution.py:16
  122.5 7.0 %collective-permute-start.31 = (bf16[16,8,256]{2,1,0:T(8,128)(2,1)S(1)}, bf16[16,8,256]{2,1,0:T(8,128)(2,1)S(1)}, u32[]{:S(2)}, u32[]{:S(2)}) collective-permute-start(bf16[16,8,256]{2,1,0:T(8,128)(2,1)S(1)} %copy-done.2), channel_id=1, source_target_pairs={{6,0},{7,1},{8,2},{9,3},{10,4},{11,5},{12,6},{13,7},{14,8},{15,9},... | collective-permute-start | bytes 196616 | tf_op jit(solution)/shard_map/ppermute | solution.py:16
  126.1 6.1 %collective-permute-start.32 = (bf16[16,8,256]{2,1,0:T(8,128)(2,1)S(1)}, bf16[16,8,256]{2,1,0:T(8,128)(2,1)S(1)}, u32[]{:S(2)}, u32[]{:S(2)}) collective-permute-start(bf16[16,8,256]{2,1,0:T(8,128)(2,1)S(1)} %copy-done.2), channel_id=1, source_target_pairs={{7,0},{8,1},{9,2},{10,3},{11,4},{12,5},{13,6},{14,7},{15,8},{16,9}... | collective-permute-start | bytes 196616 | tf_op jit(solution)/shard_map/ppermute | solution.py:16
where the time goes:
time: 142 us; the launch traced here: 140 us
  starting transfers between devices  111 us (78%)
  matrix products  15.6 us (11%)
  local copies, waits for them, and re-layouts  6.37 us (4%)
  waiting for transfers between devices  3.7 us (3%)
  other arithmetic  2.8 us (2%)
    ppermute x28, starting transfers between devices, shifted(): return lax.ppermute(block, axis, route)  102 us
    ppermute x5, starting transfers between devices, swapped(): return lax.ppermute(block, axis, route)  8.9 us
    dot_general x1, matrix products, per_device(): jnp.einsum('bsrj,bsij->bsri', gathered, near_tiles, preferred_element_typ...  5.65 us
    dot_general x5, matrix products, per_device(): jnp.dot(partner_sums[0].reshape(rhs_count, rank_size), level_coupling[0,...  4.47 us
  transfers between devices with their start and end apart: 33, of which 2 were waited for; matrix products, arithmetic and copies ran while one was open for 11% of the time, Pallas kernels for 0%

commit v1 on v0

v1 whole, which is shorter than its diff:
```python
import jax
import jax.numpy as jnp
from jax import lax
from jax.experimental import pallas as pl
from jax.experimental.pallas import tpu as pltpu
from jax.sharding import PartitionSpec as P

LEAF = 256
RANK = 64
RHS = 8
NEAR = 4
FAR = 6
UP = 5
BOXES = 16
LINE = 8
SEL = 4
SLOTS = 2 * SEL
ROWS = BOXES * RHS
PICKED = SLOTS * RHS
WIDE = LEAF + 2 * RANK
QUAD = 4 * LINE

F32 = jnp.float32
BF16 = jnp.bfloat16
VMEM = pl.BlockSpec(memory_space=pltpu.VMEM)
SMEM = pl.BlockSpec(memory_space=pltpu.SMEM)
ANY = pl.BlockSpec(memory_space=pl.ANY)


def nt(a, b):
    return lax.dot_general(a, b, (((1,), (1,)), ((), ())), preferred_element_type=F32)


def nn(a, b):
    return lax.dot_general(a, b, (((1,), (0,)), ((), ())), preferred_element_type=F32)


def iota(shape, dim):
    return lax.broadcasted_iota(jnp.int32, shape, dim)


def partner_up(line):
    return line ^ 1


def partner_down(line):
    return ((line + 1) ^ 1) - 1


def request_kernel(me_ref, near_ref, far_ref, want_ref, place_ref):
    me = me_ref[0]
    line, home = me >> 3, me & 7

    def parts(shape):
        lane = iota(shape, 1)
        return lane, lane >> 7, (lane >> 4) & 7, lane & 15

    lane, t, p, c = parts((BOXES, 3 * 128))
    lines = jnp.where(t == 0, line, jnp.where(t == 1, partner_up(line), partner_down(line)))
    candidate = ((lines * LINE + p) << 4) + c
    near, far = near_ref[...], far_ref[...]
    columns = [near[:, s : s + 1] for s in range(1, NEAR)] + [far[:, s : s + 1] for s in range(FAR)]
    hits = [column == candidate for column in columns]
    named = hits[0]
    for hit in hits[1:]:
        named = named | hit
    named = jnp.max(named.astype(jnp.int32), axis=0, keepdims=True)

    lane, t, p, c = parts((RHS, 3 * 128))
    own = (t == 0) & (p == home)
    named = jnp.where(own, 0, jnp.broadcast_to(named, (RHS, 3 * 128)))
    ahead = named
    for step in (1, 2, 4, 8):
        ahead = ahead + jnp.where(c >= step, pltpu.roll(ahead, step, 1), 0)
    slot = jnp.where(t == 0, 0, SEL) + jnp.minimum(ahead - named, SEL - 1)

    where = jnp.where(own, LINE * SLOTS + c, p * SLOTS + slot)
    where = jnp.broadcast_to(where[:1], (BOXES, 3 * 128))
    out_lane = iota((BOXES, 128), 1)
    places = jnp.zeros((BOXES, 128), jnp.int32)
    for s, hit in enumerate(hits):
        found = jnp.sum(jnp.where(hit, where, 0), axis=1, keepdims=True)
        places = jnp.where(out_lane == s, found, places)
    place_ref[...] = places

    chosen = (named > 0) & (p == iota((RHS, 3 * 128), 0))
    chosen = jnp.where(chosen, slot + 1, 0).astype(F32).astype(BF16)
    spread = ((iota((128, 128), 0) & 15) == (iota((128, 128), 1) >> 3)).astype(F32).astype(BF16)
    row = iota((RHS, 128), 1) & 7
    for k in range(3):
        value = nn(chosen[:, k * 128 : (k + 1) * 128], spread).astype(jnp.int32)
        want_ref[:, k * 128 : (k + 1) * 128] = jnp.where(value > 0, (value - 1) * RHS + row, -1)


def lift_kernel(vectors_ref, basis_ref, transfer_ref, up_ref, block_ref, top_ref):
    coefficients = []
    total = jnp.zeros((RHS, RANK), F32)
    for b in range(BOXES):
        q = nt(vectors_ref[b], basis_ref[b]).astype(BF16)
        total = total + nn(q, transfer_ref[b])
        coefficients.append(q.astype(F32))
    total = total.astype(BF16)
    lifted = [nn(total, up_ref[0, k].astype(BF16)) for k in range(UP)]
    nothing = jnp.zeros((RHS, RANK), F32)
    lifted_rows = lifted + [nothing] * (BOXES - UP)
    for i in range(BOXES // 2):
        rows = pl.ds(2 * RHS * i, 2 * RHS)
        pair = (2 * i, 2 * i + 1)
        block_ref[rows, :LEAF] = jnp.concatenate(
            [vectors_ref[b].astype(F32) for b in pair], axis=0
        ).astype(BF16)
        block_ref[rows, LEAF:] = jnp.concatenate(
            [jnp.concatenate([coefficients[b], lifted_rows[b]], axis=1) for b in pair], axis=0
        ).astype(BF16)
    top_ref[...] = jnp.concatenate([nothing, lifted[UP - 1]], axis=1)


def pick_kernel(want_ref, own_ref, up_ref, down_ref, top_a_ref, top_b_ref, out_ref):
    data = jnp.concatenate([own_ref[...], up_ref[...], down_ref[...]], axis=0)
    want = want_ref[...]
    picks = jnp.concatenate(
        [
            (jnp.broadcast_to(want[q : q + 1], (PICKED, 3 * 128)) == iota((PICKED, 3 * 128), 0))
            .astype(F32)
            .astype(BF16)
            for q in range(LINE)
        ],
        axis=0,
    )
    own_levels = own_ref[0:32, LEAF:].astype(F32)
    up_levels = up_ref[16:32, LEAF:].astype(F32)
    levels = jnp.concatenate(
        [
            own_levels[:24],
            up_levels[8:16],
            top_a_ref[...] + top_b_ref[...],
            jnp.zeros((PICKED - UP * RHS, 128), F32),
        ],
        axis=0,
    )
    selected = nn(picks, data)
    low = iota((PICKED, 128), 1) < RANK
    for q in range(LINE):
        rows = slice(q * PICKED, (q + 1) * PICKED)
        out_ref[q, :, :LEAF] = selected[rows, :LEAF].astype(BF16)
        out_ref[q, :, LEAF:] = jnp.where(low, selected[rows, LEAF:], levels).astype(BF16)


def final_kernel(
    me_ref,
    place_ref,
    scale_ref,
    count_ref,
    got_any,
    own_any,
    basis_any,
    transfer_any,
    coupling_any,
    level_any,
    tiles_any,
    out_ref,
    got,
    own,
    window,
    basis,
    transfer,
    coupling,
    level,
    tiles,
    sems,
    tile_sems,
):
    pairs = (
        (got_any, got),
        (own_any, own),
        (level_any, level),
        (transfer_any, transfer),
        (coupling_any, coupling),
        (basis_any, basis),
    )
    copies = [pltpu.make_async_copy(a, b, sems.at[i]) for i, (a, b) in enumerate(pairs)]
    tile_copies = [
        pltpu.make_async_copy(tiles_any.at[b], tiles.at[b], tile_sems.at[b]) for b in range(BOXES)
    ]
    for copy in copies + tile_copies:
        copy.start()
    for copy in copies:
        copy.wait()
    home = me_ref[0] & 7
    for p in range(LINE):
        window[p * PICKED : (p + 1) * PICKED, :] = got[p].astype(F32)
    window[LINE * PICKED :, :] = own[...].astype(F32)

    groups = [jnp.zeros((RHS, 128), F32) for _ in range(UP)]
    for p in range(LINE):
        apart = home ^ p
        chunk = window[p * PICKED : p * PICKED + UP * RHS, LEAF:]
        for k in range(UP):
            piece = chunk[k * RHS : (k + 1) * RHS]
            if k < 3:
                piece = jnp.where((apart >> k) == 1, piece, 0.0)
            groups[k] = groups[k] + piece
    far_field = jnp.zeros((RHS, RANK), F32)
    for k in range(UP):
        far_field = far_field + nn(groups[k][:, RANK:].astype(BF16), level[0, k].astype(BF16))
    far_field = far_field.astype(BF16)

    def rows_of(b, s):
        return pl.ds(pl.multiple_of(place_ref[b, s] * RHS, RHS), RHS)

    low = iota((RHS, 128), 1) < RANK
    for b in range(BOXES):
        halves = [window[rows_of(b, NEAR - 1 + s), LEAF:] for s in range(FAR)]
        joined = jnp.concatenate(
            [
                jnp.where(low, halves[2 * i], pltpu.roll(halves[2 * i + 1], RANK, 1))
                for i in range(FAR // 2)
            ],
            axis=1,
        ).astype(BF16)
        leaf = nt(joined, coupling[b]) + nt(far_field, transfer[b])
        total = nn(leaf.astype(BF16), basis[b])
        tile_copies[b].wait()
        for s in range(NEAR):
            if s == 0:
                x = window[(LINE * SLOTS + b) * RHS : (LINE * SLOTS + b + 1) * RHS, :LEAF]
            else:
                x = window[rows_of(b, s - 1), :LEAF]
            weight = jnp.where(s < count_ref[b], scale_ref[b, s], 0.0)
            total = total + weight * nt(x.astype(BF16), tiles[b, s])
        out_ref[b] = total


def pairwise(block, partner):
    count = lax.axis_size("pts")
    route = [(i, partner(i)) for i in range(count) if 0 <= partner(i) < count]
    return lax.ppermute(block, "pts", route)


def per_device(
    vectors,
    leaf_basis,
    leaf_transfer,
    leaf_coupling,
    near_tiles,
    tile_scale,
    near_boxes,
    near_counts,
    far_boxes,
    level_up,
    level_coupling,
):
    count = lax.axis_size("pts")
    lines = [[LINE * i + p for p in range(LINE)] for i in range(count // LINE)]
    me = lax.axis_index("pts").astype(jnp.int32).reshape(1)

    block, top = pl.pallas_call(
        lift_kernel,
        out_shape=(
            jax.ShapeDtypeStruct((ROWS, WIDE), BF16),
            jax.ShapeDtypeStruct((RHS, 128), F32),
        ),
        in_specs=[VMEM] * 4,
        out_specs=(VMEM, VMEM),
        name="lift",
    )(vectors, leaf_basis, leaf_transfer, level_up)

    want, place = pl.pallas_call(
        request_kernel,
        out_shape=(
            jax.ShapeDtypeStruct((LINE, 3 * 128), jnp.int32),
            jax.ShapeDtypeStruct((BOXES, 128), jnp.int32),
        ),
        in_specs=[SMEM, VMEM, VMEM],
        out_specs=(VMEM, VMEM),
        name="request",
    )(me, near_boxes, far_boxes)

    up = pairwise(block, lambda i: LINE * partner_up(i // LINE) + i % LINE)
    down = pairwise(block, lambda i: LINE * partner_down(i // LINE) + i % LINE)
    top_a = pairwise(top, lambda i: i ^ (2 * LINE))
    top_b = pairwise(top, lambda i: i ^ (3 * LINE))
    wanted = lax.all_to_all(
        want.reshape(LINE, 1, 3 * 128), "pts", 0, 0, axis_index_groups=lines
    ).reshape(LINE, 3 * 128)

    parcels = pl.pallas_call(
        pick_kernel,
        out_shape=jax.ShapeDtypeStruct((LINE, PICKED, WIDE), BF16),
        in_specs=[VMEM] * 6,
        out_specs=VMEM,
        name="pick",
    )(wanted, block, up, down, top_a, top_b)
    got = lax.all_to_all(parcels, "pts", 0, 0, axis_index_groups=lines)

    return pl.pallas_call(
        final_kernel,
        out_shape=jax.ShapeDtypeStruct((BOXES, RHS, LEAF), F32),
        in_specs=[SMEM] * 4 + [ANY] * 7,
        out_specs=VMEM,
        scratch_shapes=[
            pltpu.VMEM((LINE, PICKED, WIDE), BF16),
            pltpu.VMEM((ROWS, WIDE), BF16),
            pltpu.VMEM((LINE * PICKED + ROWS, WIDE), F32),
            pltpu.VMEM((BOXES, RANK, LEAF), BF16),
            pltpu.VMEM((BOXES, RANK, RANK), BF16),
            pltpu.VMEM((BOXES, RANK, FAR * RANK), BF16),
            pltpu.VMEM((1, UP, RANK, RANK), F32),
            pltpu.VMEM((BOXES, NEAR, LEAF, LEAF), BF16),
            pltpu.SemaphoreType.DMA((6,)),
            pltpu.SemaphoreType.DMA((BOXES,)),
        ],
        compiler_params=pltpu.CompilerParams(vmem_limit_bytes=24 * 1024 * 1024),
        name="final",
    )(
        me,
        place,
        tile_scale,
        near_counts,
        got,
        block,
        leaf_basis,
        leaf_transfer,
        leaf_coupling,
        level_coupling,
        near_tiles,
    )


def solution(mesh):
    placed = (
        P("pts", None, None),
        P("pts", None, None),
        P("pts", None, None),
        P("pts", None, None),
        P("pts", None, None, None),
        P("pts", None),
        P("pts", None),
        P("pts"),
        P("pts", None),
        P("pts", None, None, None),
        P("pts", None, None, None),
    )
    return jax.shard_map(
        per_device, mesh=mesh, in_specs=placed, out_specs=P("pts", None, None), check_vma=False
    )
```

time: 142 us -> 62.6 us (0.44)
  starting transfers between devices: 111 us -> 20.5 us
  matrix products: 15.6 us -> 0 us
  Pallas kernels: 0 us -> 14.9 us
  local copies, waits for them, and re-layouts: 6.37 us -> 15.7 us
  waiting for transfers between devices: 3.7 us -> 10.5 us
  other arithmetic: 2.8 us -> 0 us
    ppermute x33 -> x4, starting transfers between devices: 111 us -> 9.84 us  [pairwise(): return lax.ppermute(block, 'pts', route)]
    dot_general x12 -> x0, matrix products: 15.6 us -> none  [the longest x1 5.65 us: per_device(): jnp.einsum('bsrj,bsij->bsri', gathered, near_tiles, preferred_element_typ...]
    pallas_call x0 -> x4, Pallas kernels: none -> 14.9 us  [the longest x1 8.08 us: per_device(): pl.pallas_call(final_kernel, out_shape=jax.ShapeDtypeStruct((BOXES, RHS,...]
    unnamed x34 -> x28, local copies, waits for them, and re-layouts: 1.2 us -> 14.4 us
    all_to_all x0 -> x2, starting transfers between devices: none -> 10.7 us  [the longest x1 5.53 us: per_device(): lax.all_to_all(want.reshape(LINE, 1, 3 * 128), 'pts', 0, 0, axis_index_gr...]
    all_to_all x0 -> x2, waiting for transfers between devices: none -> 10.5 us  [the longest x1 7.32 us: per_device(): got = lax.all_to_all(parcels, 'pts', 0, 0, axis_index_groups=lines)]
    ppermute x33 -> x4, waiting for transfers between devices: 3.7 us -> 0.01 us  [pairwise(): return lax.ppermute(block, 'pts', route)]
    gather x3 -> x0, local copies, waits for them, and re-layouts: 1.52 us -> none  [the longest x2 0.93 us: per_device(): jnp.take(window_q, far_boxes - window_start, axis=0)]
  transfers between devices with their start and end apart: 33 -> 6, of which waited for: 2 -> 2; matrix products, arithmetic and copies ran while one was open for 11% -> 9% of each run, Pallas kernels for 0% -> 3%
where the time goes in v1:
time: 62.6 us; the launch traced here: 61.7 us
  starting transfers between devices  20.5 us (33%)
  local copies, waits for them, and re-layouts  15.7 us (25%)
  Pallas kernels  14.9 us (24%)
  waiting for transfers between devices  10.5 us (17%)
    unnamed x28, local copies, waits for them, and re-layouts  14.4 us
    ppermute x4, starting transfers between devices, pairwise(): return lax.ppermute(block, 'pts', route)  9.84 us
    pallas_call x1, Pallas kernels, per_device(): pl.pallas_call(final_kernel, out_shape=jax.ShapeDtypeStruct((BOXES, RHS,...  8.08 us
    all_to_all x1, waiting for transfers between devices, per_device(): got = lax.all_to_all(parcels, 'pts', 0, 0, axis_index_groups=lines)  7.32 us
    all_to_all x1, starting transfers between devices, per_device(): lax.all_to_all(want.reshape(LINE, 1, 3 * 128), 'pts', 0, 0, axis_index_gr...  5.53 us
    all_to_all x1, starting transfers between devices, per_device(): got = lax.all_to_all(parcels, 'pts', 0, 0, axis_index_groups=lines)  5.16 us
    all_to_all x1, waiting for transfers between devices, per_device(): lax.all_to_all(want.reshape(LINE, 1, 3 * 128), 'pts', 0, 0, axis_index_gr...  3.17 us
    pallas_call x1, Pallas kernels, per_device(): pl.pallas_call(lift_kernel, out_shape=(jax.ShapeDtypeStruct((ROWS, WIDE),...  2.78 us
  transfers between devices with their start and end apart: 6, of which 2 were waited for; matrix products, arithmetic and copies ran while one was open for 9% of the time, Pallas kernels for 3%

profile of v1, /device:TPU:25, one launch (start us, length us, event | category | flops | bytes accessed | tf_op | source)
XLA Modules:
  0.0 61.7 jit_solution(11895312096544907621)
XLA Ops:
  0.0 2.8 %lift.1 = (bf16[128,384]{1,0:T(8,128)(2,1)}, f32[8,128]{1,0:T(8,128)}) custom-call(bf16[16,8,256]{2,1,0:T(8,128)(2,1)} %vectors_ref.1, bf16[16,64,256]{2,1,0:T(8,128)(2,1)} %basis_any.1, bf16[16,64,64]{2,1,0:T(8,128)(2,1)} %transfer_any.1, f32[1,5,64,64]{3,2,1,0:T(8,128)} %up_ref.1), custom_call_target="tpu_custom_call" | custom-call | tf_op jit(solution)/shard_map/lift/pallas_call | solution.py:257
  2.8 1.6 %collective-permute-start = (bf16[128,384]{1,0:T(8,128)(2,1)}, bf16[128,384]{1,0:T(8,128)(2,1)S(1)}, u32[]{:S(2)}, u32[]{:S(2)}) collective-permute-start(bf16[128,384]{1,0:T(8,128)(2,1)} %get-tuple-element.11.own_ref.own_any), channel_id=1, source_target_pairs={{0,8},{1,9},{2,10},{3,11},{4,12},{5,13},{6,14},{7,15},{8,0},{9,1},... | collective-permute-start | bytes 294920 | tf_op jit(solution)/shard_map/ppermute | solution.py:237
  4.4 6.7 %collective-permute-start.1 = (bf16[128,384]{1,0:T(8,128)(2,1)}, bf16[128,384]{1,0:T(8,128)(2,1)S(1)}, u32[]{:S(2)}, u32[]{:S(2)}) collective-permute-start(bf16[128,384]{1,0:T(8,128)(2,1)} %get-tuple-element.11.own_ref.own_any), channel_id=1, source_target_pairs={{8,16},{9,17},{10,18},{11,19},{12,20},{13,21},{14,22},{15,23},{16,... | collective-permute-start | bytes 294920 | tf_op jit(solution)/shard_map/ppermute | solution.py:237
  11.2 1.4 %copy.15.near_ref = s32[16,4]{1,0:T(8,128)} copy(s32[16,4]{0,1:T(4,128)} %param.17) | data formatting | bytes 512 | tf_op args[6]
  12.5 1.4 %copy.16.far_ref = s32[16,6]{1,0:T(8,128)} copy(s32[16,6]{0,1:T(8,128)} %param.19) | data formatting | bytes 768 | tf_op args[8]
  13.9 1.8 %request.1 = (s32[8,384]{1,0:T(8,128)}, s32[16,128]{1,0:T(8,128)}) custom-call(s32[1]{0:T(128)} %bitcast.me_ref, s32[16,4]{1,0:T(8,128)} %copy.15.near_ref, s32[16,6]{1,0:T(8,128)} %copy.16.far_ref), custom_call_target="tpu_custom_call" | custom-call | tf_op jit(solution)/shard_map/request/pallas_call | solution.py:268
  15.7 1.3 %copy.17 = s32[8,1,384]{2,1,0:T(1,128)} copy(s32[8,1,384]{2,0,1:T(8,128)} %bitcast.6) | data formatting | bytes 24576 | tf_op jit(solution)/shard_map/reshape | solution.py:284
  17.0 5.5 %all-to-all-start = ((s32[8,1,384]{2,1,0:T(1,128)}), s32[8,1,384]{2,1,0:T(1,128)S(1)}, u32[]{:S(2)}, u32[]{:S(2)}) async-start(s32[8,1,384]{2,1,0:T(1,128)} %copy.17), calls=%async_computation | async-start | bytes 24576 | tf_op jit(solution)/shard_map/all_to_all | solution.py:283
  22.6 0.0 collective-permute-start.2
  22.6 1.5 %collective-permute-start.3 = (f32[8,128]{1,0:T(8,128)}, f32[8,128]{1,0:T(8,128)S(1)}, u32[]{:S(2)}, u32[]{:S(2)}) collective-permute-start(f32[8,128]{1,0:T(8,128)} %get-tuple-element.12), channel_id=1, source_target_pairs={{0,24},{1,25},{2,26},{3,27},{4,28},{5,29},{6,30},{7,31},{8,16},{9,... | collective-permute-start | bytes 12296 | tf_op jit(solution)/shard_map/ppermute | solution.py:237
  24.0 3.2 %all-to-all-done = s32[8,1,384]{2,1,0:T(1,128)S(1)} async-done(((s32[8,1,384]{2,1,0:T(1,128)}), s32[8,1,384]{2,1,0:T(1,128)S(1)}, u32[]{:S(2)}, u32[]{:S(2)}) %all-to-all-start) | async-done | bytes 12320 | tf_op jit(solution)/shard_map/all_to_all | solution.py:283
  27.2 0.6 copy.21
  27.8 0.0 collective-permute-done.2.top_a_ref
  27.8 0.0 copy-start.10
  27.8 0.0 collective-permute-done.3.top_b_ref
  27.8 0.0 copy-start.11
  27.8 0.0 collective-permute-done.up_ref
  27.8 0.0 copy-start.8
  27.9 0.0 collective-permute-done.1.down_ref
  27.9 0.0 copy-start.9
  27.9 0.5 copy-done.10
  28.4 0.0 copy-done.11
  28.4 0.1 copy-done.8
  28.5 0.0 copy-done.9
  28.5 2.1 %pick.1 = bf16[8,64,384]{2,1,0:T(8,128)(2,1)} custom-call(s32[8,384]{1,0:T(8,128)} %bitcast.5, bf16[128,384]{1,0:T(8,128)(2,1)} %get-tuple-element.11.own_ref.own_any, bf16[128,384]{1,0:T(8,128)(2,1)} %copy-done.8, bf16[128,384]{1,0:T(8,128)(2,1)} %copy-done.9, f32[8,128]{1,0:T(8,128)} %copy-done.10, f32[8,128]{1,0:T(8,128)} %copy-done.11), custom_call_target="tpu_custom_call" | custom-call | tf_op jit(solution)/shard_map/pick/pallas_call | solution.py:287
  30.7 5.2 %all-to-all-start.1 = ((bf16[8,64,384]{2,1,0:T(8,128)(2,1)}), bf16[8,64,384]{2,1,0:T(8,128)(2,1)S(1)}, u32[]{:S(2)}, u32[]{:S(2)}) async-start(bf16[8,64,384]{2,1,0:T(8,128)(2,1)} %pick.1), calls=%async_computation.1 | async-start | bytes 786432 | tf_op jit(solution)/shard_map/all_to_all | solution.py:294
  35.8 0.8 %copy.18.scale_ref = f32[16,4]{1,0:T(8,128)S(1)} copy(f32[16,4]{0,1:T(4,128)} %param.16) | data formatting | bytes 512 | tf_op args[5]
  36.6 7.3 %all-to-all-done.1.got_any = bf16[8,64,384]{2,1,0:T(8,128)(2,1)S(1)} async-done(((bf16[8,64,384]{2,1,0:T(8,128)(2,1)}), bf16[8,64,384]{2,1,0:T(8,128)(2,1)S(1)}, u32[]{:S(2)}, u32[]{:S(2)}) %all-to-all-start.1) | async-done | bytes 393248 | tf_op jit(solution)/shard_map/all_to_all | solution.py:294
  43.9 0.0 copy-start
  43.9 3.4 %copy-done = bf16[16,4,256,256]{3,2,1,0:T(8,128)(2,1)S(1)} copy-done((bf16[16,4,256,256]{3,2,1,0:T(8,128)(2,1)S(1)}, bf16[16,4,256,256]{3,2,1,0:T(8,128)(2,1)}, u32[]{:S(2)}) %copy-start) | copy-done | bytes 8388632
  47.3 0.0 copy-start.1
  47.3 1.0 %copy-done.1 = bf16[16,64,256]{2,1,0:T(8,128)(2,1)S(1)} copy-done((bf16[16,64,256]{2,1,0:T(8,128)(2,1)S(1)}, bf16[16,64,256]{2,1,0:T(8,128)(2,1)}, u32[]{:S(2)}) %copy-start.1) | copy-done | bytes 524312
  48.3 0.0 copy-start.2
  48.3 0.9 %copy-done.2 = bf16[16,64,64]{2,1,0:T(8,128)(2,1)S(1)} copy-done((bf16[16,64,64]{2,1,0:T(8,128)(2,1)S(1)}, bf16[16,64,64]{2,1,0:T(8,128)(2,1)}, u32[]{:S(2)}) %copy-start.2) | copy-done | bytes 131096
  49.3 0.0 copy-start.3
  49.3 1.1 %copy-done.3 = bf16[16,64,384]{2,1,0:T(8,128)(2,1)S(1)} copy-done((bf16[16,64,384]{2,1,0:T(8,128)(2,1)S(1)}, bf16[16,64,384]{2,1,0:T(8,128)(2,1)}, u32[]{:S(2)}) %copy-start.3) | copy-done | bytes 786456
  50.4 0.0 copy-start.4
  50.4 0.9 %copy-done.4 = bf16[128,384]{1,0:T(8,128)(2,1)S(1)} copy-done((bf16[128,384]{1,0:T(8,128)(2,1)S(1)}, bf16[128,384]{1,0:T(8,128)(2,1)}, u32[]{:S(2)}) %copy-start.4) | copy-done | bytes 98328
  51.3 0.0 copy-start.5
  51.3 0.9 %copy-done.5 = f32[1,5,64,64]{3,2,1,0:T(8,128)S(1)} copy-done((f32[1,5,64,64]{3,2,1,0:T(8,128)S(1)}, f32[1,5,64,64]{3,2,1,0:T(8,128)}, u32[]{:S(2)}) %copy-start.5) | copy-done | bytes 81944
  52.2 0.0 copy-start.6
  52.2 0.7 %copy-done.6 = s32[16,128]{1,0:T(8,128)S(1)} copy-done((s32[16,128]{1,0:T(8,128)S(1)}, s32[16,128]{1,0:T(8,128)}, u32[]{:S(2)}) %copy-start.6) | copy-done | bytes 8216
  52.9 0.0 copy-start.7
  52.9 0.7 %copy-done.7 = s32[16]{0:T(128)S(1)} copy-done((s32[16]{0:T(128)S(1)}, s32[16]{0:T(128)}, u32[]{:S(2)}) %copy-start.7) | copy-done | bytes 88
  53.6 8.1 %final.1 = f32[16,8,256]{2,1,0:T(8,128)} custom-call(s32[1]{0:T(128)} %bitcast.me_ref, s32[16,128]{1,0:T(8,128)S(1)} %copy-done.6, f32[16,4]{1,0:T(8,128)S(1)} %copy.18.scale_ref, s32[16]{0:T(128)S(1)} %copy-done.7, bf16[8,64,384]{2,1,0:T(8,128)(2,1)S(1)} %all-to-all-done.1.got_any, bf16[128,384]{1,0:T(8,128)(2,1)S(1)} %copy-done.4, ...), custom_call_target="tpu_custom_call" | custom-call | tf_op jit(solution)/shard_map/final/pallas_call | solution.py:296
Async XLA Ops:
  2.8 25.1 %collective-permute-start = (bf16[128,384]{1,0:T(8,128)(2,1)}, bf16[128,384]{1,0:T(8,128)(2,1)S(1)}, u32[]{:S(2)}, u32[]{:S(2)}) collective-permute-start(bf16[128,384]{1,0:T(8,128)(2,1)} %get-tuple-element.11.own_ref.own_any), channel_id=1, source_target_pairs={{0,8},{1,9},{2,10},{3,11},{4,12},{5,13},{6,14},{7,15},{8,0},{9,1},... | collective-permute-start | bytes 294920 | tf_op jit(solution)/shard_map/ppermute | solution.py:237
  4.4 23.4 %collective-permute-start.1 = (bf16[128,384]{1,0:T(8,128)(2,1)}, bf16[128,384]{1,0:T(8,128)(2,1)S(1)}, u32[]{:S(2)}, u32[]{:S(2)}) collective-permute-start(bf16[128,384]{1,0:T(8,128)(2,1)} %get-tuple-element.11.own_ref.own_any), channel_id=1, source_target_pairs={{8,16},{9,17},{10,18},{11,19},{12,20},{13,21},{14,22},{15,23},{16,... | collective-permute-start | bytes 294920 | tf_op jit(solution)/shard_map/ppermute | solution.py:237
  17.0 10.2 %all-to-all-start = ((s32[8,1,384]{2,1,0:T(1,128)}), s32[8,1,384]{2,1,0:T(1,128)S(1)}, u32[]{:S(2)}, u32[]{:S(2)}) async-start(s32[8,1,384]{2,1,0:T(1,128)} %copy.17), calls=%async_computation | async-start | bytes 24576 | tf_op jit(solution)/shard_map/all_to_all | solution.py:283
  22.6 5.2 %collective-permute-start.2 = (f32[8,128]{1,0:T(8,128)}, f32[8,128]{1,0:T(8,128)S(1)}, u32[]{:S(2)}, u32[]{:S(2)}) collective-permute-start(f32[8,128]{1,0:T(8,128)} %get-tuple-element.12), channel_id=1, source_target_pairs={{0,16},{1,17},{2,18},{3,19},{4,20},{5,21},{6,22},{7,23},{8,24},{9,... | collective-permute-start | bytes 12296 | tf_op jit(solution)/shard_map/ppermute | solution.py:237
  22.6 5.2 %collective-permute-start.3 = (f32[8,128]{1,0:T(8,128)}, f32[8,128]{1,0:T(8,128)S(1)}, u32[]{:S(2)}, u32[]{:S(2)}) collective-permute-start(f32[8,128]{1,0:T(8,128)} %get-tuple-element.12), channel_id=1, source_target_pairs={{0,24},{1,25},{2,26},{3,27},{4,28},{5,29},{6,30},{7,31},{8,16},{9,... | collective-permute-start | bytes 12296 | tf_op jit(solution)/shard_map/ppermute | solution.py:237
  27.8 0.6 copy-start.10
  27.8 0.6 copy-start.11
  27.8 0.6 %copy-start.8 = (bf16[128,384]{1,0:T(8,128)(2,1)}, bf16[128,384]{1,0:T(8,128)(2,1)S(1)}, u32[]{:S(2)}) copy-start(bf16[128,384]{1,0:T(8,128)(2,1)S(1)} %collective-permute-done.up_ref) | copy-start | bytes 294916
  27.9 0.7 %copy-start.9 = (bf16[128,384]{1,0:T(8,128)(2,1)}, bf16[128,384]{1,0:T(8,128)(2,1)S(1)}, u32[]{:S(2)}) copy-start(bf16[128,384]{1,0:T(8,128)(2,1)S(1)} %collective-permute-done.1.down_ref) | copy-start | bytes 294916
  30.7 13.2 %all-to-all-start.1 = ((bf16[8,64,384]{2,1,0:T(8,128)(2,1)}), bf16[8,64,384]{2,1,0:T(8,128)(2,1)S(1)}, u32[]{:S(2)}, u32[]{:S(2)}) async-start(bf16[8,64,384]{2,1,0:T(8,128)(2,1)} %pick.1), calls=%async_computation.1 | async-start | bytes 786432 | tf_op jit(solution)/shard_map/all_to_all | solution.py:294
  43.9 3.4 %copy-start = (bf16[16,4,256,256]{3,2,1,0:T(8,128)(2,1)S(1)}, bf16[16,4,256,256]{3,2,1,0:T(8,128)(2,1)}, u32[]{:S(2)}) copy-start(bf16[16,4,256,256]{3,2,1,0:T(8,128)(2,1)} %tiles_any.1) | copy-start | bytes 25165828
  47.3 1.0 %copy-start.1 = (bf16[16,64,256]{2,1,0:T(8,128)(2,1)S(1)}, bf16[16,64,256]{2,1,0:T(8,128)(2,1)}, u32[]{:S(2)}) copy-start(bf16[16,64,256]{2,1,0:T(8,128)(2,1)} %basis_any.1) | copy-start | bytes 1572868
  48.3 0.9 %copy-start.2 = (bf16[16,64,64]{2,1,0:T(8,128)(2,1)S(1)}, bf16[16,64,64]{2,1,0:T(8,128)(2,1)}, u32[]{:S(2)}) copy-start(bf16[16,64,64]{2,1,0:T(8,128)(2,1)} %transfer_any.1) | copy-start | bytes 393220
  49.3 1.1 %copy-start.3 = (bf16[16,64,384]{2,1,0:T(8,128)(2,1)S(1)}, bf16[16,64,384]{2,1,0:T(8,128)(2,1)}, u32[]{:S(2)}) copy-start(bf16[16,64,384]{2,1,0:T(8,128)(2,1)} %coupling_any.1) | copy-start | bytes 2359300
  50.4 0.9 %copy-start.4 = (bf16[128,384]{1,0:T(8,128)(2,1)S(1)}, bf16[128,384]{1,0:T(8,128)(2,1)}, u32[]{:S(2)}) copy-start(bf16[128,384]{1,0:T(8,128)(2,1)} %get-tuple-element.11.own_ref.own_any) | copy-start | bytes 294916
  51.3 0.9 %copy-start.5 = (f32[1,5,64,64]{3,2,1,0:T(8,128)S(1)}, f32[1,5,64,64]{3,2,1,0:T(8,128)}, u32[]{:S(2)}) copy-start(f32[1,5,64,64]{3,2,1,0:T(8,128)} %level_any.1) | copy-start | bytes 245764
  52.2 0.7 %copy-start.6 = (s32[16,128]{1,0:T(8,128)S(1)}, s32[16,128]{1,0:T(8,128)}, u32[]{:S(2)}) copy-start(s32[16,128]{1,0:T(8,128)} %get-tuple-element.9.place_ref) | copy-start | bytes 24580
  52.9 0.7 %copy-start.7 = (s32[16]{0:T(128)S(1)}, s32[16]{0:T(128)}, u32[]{:S(2)}) copy-start(s32[16]{0:T(128)} %count_ref.1) | copy-start | bytes 196

commit v2 on v0

v2 whole, which is shorter than its diff:
```python
import jax
import jax.numpy as jnp
from jax import lax
from jax.experimental import pallas as pl
from jax.experimental.pallas import tpu as pltpu
from jax.sharding import PartitionSpec as P

LEAF = 256
RANK = 64
RHS = 8
NEAR = 4
FAR = 6
UP = 5
BOXES = 16
LINE = 8
CHIPS = 4
CORES = 2
WIDE = LEAF + 2 * RANK
MIB = 1024 * 1024

F32 = jnp.float32
BF16 = jnp.bfloat16
I32 = jnp.int32
VMEM = pl.BlockSpec(memory_space=pltpu.VMEM)
SMEM = pl.BlockSpec(memory_space=pltpu.SMEM)
ANY = pl.BlockSpec(memory_space=pl.ANY)


def nt(a, b):
    return lax.dot_general(a, b, (((1,), (1,)), ((), ())), preferred_element_type=F32)


def nn(a, b):
    return lax.dot_general(a, b, (((1,), (0,)), ((), ())), preferred_element_type=F32)


def iota(shape, dim):
    return lax.broadcasted_iota(I32, shape, dim)


def partner_up(line):
    return line ^ 1


def partner_down(line):
    return ((line + 1) ^ 1) - 1


def front_kernel(
    me_ref,
    near_ref,
    far_ref,
    vectors_any,
    basis_any,
    transfer_any,
    up_any,
    block_ref,
    place_ref,
    vectors,
    basis,
    transfer,
    up,
    sems,
):
    pairs = ((vectors_any, vectors), (basis_any, basis), (transfer_any, transfer), (up_any, up))
    copies = [pltpu.make_async_copy(a, b, sems.at[i]) for i, (a, b) in enumerate(pairs)]
    for copy in copies:
        copy.start()
    line, core = me_ref[0] >> 3, me_ref[0] & 1
    for first, ref in ((0, near_ref), (8, far_ref)):
        box = ref[...]
        apart = ((box >> 4) & 1) ^ core
        beside = ((box >> 7) != line).astype(I32)
        place = (apart << 7) | (((box >> 5) & 3) << 5) | (beside << 4) | (box & 15)
        place_ref[first : first + box.shape[0], 0:BOXES] = place
    copies[0].wait()
    copies[1].wait()
    coefficients = [nt(vectors[b], basis[b]).astype(BF16) for b in range(BOXES)]
    copies[2].wait()
    total = jnp.zeros((RHS, RANK), F32)
    for b in range(BOXES):
        total = total + nn(coefficients[b], transfer[b])
    total = total.astype(BF16)
    copies[3].wait()
    lifted = [nn(total, up[0, k].astype(BF16)) for k in range(UP)]
    nothing = jnp.zeros((RHS, RANK), F32)
    for b in range(BOXES):
        block_ref[b, :, :LEAF] = vectors[b]
        extra = lifted[b] if b < UP else nothing
        block_ref[b, :, LEAF:] = jnp.concatenate(
            [coefficients[b].astype(F32), extra], axis=1
        ).astype(BF16)


def pack_kernel(me_ref, own_ref, up_ref, down_ref, top_ref, out_ref):
    me = me_ref[0]
    home, core = me & 7, me & 1
    prev_is_up = ((me >> 3) & 1) == 1
    low = iota((RHS, 128), 1) < RANK
    third = jnp.where(low, own_ref[3, :, LEAF:].astype(F32), up_ref[3, :, LEAF:].astype(F32))
    fourth = jnp.where(low, own_ref[4, :, LEAF:].astype(F32), top_ref[...])
    for chip in range(CHIPS):
        out_ref[chip, 0] = own_ref[...]
        out_ref[chip, 0, 3, :, LEAF:] = third.astype(BF16)
        out_ref[chip, 0, 4, :, LEAF:] = fourth.astype(BF16)
        use_prev = home > 2 * chip + 1 - core
        use_up = use_prev == prev_is_up

        @pl.when(use_up)
        def _():
            out_ref[chip, 1] = up_ref[...]

        @pl.when(jnp.logical_not(use_up))
        def _():
            out_ref[chip, 1] = down_ref[...]


def stage_kernel(
    count_ref,
    scale_ref,
    after_any,
    vectors_any,
    tiles_any,
    basis_any,
    transfer_any,
    coupling_any,
    level_any,
    near_ref,
    basis_ref,
    transfer_ref,
    coupling_ref,
    level_ref,
    kept_ref,
    vectors,
    mine,
    sems,
    keep_sems,
):
    copies = [pltpu.make_async_copy(vectors_any, vectors, keep_sems.at[5])]
    copies += [
        pltpu.make_async_copy(tiles_any.at[pl.ds(b, 4), 0], mine.at[pl.ds(b, 4)], sems.at[b // 4])
        for b in range(0, BOXES, 4)
    ]
    pairs = (
        (tiles_any.at[:, pl.ds(1, NEAR - 1)], kept_ref),
        (coupling_any, coupling_ref),
        (transfer_any, transfer_ref),
        (basis_any, basis_ref),
        (level_any, level_ref),
    )
    keeps = [pltpu.make_async_copy(a, b, keep_sems.at[i]) for i, (a, b) in enumerate(pairs)]
    for copy in copies + keeps:
        copy.start()
    copies[0].wait()
    for first in range(0, BOXES, 4):
        copies[1 + first // 4].wait()
        parts = [nt(vectors[b], mine[b]) for b in range(first, first + 4)]
        for b in range(first, first + 4):
            weight = jnp.where(count_ref[b] > 0, scale_ref[0, b], 0.0)
            near_ref[b] = weight * parts[b - first]
    for keep in keeps:
        keep.wait()


def final_kernel(
    me_ref,
    count_ref,
    scale_ref,
    place_any,
    same_any,
    other_any,
    near,
    basis,
    transfer,
    coupling,
    level,
    tiles,
    out_ref,
    window,
    place,
    sems,
):
    copies = [
        pltpu.make_async_copy(place_any, place, sems.at[0]),
        pltpu.make_async_copy(same_any, window.at[0], sems.at[1]),
        pltpu.make_async_copy(other_any, window.at[1], sems.at[2]),
    ]
    for copy in copies:
        copy.start()
    for copy in copies:
        copy.wait()
    home, core = me_ref[0] & 7, me_ref[0] & 1

    groups = [jnp.zeros((RHS, 128), F32) for _ in range(UP)]
    for half in range(2):
        for chip in range(CHIPS):
            apart = home ^ (2 * chip + (core ^ half))
            for k in range(UP):
                piece = window[half, chip, 0, k, :, LEAF:].astype(F32)
                if k < 3:
                    piece = jnp.where((apart >> k) == 1, piece, 0.0)
                groups[k] = groups[k] + piece
    far_field = jnp.zeros((RHS, RANK), F32)
    for k in range(UP):
        far_field = far_field + nn(groups[k][:, RANK:].astype(BF16), level[0, k].astype(BF16))
    far_field = far_field.astype(BF16)

    def entry(row, b):
        at = place[row, b]
        return at >> 7, (at >> 5) & 3, (at >> 4) & 1, at & 15

    low = iota((RHS, 128), 1) < RANK
    leaves = []
    for b in range(BOXES):
        halves = [window[(*entry(8 + s, b), slice(None), slice(LEAF, WIDE))].astype(F32) for s in range(FAR)]
        joined = jnp.concatenate(
            [
                jnp.where(low, halves[2 * i], pltpu.roll(halves[2 * i + 1], RANK, 1))
                for i in range(FAR // 2)
            ],
            axis=1,
        ).astype(BF16)
        leaves.append(nt(joined, coupling[b]))
    leaves = [(leaves[b] + nt(far_field, transfer[b])).astype(BF16) for b in range(BOXES)]
    for b in range(BOXES):
        out_ref[b] = near[b] + nn(leaves[b], basis[b])
    for first in range(0, BOXES, 2):
        pair = range(first, first + 2)
        parts = [
            [
                nt(window[(*entry(s, b), slice(None), slice(0, LEAF))], tiles[b, s - 1])
                for s in range(1, NEAR)
            ]
            for b in pair
        ]
        for b in pair:
            total = out_ref[b]
            for s in range(1, NEAR):
                weight = jnp.where(s < count_ref[b], scale_ref[s, b], 0.0)
                total = total + weight * parts[b - first][s - 1]
            out_ref[b] = total


def pairwise(block, partner):
    count = lax.axis_size("pts")
    route = [(i, partner(i)) for i in range(count) if 0 <= partner(i) < count]
    return lax.ppermute(block, "pts", route)


def shape_of(shape, dtype):
    return jax.ShapeDtypeStruct(shape, dtype)


def per_device(
    vectors,
    leaf_basis,
    leaf_transfer,
    leaf_coupling,
    near_tiles,
    tile_scale,
    near_boxes,
    near_counts,
    far_boxes,
    level_up,
    level_coupling,
):
    count = lax.axis_size("pts")
    rows = [
        [LINE * i + CORES * c + k for c in range(CHIPS)]
        for i in range(count // LINE)
        for k in range(CORES)
    ]
    me = lax.axis_index("pts").astype(I32).reshape(1)
    scales = tile_scale.T

    def off(x):
        return pltpu.with_memory_space_constraint(x, pltpu.HBM)

    block, place = pl.pallas_call(
        front_kernel,
        out_shape=(
            shape_of((BOXES, RHS, WIDE), BF16),
            shape_of((BOXES, 128), I32),
        ),
        in_specs=[SMEM, VMEM, VMEM] + [ANY] * 4,
        out_specs=(VMEM,) * 2,
        scratch_shapes=[
            pltpu.VMEM((BOXES, RHS, LEAF), BF16),
            pltpu.VMEM((BOXES, RANK, LEAF), BF16),
            pltpu.VMEM((BOXES, RANK, RANK), BF16),
            pltpu.VMEM((1, UP, RANK, RANK), F32),
            pltpu.SemaphoreType.DMA((4,)),
        ],
        compiler_params=pltpu.CompilerParams(vmem_limit_bytes=8 * MIB),
        name="front",
    )(
        me,
        off(near_boxes.T),
        off(far_boxes.T),
        off(vectors),
        off(leaf_basis),
        off(leaf_transfer),
        off(level_up),
    )

    up = pairwise(block, lambda i: LINE * partner_up(i // LINE) + i % LINE)
    down = pairwise(block, lambda i: LINE * partner_down(i // LINE) + i % LINE)
    tops = block[UP - 1, :, LEAF:].astype(F32) + up[UP - 1, :, LEAF:].astype(F32)
    top = pairwise(tops, lambda i: i ^ (2 * LINE))

    parcels = pl.pallas_call(
        pack_kernel,
        out_shape=shape_of((CHIPS, 2, BOXES, RHS, WIDE), BF16),
        in_specs=[SMEM] + [VMEM] * 4,
        out_specs=VMEM,
        compiler_params=pltpu.CompilerParams(vmem_limit_bytes=8 * MIB),
        name="pack",
    )(me, block, up, down, top)
    same = lax.all_to_all(parcels, "pts", 0, 0, axis_index_groups=rows)
    other = pairwise(same, lambda i: i ^ 1)

    near, basis, transfer, coupling, level, kept = pl.pallas_call(
        stage_kernel,
        out_shape=(
            pltpu.VMEM((BOXES, RHS, LEAF), F32),
            pltpu.VMEM((BOXES, RANK, LEAF), BF16),
            pltpu.VMEM((BOXES, RANK, RANK), BF16),
            pltpu.VMEM((BOXES, RANK, FAR * RANK), BF16),
            pltpu.VMEM((1, UP, RANK, RANK), F32),
            pltpu.VMEM((BOXES, NEAR - 1, LEAF, LEAF), BF16),
        ),
        in_specs=[SMEM, SMEM] + [ANY] * 7,
        out_specs=(VMEM,) + (ANY,) * 5,
        scratch_shapes=[
            pltpu.VMEM((BOXES, RHS, LEAF), BF16),
            pltpu.VMEM((BOXES, LEAF, LEAF), BF16),
            pltpu.SemaphoreType.DMA((4,)),
            pltpu.SemaphoreType.DMA((6,)),
        ],
        compiler_params=pltpu.CompilerParams(vmem_limit_bytes=16 * MIB),
        name="stage",
    )(
        off(near_counts),
        off(scales),
        parcels,
        off(vectors),
        off(near_tiles),
        off(leaf_basis),
        off(leaf_transfer),
        off(leaf_coupling),
        off(level_coupling),
    )

    return pl.pallas_call(
        final_kernel,
        out_shape=shape_of((BOXES, RHS, LEAF), F32),
        in_specs=[SMEM] * 3 + [ANY] * 3 + [VMEM] * 6,
        out_specs=VMEM,
        scratch_shapes=[
            pltpu.VMEM((2, CHIPS, 2, BOXES, RHS, WIDE), BF16),
            pltpu.SMEM((BOXES, 128), I32),
            pltpu.SemaphoreType.DMA((3,)),
        ],
        compiler_params=pltpu.CompilerParams(vmem_limit_bytes=16 * MIB),
        name="final",
    )(
        me,
        off(near_counts),
        off(scales),
        place,
        same,
        other,
        near,
        basis,
        transfer,
        coupling,
        level,
        kept,
    )


def solution(mesh):
    placed = (
        P("pts", None, None),
        P("pts", None, None),
        P("pts", None, None),
        P("pts", None, None),
        P("pts", None, None, None),
        P("pts", None),
        P("pts", None),
        P("pts"),
        P("pts", None),
        P("pts", None, None, None),
        P("pts", None, None, None),
    )
    return jax.shard_map(
        per_device, mesh=mesh, in_specs=placed, out_specs=P("pts", None, None), check_vma=False
    )
```

time: 142 us -> 41.3 us (0.29); the launches traced: 140 us -> 41.1 us
  starting transfers between devices: 111 us -> 12.4 us
  matrix products: 15.6 us -> 0 us
  blocking collectives: 0 us -> 13.2 us
  Pallas kernels: 0 us -> 12.1 us
  local copies, waits for them, and re-layouts: 6.37 us -> 0 us
  other arithmetic: 2.8 us -> 0.01 us
    ppermute x33 -> x4, starting transfers between devices: 111 us -> 12.4 us  [pairwise(): return lax.ppermute(block, 'pts', route)]
    dot_general x12 -> x0, matrix products: 15.6 us -> none  [the longest x1 5.65 us: per_device(): jnp.einsum('bsrj,bsij->bsri', gathered, near_tiles, preferred_element_typ...]
    all_to_all x0 -> x1, blocking collectives: none -> 13.2 us  [per_device(): same = lax.all_to_all(parcels, 'pts', 0, 0, axis_index_groups=rows)]
    pallas_call x0 -> x4, Pallas kernels: none -> 12.1 us  [the longest x1 4.83 us: per_device(): pl.pallas_call(stage_kernel, out_shape=(pltpu.VMEM((BOXES, RHS, LEAF), F3...]
    reshape x3 -> x0, local copies, waits for them, and re-layouts: 1.97 us -> none  [the longest x1 1.78 us: per_device(): coupling = leaf_coupling.reshape(box_count, rank_size, far_slots, rank_size)]
    gather x3 -> x0, local copies, waits for them, and re-layouts: 1.52 us -> none  [the longest x2 0.93 us: per_device(): jnp.take(window_q, far_boxes - window_start, axis=0)]
    ppermute x33 -> x4, waiting for transfers between devices: 3.7 us -> 3.35 us  [pairwise(): return lax.ppermute(block, 'pts', route)]
  transfers between devices with their start and end apart: 33 -> 4, of which waited for: 2 -> 2; matrix products, arithmetic and copies ran while one was open for 11% -> 0% of each run, Pallas kernels for 0% -> 12%
where the time goes in v2:
time: 41.3 us; the launch traced here: 41.1 us
  blocking collectives  13.2 us (32%)
  starting transfers between devices  12.4 us (30%)
  Pallas kernels  12.1 us (29%)
  waiting for transfers between devices  3.35 us (8%)
    all_to_all x1, blocking collectives, per_device(): same = lax.all_to_all(parcels, 'pts', 0, 0, axis_index_groups=rows)  13.2 us
    ppermute x4, starting transfers between devices, pairwise(): return lax.ppermute(block, 'pts', route)  12.4 us
    pallas_call x1, Pallas kernels, per_device(): pl.pallas_call(stage_kernel, out_shape=(pltpu.VMEM((BOXES, RHS, LEAF), F3...  4.83 us
    pallas_call x1, Pallas kernels, per_device(): pl.pallas_call(final_kernel, out_shape=shape_of((BOXES, RHS, LEAF), F32),...  4.55 us
    ppermute x4, waiting for transfers between devices, pairwise(): return lax.ppermute(block, 'pts', route)  3.35 us
    pallas_call x1, Pallas kernels, per_device(): pl.pallas_call(front_kernel, out_shape=(shape_of((BOXES, RHS, WIDE), BF16...  2.6 us
  transfers between devices with their start and end apart: 4, of which 2 were waited for; matrix products, arithmetic and copies ran while one was open for 0% of the time, Pallas kernels for 12%

profile of v2, /device:TPU:25, one launch (start us, length us, event | category | flops | bytes accessed | tf_op | source)
XLA Modules:
  0.0 41.1 jit_solution(10626523426885830067)
XLA Ops:
  0.0 2.6 %front.1 = (bf16[16,8,384]{2,1,0:T(8,128)(2,1)S(1)}, s32[16,128]{1,0:T(8,128)S(1)}) custom-call(s32[1]{0:T(128)} %bitcast.me_ref, s32[4,16]{1,0:T(4,128)} %bitcast.9, s32[6,16]{1,0:T(8,128)} %bitcast.8, bf16[16,8,256]{2,1,0:T(8,128)(2,1)} %vectors_any.3, bf16[16,64,256]{2,1,0:T(8,128)(2,1)} %basis_any.3, bf16[16,64,64]{2,1,0:T(8,128)(2,1)} %transfer_any.3, ...), custom_call_target="tpu_custom_call" | custom-call | tf_op jit(solution)/shard_map/front/pallas_call | solution.py:279
  2.6 1.7 %collective-permute-start = (bf16[16,8,384]{2,1,0:T(8,128)(2,1)S(1)}, bf16[16,8,384]{2,1,0:T(8,128)(2,1)S(1)}, u32[]{:S(2)}, u32[]{:S(2)}) collective-permute-start(bf16[16,8,384]{2,1,0:T(8,128)(2,1)S(1)} %get-tuple-element.14.own_ref), channel_id=1, source_target_pairs={{0,8},{1,9},{2,10},{3,11},{4,12},{5,13},{6,14},{7,15},{8,0},{9,1},... | collective-permute-start | bytes 294920 | tf_op jit(solution)/shard_map/ppermute | solution.py:247
  4.3 6.7 %collective-permute-start.1 = (bf16[16,8,384]{2,1,0:T(8,128)(2,1)S(1)}, bf16[16,8,384]{2,1,0:T(8,128)(2,1)S(1)}, u32[]{:S(2)}, u32[]{:S(2)}) collective-permute-start(bf16[16,8,384]{2,1,0:T(8,128)(2,1)S(1)} %get-tuple-element.14.own_ref), channel_id=1, source_target_pairs={{8,16},{9,17},{10,18},{11,19},{12,20},{13,21},{14,22},{15,23},{16,... | collective-permute-start | bytes 294920 | tf_op jit(solution)/shard_map/ppermute | solution.py:247
  11.1 0.0 collective-permute-done.up_ref
  11.1 0.1 collective-permute-start.2
  11.2 1.9 %collective-permute-done.1.down_ref = bf16[16,8,384]{2,1,0:T(8,128)(2,1)S(1)} collective-permute-done((bf16[16,8,384]{2,1,0:T(8,128)(2,1)S(1)}, bf16[16,8,384]{2,1,0:T(8,128)(2,1)S(1)}, u32[]{:S(2)}, u32[]{:S(2)}) %collective-permute-start.1) | collective-permute-done | bytes 98336 | tf_op jit(solution)/shard_map/ppermute | solution.py:247
  13.1 1.5 %collective-permute-done.2.top_ref = f32[8,128]{1,0:T(8,128)S(1)} collective-permute-done((f32[8,128]{1,0:T(8,128)S(1)}, f32[8,128]{1,0:T(8,128)S(1)}, u32[]{:S(2)}, u32[]{:S(2)}) %collective-permute-start.2) | collective-permute-done | bytes 4128 | tf_op jit(solution)/shard_map/ppermute | solution.py:247
  14.6 0.1 pack.1.after_any
  14.6 13.2 %all_to_all.5.same_any = bf16[4,2,16,8,384]{4,3,2,1,0:T(8,128)(2,1)S(1)} all-to-all(bf16[4,2,16,8,384]{4,3,2,1,0:T(8,128)(2,1)S(1)} %pack.1.after_any), channel_id=1, replica_groups={{0,2,4,6},{1,3,5,7},{8,10,12,14},{9,11,13,15},{16,18,20,22},{17,19,21,2..., dimensions={0} | all-to-all | bytes 1572864 | tf_op jit(solution)/shard_map/all_to_all | solution.py:319
  27.8 3.9 %collective-permute-start.3 = (bf16[4,2,16,8,384]{4,3,2,1,0:T(8,128)(2,1)S(1)}, bf16[4,2,16,8,384]{4,3,2,1,0:T(8,128)(2,1)S(1)}, u32[]{:S(2)}, u32[]{:S(2)}) collective-permute-start(bf16[4,2,16,8,384]{4,3,2,1,0:T(8,128)(2,1)S(1)} %all_to_all.5.same_any), channel_id=1, source_target_pairs={{0,1},{1,0},{2,3},{3,2},{4,5},{5,4},{6,7},{7,6},{8,9},{9,8},{10,11... | collective-permute-start | bytes 2359304 | tf_op jit(solution)/shard_map/ppermute | solution.py:247
  31.7 4.8 %stage.1 = (f32[16,8,256]{2,1,0:T(8,128)S(1)}, bf16[16,64,256]{2,1,0:T(8,128)(2,1)S(1)}, bf16[16,64,64]{2,1,0:T(8,128)(2,1)S(1)}, bf16[16,64,384]{2,1,0:T(8,128)...) custom-call(s32[16]{0:T(128)} %count_ref.3, f32[4,16]{1,0:T(4,128)} %bitcast.6, ...), custom_call_target="tpu_custom_call" | custom-call | tf_op jit(solution)/shard_map/stage/pallas_call | solution.py:322
  36.5 0.0 collective-permute-done.3.other_any
  36.5 4.6 %final.1 = f32[16,8,256]{2,1,0:T(8,128)} custom-call(s32[1]{0:T(128)} %bitcast.me_ref, s32[16]{0:T(128)} %count_ref.3, f32[4,16]{1,0:T(4,128)} %bitcast.7, s32[16,128]{1,0:T(8,128)S(1)} %get-tuple-element.13.place_any, bf16[4,2,16,8,384]{4,3,2,1,0:T(8,128)(2,1)S(1)} %all_to_all.5.same_any, bf16[4,2,16,8,384]{4,3,2,1,0:T(8,128)(2,1)S(1)} %collective-permute-done.3.other_any, ...), custom_call_target="tpu_custom_call" | custom-call | tf_op jit(solution)/shard_map/final/pallas_call | solution.py:354
  (1 shorter events, 0.0 us)
Async XLA Ops:
  2.6 8.5 %collective-permute-start = (bf16[16,8,384]{2,1,0:T(8,128)(2,1)S(1)}, bf16[16,8,384]{2,1,0:T(8,128)(2,1)S(1)}, u32[]{:S(2)}, u32[]{:S(2)}) collective-permute-start(bf16[16,8,384]{2,1,0:T(8,128)(2,1)S(1)} %get-tuple-element.14.own_ref), channel_id=1, source_target_pairs={{0,8},{1,9},{2,10},{3,11},{4,12},{5,13},{6,14},{7,15},{8,0},{9,1},... | collective-permute-start | bytes 294920 | tf_op jit(solution)/shard_map/ppermute | solution.py:247
  4.3 8.7 %collective-permute-start.1 = (bf16[16,8,384]{2,1,0:T(8,128)(2,1)S(1)}, bf16[16,8,384]{2,1,0:T(8,128)(2,1)S(1)}, u32[]{:S(2)}, u32[]{:S(2)}) collective-permute-start(bf16[16,8,384]{2,1,0:T(8,128)(2,1)S(1)} %get-tuple-element.14.own_ref), channel_id=1, source_target_pairs={{8,16},{9,17},{10,18},{11,19},{12,20},{13,21},{14,22},{15,23},{16,... | collective-permute-start | bytes 294920 | tf_op jit(solution)/shard_map/ppermute | solution.py:247
  11.1 3.4 %collective-permute-start.2 = (f32[8,128]{1,0:T(8,128)S(1)}, f32[8,128]{1,0:T(8,128)S(1)}, u32[]{:S(2)}, u32[]{:S(2)}) collective-permute-start(f32[8,128]{1,0:T(8,128)S(1)} %add_bitcast_fusion), channel_id=1, source_target_pairs={{0,16},{1,17},{2,18},{3,19},{4,20},{5,21},{6,22},{7,23},{8,24},{9,... | collective-permute-start | bytes 12296 | tf_op jit(solution)/shard_map/ppermute | solution.py:247
  27.8 8.7 %collective-permute-start.3 = (bf16[4,2,16,8,384]{4,3,2,1,0:T(8,128)(2,1)S(1)}, bf16[4,2,16,8,384]{4,3,2,1,0:T(8,128)(2,1)S(1)}, u32[]{:S(2)}, u32[]{:S(2)}) collective-permute-start(bf16[4,2,16,8,384]{4,3,2,1,0:T(8,128)(2,1)S(1)} %all_to_all.5.same_any), channel_id=1, source_target_pairs={{0,1},{1,0},{2,3},{3,2},{4,5},{5,4},{6,7},{7,6},{8,9},{9,8},{10,11... | collective-permute-start | bytes 2359304 | tf_op jit(solution)/shard_map/ppermute | solution.py:247

commit v3 on v2

v3 whole, which is shorter than its diff:
```python
import jax
import jax.numpy as jnp
from jax import lax
from jax.experimental import pallas as pl
from jax.experimental.pallas import tpu as pltpu
from jax.sharding import PartitionSpec as P

LEAF = 256
RANK = 64
RHS = 8
NEAR = 4
FAR = 6
UP = 5
BOXES = 16
LINE = 8
CHIPS = 4
CORES = 2
WIDE = LEAF + 2 * RANK
MIB = 1024 * 1024

F32 = jnp.float32
BF16 = jnp.bfloat16
I32 = jnp.int32
VMEM = pl.BlockSpec(memory_space=pltpu.VMEM)
SMEM = pl.BlockSpec(memory_space=pltpu.SMEM)
ANY = pl.BlockSpec(memory_space=pl.ANY)


def nt(a, b):
    return lax.dot_general(a, b, (((1,), (1,)), ((), ())), preferred_element_type=F32)


def nn(a, b):
    return lax.dot_general(a, b, (((1,), (0,)), ((), ())), preferred_element_type=F32)


def iota(shape, dim):
    return lax.broadcasted_iota(I32, shape, dim)


def partner_up(line):
    return line ^ 1


def partner_down(line):
    return ((line + 1) ^ 1) - 1


def front_kernel(
    me_ref,
    near_any,
    far_any,
    count_any,
    scale_any,
    vectors_any,
    basis_any,
    transfer_any,
    up_any,
    block_ref,
    place_ref,
    weight_ref,
    near,
    far,
    count,
    scale,
    vectors,
    basis,
    transfer,
    up,
    sems,
):
    pairs = (
        (vectors_any, vectors),
        (basis_any, basis),
        (transfer_any, transfer),
        (up_any, up),
        (near_any, near),
        (far_any, far),
        (count_any, count),
        (scale_any, scale),
    )
    copies = [pltpu.make_async_copy(a, b, sems.at[i]) for i, (a, b) in enumerate(pairs)]
    for copy in copies:
        copy.start()
    copies[0].wait()
    copies[1].wait()
    coefficients = [nt(vectors[b], basis[b]).astype(BF16) for b in range(BOXES)]
    copies[2].wait()
    total = jnp.zeros((RHS, RANK), F32)
    for b in range(BOXES):
        total = total + nn(coefficients[b], transfer[b])
    total = total.astype(BF16)
    copies[3].wait()
    lifted = [nn(total, up[0, k].astype(BF16)) for k in range(UP)]
    nothing = jnp.zeros((RHS, RANK), F32)
    for b in range(BOXES):
        block_ref[b, :, :LEAF] = vectors[b]
        extra = lifted[b] if b < UP else nothing
        block_ref[b, :, LEAF:] = jnp.concatenate(
            [coefficients[b].astype(F32), extra], axis=1
        ).astype(BF16)
    for copy in copies[4:]:
        copy.wait()
    me = me_ref[0]
    line, home, core = me >> 3, (me >> 1) & 3, me & 1
    place_ref[...] = jnp.full((BOXES, 128), me, I32)
    for first, ref in ((0, near), (8, far)):
        box = ref[...]
        apart = ((box >> 4) & 1) ^ core
        beside = ((box >> 7) != line).astype(I32)
        chip = ((box >> 5) & 3) ^ home
        place = (apart << 7) | (beside << 6) | (chip << 4) | (box & 15)
        place_ref[first : first + box.shape[0], 0:BOXES] = place
    used = iota((NEAR, BOXES), 0) < jnp.broadcast_to(count[...].reshape(1, BOXES), (NEAR, BOXES))
    weight_ref[0:NEAR, 0:BOXES] = jnp.where(used, scale[...], 0.0)


def join_kernel(near_any, own_ref, first_ref, second_ref, third_ref, line_ref, top_ref):
    top = jnp.zeros((RHS, 128), F32)
    for k, ref in enumerate((own_ref, first_ref, second_ref, third_ref)):
        line_ref[k] = ref[...]
        top = top + ref[UP - 1, :, LEAF:].astype(F32)
    top_ref[...] = top


def pack_kernel(me_ref, ready_any, line_ref, up_ref, down_ref, third, top_a, top_b, out_ref):
    me = me_ref[0]
    home, core = me & 7, me & 1
    prev_is_up = ((me >> 3) & 1) == 1
    out_ref[0] = line_ref[...]
    for k in range(CHIPS):
        use_prev = (home ^ (2 * k)) > home if k else core == 1
        use_up = use_prev == prev_is_up

        @pl.when(use_up)
        def _():
            out_ref[1, k] = up_ref[k]

        @pl.when(jnp.logical_not(use_up))
        def _():
            out_ref[1, k] = down_ref[k]

    low = iota((RHS, 128), 1) < RANK
    for box, levels in ((3, third[...]), (4, top_a[...] + top_b[...])):
        mixed = jnp.where(low, line_ref[0, box, :, LEAF:].astype(F32), levels)
        out_ref[0, 0, box, :, LEAF:] = mixed.astype(BF16)


def own_kernel(weight_any, after_any, vectors_any, tiles_any, near_ref, weight, vectors, mine, sems):
    copies = [
        pltpu.make_async_copy(vectors_any, vectors, sems.at[4]),
        pltpu.make_async_copy(weight_any, weight, sems.at[5]),
    ]
    parts = [
        pltpu.make_async_copy(tiles_any.at[pl.ds(b, 4), 0], mine.at[pl.ds(b, 4)], sems.at[b // 4])
        for b in range(0, BOXES, 4)
    ]
    for copy in copies + parts:
        copy.start()
    for copy in copies:
        copy.wait()
    for first in range(0, BOXES, 4):
        parts[first // 4].wait()
        products = [nt(vectors[b], mine[b]) for b in range(first, first + 4)]
        for b in range(first, first + 4):
            near_ref[b] = weight[0, b] * products[b - first]


def stage_kernel(
    after_any,
    tiles_any,
    basis_any,
    transfer_any,
    coupling_any,
    level_any,
    tiles_ref,
    basis_ref,
    transfer_ref,
    coupling_ref,
    level_ref,
    ready_ref,
    sems,
):
    pairs = (
        (tiles_any.at[:, pl.ds(1, NEAR - 1)], tiles_ref),
        (coupling_any, coupling_ref),
        (transfer_any, transfer_ref),
        (basis_any, basis_ref),
        (level_any, level_ref),
    )
    copies = [pltpu.make_async_copy(a, b, sems.at[i]) for i, (a, b) in enumerate(pairs)]
    for copy in copies:
        copy.start()
    ready_ref[...] = jnp.zeros((8, 128), F32)
    for copy in copies:
        copy.wait()


def final_kernel(
    place_any,
    weight_any,
    same_any,
    other_any,
    near,
    tiles,
    basis,
    transfer,
    coupling,
    level,
    out_any,
    window,
    place,
    weight,
    out,
    sems,
    out_sems,
):
    pairs = (
        (place_any, place),
        (weight_any, weight),
        (same_any, window.at[0]),
        (other_any, window.at[1]),
    )
    copies = [pltpu.make_async_copy(a, b, sems.at[i]) for i, (a, b) in enumerate(pairs)]
    for copy in copies:
        copy.start()
    for copy in copies:
        copy.wait()

    def entry(row, b):
        at = place[row, b]
        return at >> 7, (at >> 6) & 1, (at >> 4) & 3, at & 15

    def levels(half, k, level):
        return window[half, 0, k, level, :, LEAF:].astype(F32)

    groups = [
        levels(1, 0, 0),
        levels(0, 1, 1) + levels(1, 1, 1),
        levels(0, 2, 2) + levels(1, 2, 2) + levels(0, 3, 2) + levels(1, 3, 2),
        levels(0, 0, 3) + levels(1, 0, 3),
        levels(0, 0, 4) + levels(1, 0, 4),
    ]
    far_field = jnp.zeros((RHS, RANK), F32)
    for k in range(UP):
        far_field = far_field + nn(groups[k][:, RANK:].astype(BF16), level[0, k].astype(BF16))
    far_field = far_field.astype(BF16)

    low = iota((RHS, 128), 1) < RANK
    leaves = []
    for b in range(BOXES):
        halves = [
            window[(*entry(8 + s, b), slice(None), slice(LEAF, WIDE))].astype(F32)
            for s in range(FAR)
        ]
        joined = jnp.concatenate(
            [
                jnp.where(low, halves[2 * i], pltpu.roll(halves[2 * i + 1], RANK, 1))
                for i in range(FAR // 2)
            ],
            axis=1,
        ).astype(BF16)
        leaves.append(nt(joined, coupling[b]))
    leaves = [(leaves[b] + nt(far_field, transfer[b])).astype(BF16) for b in range(BOXES)]
    for b in range(BOXES):
        out[b] = near[b] + nn(leaves[b], basis[b])
    outs = []
    for first in range(0, BOXES, 2):
        parts = [
            [
                nt(window[(*entry(s, b), slice(None), slice(0, LEAF))], tiles[b, s - 1])
                for s in range(1, NEAR)
            ]
            for b in range(first, first + 2)
        ]
        for b in range(first, first + 2):
            total = out[b]
            for s in range(1, NEAR):
                total = total + weight[s, b] * parts[b - first][s - 1]
            out[b] = total
        if first % 8 == 6:
            rows = pl.ds(first - 6, 8)
            outs.append(
                pltpu.make_async_copy(out.at[rows], out_any.at[rows], out_sems.at[first // 8])
            )
            outs[-1].start()
    for copy in outs:
        copy.wait()


def pairwise(block, partner):
    count = lax.axis_size("pts")
    route = [(i, partner(i)) for i in range(count) if 0 <= partner(i) < count]
    return lax.ppermute(block, "pts", route)


def shape_of(shape, dtype):
    return jax.ShapeDtypeStruct(shape, dtype)


def per_device(
    vectors,
    leaf_basis,
    leaf_transfer,
    leaf_coupling,
    near_tiles,
    tile_scale,
    near_boxes,
    near_counts,
    far_boxes,
    level_up,
    level_coupling,
):
    me = lax.axis_index("pts").astype(I32).reshape(1)

    def off(x):
        return pltpu.with_memory_space_constraint(x, pltpu.HBM)

    block, place, weight = pl.pallas_call(
        front_kernel,
        out_shape=(
            shape_of((BOXES, RHS, WIDE), BF16),
            shape_of((BOXES, 128), I32),
            shape_of((8, 128), F32),
        ),
        in_specs=[SMEM] + [ANY] * 8,
        out_specs=(VMEM,) * 3,
        scratch_shapes=[
            pltpu.VMEM((NEAR, BOXES), I32),
            pltpu.VMEM((FAR, BOXES), I32),
            pltpu.VMEM((BOXES,), I32),
            pltpu.VMEM((NEAR, BOXES), F32),
            pltpu.VMEM((BOXES, RHS, LEAF), BF16),
            pltpu.VMEM((BOXES, RANK, LEAF), BF16),
            pltpu.VMEM((BOXES, RANK, RANK), BF16),
            pltpu.VMEM((1, UP, RANK, RANK), F32),
            pltpu.SemaphoreType.DMA((8,)),
        ],
        compiler_params=pltpu.CompilerParams(vmem_limit_bytes=8 * MIB),
        name="front",
    )(
        me,
        off(near_boxes.T),
        off(far_boxes.T),
        off(near_counts),
        off(tile_scale.T),
        off(vectors),
        off(leaf_basis),
        off(leaf_transfer),
        off(level_up),
    )

    near = pl.pallas_call(
        own_kernel,
        out_shape=shape_of((BOXES, RHS, LEAF), F32),
        in_specs=[ANY] * 4,
        out_specs=VMEM,
        scratch_shapes=[
            pltpu.SMEM((8, 128), F32),
            pltpu.VMEM((BOXES, RHS, LEAF), BF16),
            pltpu.VMEM((BOXES, LEAF, LEAF), BF16),
            pltpu.SemaphoreType.DMA((6,)),
        ],
        compiler_params=pltpu.CompilerParams(vmem_limit_bytes=8 * MIB),
        name="own",
    )(weight, block, off(vectors), off(near_tiles))

    line, tops = pl.pallas_call(
        join_kernel,
        out_shape=(
            shape_of((CHIPS, BOXES, RHS, WIDE), BF16),
            shape_of((RHS, 128), F32),
        ),
        in_specs=[ANY] + [VMEM] * CHIPS,
        out_specs=(VMEM, VMEM),
        compiler_params=pltpu.CompilerParams(vmem_limit_bytes=4 * MIB),
        name="join",
    )(
        near,
        block,
        *[pairwise(block, lambda i, k=k: i ^ (CORES * k)) for k in range(1, CHIPS)],
    )

    tiles, basis, transfer, coupling, level, ready = pl.pallas_call(
        stage_kernel,
        out_shape=(
            pltpu.VMEM((BOXES, NEAR - 1, LEAF, LEAF), BF16),
            pltpu.VMEM((BOXES, RANK, LEAF), BF16),
            pltpu.VMEM((BOXES, RANK, RANK), BF16),
            pltpu.VMEM((BOXES, RANK, FAR * RANK), BF16),
            pltpu.VMEM((1, UP, RANK, RANK), F32),
            shape_of((8, 128), F32),
        ),
        in_specs=[ANY] * 6,
        out_specs=(ANY,) * 5 + (VMEM,),
        scratch_shapes=[pltpu.SemaphoreType.DMA((5,))],
        compiler_params=pltpu.CompilerParams(vmem_limit_bytes=4 * MIB),
        name="stage",
    )(
        tops,
        off(near_tiles),
        off(leaf_basis),
        off(leaf_transfer),
        off(leaf_coupling),
        off(level_coupling),
    )

    up = pairwise(line, lambda i: LINE * partner_up(i // LINE) + i % LINE)
    down = pairwise(line, lambda i: LINE * partner_down(i // LINE) + i % LINE)
    third = up[:, 3, :, LEAF:].astype(F32).sum(axis=0)
    top_a = pairwise(tops, lambda i: i ^ (2 * LINE))
    top_b = pairwise(tops, lambda i: i ^ (3 * LINE))
    same = pl.pallas_call(
        pack_kernel,
        out_shape=shape_of((2, CHIPS, BOXES, RHS, WIDE), BF16),
        in_specs=[SMEM, ANY] + [VMEM] * 6,
        out_specs=VMEM,
        compiler_params=pltpu.CompilerParams(vmem_limit_bytes=4 * MIB),
        name="pack",
    )(me, ready, line, up, down, third, top_a, top_b)
    other = pairwise(same, lambda i: i ^ 1)

    return pl.pallas_call(
        final_kernel,
        out_shape=shape_of((BOXES, RHS, LEAF), F32),
        in_specs=[ANY] * 4 + [VMEM] * 6,
        out_specs=ANY,
        scratch_shapes=[
            pltpu.VMEM((CORES, 2, CHIPS, BOXES, RHS, WIDE), BF16),
            pltpu.SMEM((BOXES, 128), I32),
            pltpu.SMEM((8, 128), F32),
            pltpu.VMEM((BOXES, RHS, LEAF), F32),
            pltpu.SemaphoreType.DMA((4,)),
            pltpu.SemaphoreType.DMA((2,)),
        ],
        compiler_params=pltpu.CompilerParams(vmem_limit_bytes=16 * MIB),
        name="final",
    )(place, weight, same, other, near, tiles, basis, transfer, coupling, level)


def solution(mesh):
    placed = (
        P("pts", None, None),
        P("pts", None, None),
        P("pts", None, None),
        P("pts", None, None),
        P("pts", None, None, None),
        P("pts", None),
        P("pts", None),
        P("pts"),
        P("pts", None),
        P("pts", None, None, None),
        P("pts", None, None, None),
    )
    return jax.shard_map(
        per_device, mesh=mesh, in_specs=placed, out_specs=P("pts", None, None), check_vma=False
    )
```

time: 41.3 us -> 34.6 us (0.84)
  blocking collectives: 13.2 us -> 0 us
  starting transfers between devices: 12.4 us -> 17.1 us
  waiting for transfers between devices: 3.35 us -> 5.5 us
  Pallas kernels: 12.1 us -> 11.3 us
    all_to_all x1 -> x0, blocking collectives: 13.2 us -> none  [per_device(): same = lax.all_to_all(parcels, 'pts', 0, 0, axis_index_groups=rows)]
    ppermute x4 -> x8, starting transfers between devices: 12.4 us -> 17.1 us  [pairwise(): return lax.ppermute(block, 'pts', route)]
    ppermute x4 -> x8, waiting for transfers between devices: 3.35 us -> 5.5 us  [pairwise(): return lax.ppermute(block, 'pts', route)]
    pallas_call x1, Pallas kernels: 4.55 us -> 3.89 us  [per_device(): pl.pallas_call(final_kernel, out_shape=shape_of((BOXES, RHS, LEAF), F32),...]
    pallas_call x1, Pallas kernels: 2.6 us -> 1.95 us  [per_device(): pl.pallas_call(front_kernel, out_shape=(shape_of((BOXES, RHS, WIDE), BF16...]
    pallas_call x2 -> x4, Pallas kernels: 4.91 us -> 5.49 us  [the longest x1 3.22 us: per_device(): pl.pallas_call(stage_kernel, out_shape=(pltpu.VMEM((BOXES, NEAR - 1, LEAF...]
  transfers between devices with their start and end apart: 4 -> 8, of which waited for: 2 -> 5; matrix products, arithmetic and copies ran while one was open for 0% -> 0% of each run, Pallas kernels for 12% -> 16%
where the time goes in v3:
time: 34.6 us; the launch traced here: 34.1 us
  starting transfers between devices  17.1 us (49%)
  Pallas kernels  11.3 us (33%)
  waiting for transfers between devices  5.5 us (16%)
    ppermute x8, starting transfers between devices, pairwise(): return lax.ppermute(block, 'pts', route)  17.1 us
    ppermute x8, waiting for transfers between devices, pairwise(): return lax.ppermute(block, 'pts', route)  5.5 us
    pallas_call x1, Pallas kernels, per_device(): pl.pallas_call(final_kernel, out_shape=shape_of((BOXES, RHS, LEAF), F32),...  3.89 us
    pallas_call x1, Pallas kernels, per_device(): pl.pallas_call(stage_kernel, out_shape=(pltpu.VMEM((BOXES, NEAR - 1, LEAF...  3.22 us
    pallas_call x1, Pallas kernels, per_device(): pl.pallas_call(own_kernel, out_shape=shape_of((BOXES, RHS, LEAF), F32), i...  2.14 us
    pallas_call x1, Pallas kernels, per_device(): pl.pallas_call(front_kernel, out_shape=(shape_of((BOXES, RHS, WIDE), BF16...  1.95 us
  transfers between devices with their start and end apart: 8, of which 5 were waited for; matrix products, arithmetic and copies ran while one was open for 0% of the time, Pallas kernels for 16%

profile of v3, /device:TPU:25, one launch (start us, length us, event | category | flops | bytes accessed | tf_op | source)
XLA Modules:
  0.0 34.1 jit_solution(14292066522932883016)
XLA Ops:
  0.0 1.9 %front.1 = (bf16[16,8,384]{2,1,0:T(8,128)(2,1)S(1)}, s32[16,128]{1,0:T(8,128)S(1)}, f32[8,128]{1,0:T(8,128)S(1)}) custom-call(s32[1]{0:T(128)} %bitcast.me_ref, s32[4,16]{1,0:T(4,128)} %bitcast.5, s32[6,16]{1,0:T(8,128)} %bitcast.4, s32[16]{0:T(128)} %count_any.1, f32[4,16]{1,0:T(4,128)} %bitcast.6, bf16[16,8,256]{2,1,0:T(8,128)(2,1)} %vectors_any.3, ...), custom_call_target="tpu_custom_call" | custom-call | tf_op jit(solution)/shard_map/front/pallas_call | solution.py:319
  2.0 2.6 %collective-permute-start.2 = (bf16[16,8,384]{2,1,0:T(8,128)(2,1)S(1)}, bf16[16,8,384]{2,1,0:T(8,128)(2,1)S(1)}, u32[]{:S(2)}, u32[]{:S(2)}) collective-permute-start(bf16[16,8,384]{2,1,0:T(8,128)(2,1)S(1)} %get-tuple-element.18.after_any.own_ref), channel_id=1, source_target_pairs={{0,6},{1,7},{2,4},{3,5},{4,2},{5,3},{6,0},{7,1},{8,14},{9,15},{10,... | collective-permute-start | bytes 294920 | tf_op jit(solution)/shard_map/ppermute | solution.py:294
  4.5 0.5 %collective-permute-start.1 = (bf16[16,8,384]{2,1,0:T(8,128)(2,1)S(1)}, bf16[16,8,384]{2,1,0:T(8,128)(2,1)S(1)}, u32[]{:S(2)}, u32[]{:S(2)}) collective-permute-start(bf16[16,8,384]{2,1,0:T(8,128)(2,1)S(1)} %get-tuple-element.18.after_any.own_ref), channel_id=1, source_target_pairs={{0,4},{1,5},{2,6},{3,7},{4,0},{5,1},{6,2},{7,3},{8,12},{9,13},{10,... | collective-permute-start | bytes 294920 | tf_op jit(solution)/shard_map/ppermute | solution.py:294
  5.0 0.3 collective-permute-start
  5.3 2.1 %own.1.near_any.near = f32[16,8,256]{2,1,0:T(8,128)S(1)} custom-call(f32[8,128]{1,0:T(8,128)S(1)} %get-tuple-element.17.weight_any, bf16[16,8,384]{2,1,0:T(8,128)(2,1)S(1)} %get-tuple-element.18.after_any.own_ref, bf16[16,8,256]{2,1,0:T(8,128)(2,1)} %vectors_any.3, bf16[16,4,256,256]{3,2,1,0:T(8,128)(2,1)} %tiles_any.3), custom_call_target="tpu_custom_call" | custom-call | tf_op jit(solution)/shard_map/own/pallas_call | solution.py:353
  7.4 0.3 collective-permute-done.2.third_ref
  7.7 1.8 %collective-permute-done.1.second_ref = bf16[16,8,384]{2,1,0:T(8,128)(2,1)S(1)} collective-permute-done((bf16[16,8,384]{2,1,0:T(8,128)(2,1)S(1)}, bf16[16,8,384]{2,1,0:T(8,128)(2,1)S(1)}, u32[]{:S(2)}, u32[]{:S(2)}) %collective-permute-start.1) | collective-permute-done | bytes 98336 | tf_op jit(solution)/shard_map/ppermute | solution.py:294
  9.5 0.0 collective-permute-done.first_ref
  9.5 1.7 %collective-permute-start.3 = (bf16[4,16,8,384]{3,2,1,0:T(8,128)(2,1)S(1)}, bf16[4,16,8,384]{3,2,1,0:T(8,128)(2,1)S(1)}, u32[]{:S(2)}, u32[]{:S(2)}) collective-permute-start(bf16[4,16,8,384]{3,2,1,0:T(8,128)(2,1)S(1)} %get-tuple-element.21.line_ref), channel_id=1, source_target_pairs={{0,8},{1,9},{2,10},{3,11},{4,12},{5,13},{6,14},{7,15},{8,0},{9,1},... | collective-permute-start | bytes 1179656 | tf_op jit(solution)/shard_map/ppermute | solution.py:294
  11.3 6.7 %collective-permute-start.4 = (bf16[4,16,8,384]{3,2,1,0:T(8,128)(2,1)S(1)}, bf16[4,16,8,384]{3,2,1,0:T(8,128)(2,1)S(1)}, u32[]{:S(2)}, u32[]{:S(2)}) collective-permute-start(bf16[4,16,8,384]{3,2,1,0:T(8,128)(2,1)S(1)} %get-tuple-element.21.line_ref), channel_id=1, source_target_pairs={{8,16},{9,17},{10,18},{11,19},{12,20},{13,21},{14,22},{15,23},{16,... | collective-permute-start | bytes 1179656 | tf_op jit(solution)/shard_map/ppermute | solution.py:294
  18.0 1.5 %collective-permute-start.6 = (f32[8,128]{1,0:T(8,128)S(1)}, f32[8,128]{1,0:T(8,128)S(1)}, u32[]{:S(2)}, u32[]{:S(2)}) collective-permute-start(f32[8,128]{1,0:T(8,128)S(1)} %get-tuple-element.19.after_any), channel_id=1, source_target_pairs={{0,24},{1,25},{2,26},{3,27},{4,28},{5,29},{6,30},{7,31},{8,16},{9,... | collective-permute-start | bytes 12296 | tf_op jit(solution)/shard_map/ppermute | solution.py:294
  19.5 0.0 collective-permute-start.5
  19.6 3.2 %stage.1 = (bf16[16,3,256,256]{3,2,1,0:T(8,128)(2,1)S(1)}, bf16[16,64,256]{2,1,0:T(8,128)(2,1)S(1)}, bf16[16,64,64]{2,1,0:T(8,128)(2,1)S(1)}, bf16[16,64,384]{2,...) custom-call(f32[8,128]{1,0:T(8,128)S(1)} %get-tuple-element.19.after_any, ...), custom_call_target="tpu_custom_call" | custom-call | tf_op jit(solution)/shard_map/stage/pallas_call | solution.py:384
  22.8 0.0 collective-permute-done.3.up_ref
  22.8 0.0 collective-permute-done.6.top_b
  22.8 0.5 %collective-permute-done.5.top_a = f32[8,128]{1,0:T(8,128)S(1)} collective-permute-done((f32[8,128]{1,0:T(8,128)S(1)}, f32[8,128]{1,0:T(8,128)S(1)}, u32[]{:S(2)}, u32[]{:S(2)}) %collective-permute-start.5) | collective-permute-done | bytes 4128 | tf_op jit(solution)/shard_map/ppermute | solution.py:294
  23.3 1.0 %collective-permute-done.4.down_ref = bf16[4,16,8,384]{3,2,1,0:T(8,128)(2,1)S(1)} collective-permute-done((bf16[4,16,8,384]{3,2,1,0:T(8,128)(2,1)S(1)}, bf16[4,16,8,384]{3,2,1,0:T(8,128)(2,1)S(1)}, u32[]{:S(2)}, u32[]{:S(2)}) %collective-permute-start.4) | collective-permute-done | bytes 393248 | tf_op jit(solution)/shard_map/ppermute | solution.py:294
  24.3 0.1 pack.1.same_any
  24.4 3.8 %collective-permute-start.7 = (bf16[2,4,16,8,384]{4,3,2,1,0:T(8,128)(2,1)S(1)}, bf16[2,4,16,8,384]{4,3,2,1,0:T(8,128)(2,1)S(1)}, u32[]{:S(2)}, u32[]{:S(2)}) collective-permute-start(bf16[2,4,16,8,384]{4,3,2,1,0:T(8,128)(2,1)S(1)} %pack.1.same_any), channel_id=1, source_target_pairs={{0,1},{1,0},{2,3},{3,2},{4,5},{5,4},{6,7},{7,6},{8,9},{9,8},{10,11... | collective-permute-start | bytes 2359304 | tf_op jit(solution)/shard_map/ppermute | solution.py:294
  28.3 1.9 %collective-permute-done.7.other_any = bf16[2,4,16,8,384]{4,3,2,1,0:T(8,128)(2,1)S(1)} collective-permute-done((bf16[2,4,16,8,384]{4,3,2,1,0:T(8,128)(2,1)S(1)}, bf16[2,4,16,8,384]{4,3,2,1,0:T(8,128)(2,1)S(1)}, u32[]{:S(2)}, u32[]{:S(2)}) %collective-permute-start.7) | collective-permute-done | bytes 786464 | tf_op jit(solution)/shard_map/ppermute | solution.py:294
  30.2 3.9 %final.1 = f32[16,8,256]{2,1,0:T(8,128)} custom-call(s32[16,128]{1,0:T(8,128)S(1)} %get-tuple-element.16.place_any, f32[8,128]{1,0:T(8,128)S(1)} %get-tuple-element.17.weight_any, bf16[2,4,16,8,384]{4,3,2,1,0:T(8,128)(2,1)S(1)} %pack.1.same_any, bf16[2,4,16,8,384]{4,3,2,1,0:T(8,128)(2,1)S(1)} %collective-permute-done.7.other_any, ...), custom_call_target="tpu_custom_call" | custom-call | tf_op jit(solution)/shard_map/final/pallas_call | solution.py:423
  (2 shorter events, 0.0 us)
Async XLA Ops:
  2.0 5.8 %collective-permute-start.2 = (bf16[16,8,384]{2,1,0:T(8,128)(2,1)S(1)}, bf16[16,8,384]{2,1,0:T(8,128)(2,1)S(1)}, u32[]{:S(2)}, u32[]{:S(2)}) collective-permute-start(bf16[16,8,384]{2,1,0:T(8,128)(2,1)S(1)} %get-tuple-element.18.after_any.own_ref), channel_id=1, source_target_pairs={{0,6},{1,7},{2,4},{3,5},{4,2},{5,3},{6,0},{7,1},{8,14},{9,15},{10,... | collective-permute-start | bytes 294920 | tf_op jit(solution)/shard_map/ppermute | solution.py:294
  4.5 5.0 %collective-permute-start.1 = (bf16[16,8,384]{2,1,0:T(8,128)(2,1)S(1)}, bf16[16,8,384]{2,1,0:T(8,128)(2,1)S(1)}, u32[]{:S(2)}, u32[]{:S(2)}) collective-permute-start(bf16[16,8,384]{2,1,0:T(8,128)(2,1)S(1)} %get-tuple-element.18.after_any.own_ref), channel_id=1, source_target_pairs={{0,4},{1,5},{2,6},{3,7},{4,0},{5,1},{6,2},{7,3},{8,12},{9,13},{10,... | collective-permute-start | bytes 294920 | tf_op jit(solution)/shard_map/ppermute | solution.py:294
  5.0 4.5 %collective-permute-start = (bf16[16,8,384]{2,1,0:T(8,128)(2,1)S(1)}, bf16[16,8,384]{2,1,0:T(8,128)(2,1)S(1)}, u32[]{:S(2)}, u32[]{:S(2)}) collective-permute-start(bf16[16,8,384]{2,1,0:T(8,128)(2,1)S(1)} %get-tuple-element.18.after_any.own_ref), channel_id=1, source_target_pairs={{0,2},{1,3},{2,0},{3,1},{4,6},{5,7},{6,4},{7,5},{8,10},{9,11},{10,... | collective-permute-start | bytes 294920 | tf_op jit(solution)/shard_map/ppermute | solution.py:294
  9.5 13.2 %collective-permute-start.3 = (bf16[4,16,8,384]{3,2,1,0:T(8,128)(2,1)S(1)}, bf16[4,16,8,384]{3,2,1,0:T(8,128)(2,1)S(1)}, u32[]{:S(2)}, u32[]{:S(2)}) collective-permute-start(bf16[4,16,8,384]{3,2,1,0:T(8,128)(2,1)S(1)} %get-tuple-element.21.line_ref), channel_id=1, source_target_pairs={{0,8},{1,9},{2,10},{3,11},{4,12},{5,13},{6,14},{7,15},{8,0},{9,1},... | collective-permute-start | bytes 1179656 | tf_op jit(solution)/shard_map/ppermute | solution.py:294
  11.3 13.1 %collective-permute-start.4 = (bf16[4,16,8,384]{3,2,1,0:T(8,128)(2,1)S(1)}, bf16[4,16,8,384]{3,2,1,0:T(8,128)(2,1)S(1)}, u32[]{:S(2)}, u32[]{:S(2)}) collective-permute-start(bf16[4,16,8,384]{3,2,1,0:T(8,128)(2,1)S(1)} %get-tuple-element.21.line_ref), channel_id=1, source_target_pairs={{8,16},{9,17},{10,18},{11,19},{12,20},{13,21},{14,22},{15,23},{16,... | collective-permute-start | bytes 1179656 | tf_op jit(solution)/shard_map/ppermute | solution.py:294
  18.0 4.8 %collective-permute-start.6 = (f32[8,128]{1,0:T(8,128)S(1)}, f32[8,128]{1,0:T(8,128)S(1)}, u32[]{:S(2)}, u32[]{:S(2)}) collective-permute-start(f32[8,128]{1,0:T(8,128)S(1)} %get-tuple-element.19.after_any), channel_id=1, source_target_pairs={{0,24},{1,25},{2,26},{3,27},{4,28},{5,29},{6,30},{7,31},{8,16},{9,... | collective-permute-start | bytes 12296 | tf_op jit(solution)/shard_map/ppermute | solution.py:294
  19.5 3.8 %collective-permute-start.5 = (f32[8,128]{1,0:T(8,128)S(1)}, f32[8,128]{1,0:T(8,128)S(1)}, u32[]{:S(2)}, u32[]{:S(2)}) collective-permute-start(f32[8,128]{1,0:T(8,128)S(1)} %get-tuple-element.19.after_any), channel_id=1, source_target_pairs={{0,16},{1,17},{2,18},{3,19},{4,20},{5,21},{6,22},{7,23},{8,24},{9,... | collective-permute-start | bytes 12296 | tf_op jit(solution)/shard_map/ppermute | solution.py:294
  24.4 5.7 %collective-permute-start.7 = (bf16[2,4,16,8,384]{4,3,2,1,0:T(8,128)(2,1)S(1)}, bf16[2,4,16,8,384]{4,3,2,1,0:T(8,128)(2,1)S(1)}, u32[]{:S(2)}, u32[]{:S(2)}) collective-permute-start(bf16[2,4,16,8,384]{4,3,2,1,0:T(8,128)(2,1)S(1)} %pack.1.same_any), channel_id=1, source_target_pairs={{0,1},{1,0},{2,3},{3,2},{4,5},{5,4},{6,7},{7,6},{8,9},{9,8},{10,11... | collective-permute-start | bytes 2359304 | tf_op jit(solution)/shard_map/ppermute | solution.py:294

commit v4 on v3

--- a/solution.py
+++ b/solution.py
@@ -15,7 +15,10 @@
 LINE = 8
 CHIPS = 4
 CORES = 2
-WIDE = LEAF + 2 * RANK
+PER_ROW = LEAF // RANK
+Q_ROW = BOXES
+LIFT_ROW = Q_ROW + BOXES // PER_ROW
+ROWS = LIFT_ROW + 2
 MIB = 1024 * 1024
 
 F32 = jnp.float32
@@ -80,25 +83,8 @@
         (scale_any, scale),
     )
     copies = [pltpu.make_async_copy(a, b, sems.at[i]) for i, (a, b) in enumerate(pairs)]
-    for copy in copies:
+    for copy in copies[4:] + copies[:4]:
         copy.start()
-    copies[0].wait()
-    copies[1].wait()
-    coefficients = [nt(vectors[b], basis[b]).astype(BF16) for b in range(BOXES)]
-    copies[2].wait()
-    total = jnp.zeros((RHS, RANK), F32)
-    for b in range(BOXES):
-        total = total + nn(coefficients[b], transfer[b])
-    total = total.astype(BF16)
-    copies[3].wait()
-    lifted = [nn(total, up[0, k].astype(BF16)) for k in range(UP)]
-    nothing = jnp.zeros((RHS, RANK), F32)
-    for b in range(BOXES):
-        block_ref[b, :, :LEAF] = vectors[b]
-        extra = lifted[b] if b < UP else nothing
-        block_ref[b, :, LEAF:] = jnp.concatenate(
-            [coefficients[b].astype(F32), extra], axis=1
-        ).astype(BF16)
     for copy in copies[4:]:
         copy.wait()
     me = me_ref[0]
@@ -113,17 +99,37 @@
         place_ref[first : first + box.shape[0], 0:BOXES] = place
     used = iota((NEAR, BOXES), 0) < jnp.broadcast_to(count[...].reshape(1, BOXES), (NEAR, BOXES))
     weight_ref[0:NEAR, 0:BOXES] = jnp.where(used, scale[...], 0.0)
-
-
-def join_kernel(near_any, own_ref, first_ref, second_ref, third_ref, line_ref, top_ref):
+    copies[0].wait()
+    copies[1].wait()
+    coefficients = [nt(vectors[b], basis[b]).astype(BF16) for b in range(BOXES)]
+    copies[2].wait()
+    total = jnp.zeros((RHS, RANK), F32)
+    for b in range(BOXES):
+        total = total + nn(coefficients[b], transfer[b])
+    total = total.astype(BF16)
+    copies[3].wait()
+    lifted = [nn(total, up[0, k].astype(BF16)) for k in range(UP)]
+    nothing = jnp.zeros((RHS, RANK), F32)
+    block_ref[:BOXES] = vectors[...]
+
+    def put(row, pieces):
+        block_ref[row] = jnp.concatenate(pieces, axis=1).astype(BF16)
+
+    for j in range(PER_ROW):
+        put(Q_ROW + j, [coefficients[PER_ROW * g + j].astype(F32) for g in range(PER_ROW)])
+    put(LIFT_ROW, lifted[:4])
+    put(LIFT_ROW + 1, [lifted[4], nothing, nothing, nothing])
+
+
+def join_kernel(ready_any, own_ref, first_ref, second_ref, third_ref, line_ref, top_ref):
     top = jnp.zeros((RHS, 128), F32)
     for k, ref in enumerate((own_ref, first_ref, second_ref, third_ref)):
         line_ref[k] = ref[...]
-        top = top + ref[UP - 1, :, LEAF:].astype(F32)
+        top = top + ref[LIFT_ROW + 1, :, :128].astype(F32)
     top_ref[...] = top
 
 
-def pack_kernel(me_ref, ready_any, line_ref, up_ref, down_ref, third, top_a, top_b, out_ref):
+def pack_kernel(me_ref, line_ref, up_ref, down_ref, third, top, out_ref):
     me = me_ref[0]
     home, core = me & 7, me & 1
     prev_is_up = ((me >> 3) & 1) == 1
@@ -141,9 +147,9 @@
             out_ref[1, k] = down_ref[k]
 
     low = iota((RHS, 128), 1) < RANK
-    for box, levels in ((3, third[...]), (4, top_a[...] + top_b[...])):
-        mixed = jnp.where(low, line_ref[0, box, :, LEAF:].astype(F32), levels)
-        out_ref[0, 0, box, :, LEAF:] = mixed.astype(BF16)
+    mixed = jnp.where(low, line_ref[0, LIFT_ROW, :, 128:].astype(F32), third[...])
+    out_ref[0, 0, LIFT_ROW, :, 128:] = mixed.astype(BF16)
+    out_ref[0, 0, LIFT_ROW + 1, :, :128] = top[...].astype(BF16)
 
 
 def own_kernel(weight_any, after_any, vectors_any, tiles_any, near_ref, weight, vectors, mine, sems):
@@ -232,7 +238,19 @@
         return at >> 7, (at >> 6) & 1, (at >> 4) & 3, at & 15
 
     def levels(half, k, level):
-        return window[half, 0, k, level, :, LEAF:].astype(F32)
+        row, lane = LIFT_ROW + level // PER_ROW, level % PER_ROW * RANK
+        return window[half, 0, k, row].astype(F32)[:, lane : lane + RANK]
+
+    for first in range(0, BOXES, 2):
+        parts = [
+            [nt(window[entry(s, b)], tiles[b, s - 1]) for s in range(1, NEAR)]
+            for b in range(first, first + 2)
+        ]
+        for b in range(first, first + 2):
+            total = near[b]
+            for s in range(1, NEAR):
+                total = total + weight[s, b] * parts[b - first][s - 1]
+            out[b] = total
 
     groups = [
         levels(1, 0, 0),
@@ -243,45 +261,32 @@
     ]
     far_field = jnp.zeros((RHS, RANK), F32)
     for k in range(UP):
-        far_field = far_field + nn(groups[k][:, RANK:].astype(BF16), level[0, k].astype(BF16))
+        far_field = far_field + nn(groups[k].astype(BF16), level[0, k].astype(BF16))
     far_field = far_field.astype(BF16)
 
     low = iota((RHS, 128), 1) < RANK
+
+    def coefficient(row, b, odd):
+        half, line, k, box = entry(row, b)
+        lanes = pl.ds(pl.multiple_of((box >> 3) * 128, 128), 128)
+        piece = window[half, line, k, Q_ROW + (box & 3), :, lanes].astype(F32)
+        return pltpu.roll(piece, (((box >> 2) & 1) ^ odd) * RANK, 1)
+
     leaves = []
     for b in range(BOXES):
-        halves = [
-            window[(*entry(8 + s, b), slice(None), slice(LEAF, WIDE))].astype(F32)
-            for s in range(FAR)
-        ]
+        halves = [coefficient(8 + s, b, s & 1) for s in range(FAR)]
         joined = jnp.concatenate(
-            [
-                jnp.where(low, halves[2 * i], pltpu.roll(halves[2 * i + 1], RANK, 1))
-                for i in range(FAR // 2)
-            ],
-            axis=1,
+            [jnp.where(low, halves[2 * i], halves[2 * i + 1]) for i in range(FAR // 2)], axis=1
         ).astype(BF16)
         leaves.append(nt(joined, coupling[b]))
     leaves = [(leaves[b] + nt(far_field, transfer[b])).astype(BF16) for b in range(BOXES)]
+    outs = []
     for b in range(BOXES):
-        out[b] = near[b] + nn(leaves[b], basis[b])
-    outs = []
-    for first in range(0, BOXES, 2):
-        parts = [
-            [
-                nt(window[(*entry(s, b), slice(None), slice(0, LEAF))], tiles[b, s - 1])
-                for s in range(1, NEAR)
-            ]
-            for b in range(first, first + 2)
-        ]
-        for b in range(first, first + 2):
-            total = out[b]
-            for s in range(1, NEAR):
-                total = total + weight[s, b] * parts[b - first][s - 1]
-            out[b] = total
-        if first % 8 == 6:
-            rows = pl.ds(first - 6, 8)
+        out[b] = out[b] + nn(leaves[b], basis[b])
+        if b % 8 == 7:
+            rows = pl.ds(b - 7, 8)
             outs.append(
-                pltpu.make_async_copy(out.at[rows], out_any.at[rows], out_sems.at[first // 8])
+                pltpu.make_async_copy(out.at[rows], out_any.at[rows], out_sems.at[b // 8])
             )
             outs[-1].start()
     for copy in outs:
@@ -319,7 +324,7 @@
     block, place, weight = pl.pallas_call(
         front_kernel,
         out_shape=(
-            shape_of((BOXES, RHS, WIDE), BF16),
+            shape_of((ROWS, RHS, LEAF), BF16),
             shape_of((BOXES, 128), I32),
             shape_of((8, 128), F32),
         ),
@@ -350,37 +355,6 @@
         off(level_up),
     )
 
-    near = pl.pallas_call(
-        own_kernel,
-        out_shape=shape_of((BOXES, RHS, LEAF), F32),
-        in_specs=[ANY] * 4,
-        out_specs=VMEM,
-        scratch_shapes=[
-            pltpu.SMEM((8, 128), F32),
-            pltpu.VMEM((BOXES, RHS, LEAF), BF16),
-            pltpu.VMEM((BOXES, LEAF, LEAF), BF16),
-            pltpu.SemaphoreType.DMA((6,)),
-        ],
-        compiler_params=pltpu.CompilerParams(vmem_limit_bytes=8 * MIB),
-        name="own",
-    )(weight, block, off(vectors), off(near_tiles))
-
-    line, tops = pl.pallas_call(
-        join_kernel,
-        out_shape=(
-            shape_of((CHIPS, BOXES, RHS, WIDE), BF16),
-            shape_of((RHS, 128), F32),
-        ),
-        in_specs=[ANY] + [VMEM] * CHIPS,
-        out_specs=(VMEM, VMEM),
-        compiler_params=pltpu.CompilerParams(vmem_limit_bytes=4 * MIB),
-        name="join",
-    )(
-        near,
-        block,
-        *[pairwise(block, lambda i, k=k: i ^ (CORES * k)) for k in range(1, CHIPS)],
-    )
-
     tiles, basis, transfer, coupling, level, ready = pl.pallas_call(
         stage_kernel,
         out_shape=(
@@ -397,7 +371,7 @@
         compiler_params=pltpu.CompilerParams(vmem_limit_bytes=4 * MIB),
         name="stage",
     )(
-        tops,
+        block,
         off(near_tiles),
         off(leaf_basis),
         off(leaf_transfer),
@@ -405,20 +379,51 @@
         off(level_coupling),
     )
 
+    line, tops = pl.pallas_call(
+        join_kernel,
+        out_shape=(
+            shape_of((CHIPS, ROWS, RHS, LEAF), BF16),
+            shape_of((RHS, 128), F32),
+        ),
+        in_specs=[ANY] + [VMEM] * CHIPS,
+        out_specs=(VMEM, VMEM),
+        compiler_params=pltpu.CompilerParams(vmem_limit_bytes=4 * MIB),
+        name="join",
+    )(
+        ready,
+        block,
+        *[pairwise(block, lambda i, k=k: i ^ (CORES * k)) for k in range(1, CHIPS)],
+    )
+
     up = pairwise(line, lambda i: LINE * partner_up(i // LINE) + i % LINE)
     down = pairwise(line, lambda i: LINE * partner_down(i // LINE) + i % LINE)
-    third = up[:, 3, :, LEAF:].astype(F32).sum(axis=0)
-    top_a = pairwise(tops, lambda i: i ^ (2 * LINE))
-    top_b = pairwise(tops, lambda i: i ^ (3 * LINE))
+    third = up[:, LIFT_ROW, :, 128:].astype(F32).sum(axis=0)
+    tops = tops + up[:, LIFT_ROW + 1, :, :128].astype(F32).sum(axis=0)
+    top = pairwise(tops, lambda i: i ^ (2 * LINE))
     same = pl.pallas_call(
         pack_kernel,
-        out_shape=shape_of((2, CHIPS, BOXES, RHS, WIDE), BF16),
-        in_specs=[SMEM, ANY] + [VMEM] * 6,
+        out_shape=shape_of((2, CHIPS, ROWS, RHS, LEAF), BF16),
+        in_specs=[SMEM] + [VMEM] * 5,
         out_specs=VMEM,
         compiler_params=pltpu.CompilerParams(vmem_limit_bytes=4 * MIB),
         name="pack",
-    )(me, ready, line, up, down, third, top_a, top_b)
+    )(me, line, up, down, third, top)
     other = pairwise(same, lambda i: i ^ 1)
+
+    near = pl.pallas_call(
+        own_kernel,
+        out_shape=shape_of((BOXES, RHS, LEAF), F32),
+        in_specs=[ANY] * 4,
+        out_specs=VMEM,
+        scratch_shapes=[
+            pltpu.SMEM((8, 128), F32),
+            pltpu.VMEM((BOXES, RHS, LEAF), BF16),
+            pltpu.VMEM((BOXES, LEAF, LEAF), BF16),
+            pltpu.SemaphoreType.DMA((6,)),
+        ],
+        compiler_params=pltpu.CompilerParams(vmem_limit_bytes=8 * MIB),
+        name="own",
+    )(weight, same, off(vectors), off(near_tiles))
 
     return pl.pallas_call(
         final_kernel,
@@ -426,7 +431,7 @@
         in_specs=[ANY] * 4 + [VMEM] * 6,
         out_specs=ANY,
         scratch_shapes=[
-            pltpu.VMEM((CORES, 2, CHIPS, BOXES, RHS, WIDE), BF16),
+            pltpu.VMEM((CORES, 2, CHIPS, ROWS, RHS, LEAF), BF16),
             pltpu.SMEM((BOXES, 128), I32),
             pltpu.SMEM((8, 128), F32),
             pltpu.VMEM((BOXES, RHS, LEAF), F32),

time: 34.6 us -> 33.8 us (0.977); the launches traced: 34.1 us -> 33.7 us
  waiting for transfers between devices: 5.5 us -> 4.35 us
  starting transfers between devices: 17.1 us -> 17.7 us
    ppermute x8 -> x7, waiting for transfers between devices: 5.5 us -> 4.35 us  [pairwise(): return lax.ppermute(block, 'pts', route)]
    ppermute x8 -> x7, starting transfers between devices: 17.1 us -> 17.7 us  [pairwise(): return lax.ppermute(block, 'pts', route)]
  transfers between devices with their start and end apart: 8 -> 7, of which waited for: 5 -> 2; matrix products, arithmetic and copies ran while one was open for 0% -> 0% of each run, Pallas kernels for 16% -> 16%
where the time goes in v4:
time: 33.8 us; the launch traced here: 33.7 us
  starting transfers between devices  17.7 us (52%)
  Pallas kernels  11.5 us (34%)
  waiting for transfers between devices  4.35 us (13%)
    ppermute x7, starting transfers between devices, pairwise(): return lax.ppermute(block, 'pts', route)  17.7 us
    ppermute x7, waiting for transfers between devices, pairwise(): return lax.ppermute(block, 'pts', route)  4.35 us
    pallas_call x1, Pallas kernels, per_device(): pl.pallas_call(final_kernel, out_shape=shape_of((BOXES, RHS, LEAF), F32),...  4.08 us
    pallas_call x1, Pallas kernels, per_device(): pl.pallas_call(stage_kernel, out_shape=(pltpu.VMEM((BOXES, NEAR - 1, LEAF...  3.22 us
    pallas_call x1, Pallas kernels, per_device(): pl.pallas_call(own_kernel, out_shape=shape_of((BOXES, RHS, LEAF), F32), i...  2.14 us
    pallas_call x1, Pallas kernels, per_device(): pl.pallas_call(front_kernel, out_shape=(shape_of((ROWS, RHS, LEAF), BF16)...  1.99 us
  transfers between devices with their start and end apart: 7, of which 2 were waited for; matrix products, arithmetic and copies ran while one was open for 0% of the time, Pallas kernels for 16%

profile of v4, /device:TPU:25, one launch (start us, length us, event | category | flops | bytes accessed | tf_op | source)
XLA Modules:
  0.0 33.7 jit_solution(8956519584657959530)
XLA Ops:
  0.0 2.0 %front.1 = (bf16[22,8,256]{2,1,0:T(8,128)(2,1)S(1)}, s32[16,128]{1,0:T(8,128)S(1)}, f32[8,128]{1,0:T(8,128)S(1)}) custom-call(s32[1]{0:T(128)} %bitcast.me_ref, s32[4,16]{1,0:T(4,128)} %bitcast.5, s32[6,16]{1,0:T(8,128)} %bitcast.4, s32[16]{0:T(128)} %count_any.1, f32[4,16]{1,0:T(4,128)} %bitcast.6, bf16[16,8,256]{2,1,0:T(8,128)(2,1)} %vectors_any.3, ...), custom_call_target="tpu_custom_call" | custom-call | tf_op jit(solution)/shard_map/front/pallas_call | solution.py:324
  2.0 2.6 %collective-permute-start.2 = (bf16[22,8,256]{2,1,0:T(8,128)(2,1)S(1)}, bf16[22,8,256]{2,1,0:T(8,128)(2,1)S(1)}, u32[]{:S(2)}, u32[]{:S(2)}) collective-permute-start(bf16[22,8,256]{2,1,0:T(8,128)(2,1)S(1)} %get-tuple-element.18.after_any.own_ref), channel_id=1, source_target_pairs={{0,6},{1,7},{2,4},{3,5},{4,2},{5,3},{6,0},{7,1},{8,14},{9,15},{10,... | collective-permute-start | bytes 270344 | tf_op jit(solution)/shard_map/ppermute | solution.py:299
  4.6 0.5 %collective-permute-start.1 = (bf16[22,8,256]{2,1,0:T(8,128)(2,1)S(1)}, bf16[22,8,256]{2,1,0:T(8,128)(2,1)S(1)}, u32[]{:S(2)}, u32[]{:S(2)}) collective-permute-start(bf16[22,8,256]{2,1,0:T(8,128)(2,1)S(1)} %get-tuple-element.18.after_any.own_ref), channel_id=1, source_target_pairs={{0,4},{1,5},{2,6},{3,7},{4,0},{5,1},{6,2},{7,3},{8,12},{9,13},{10,... | collective-permute-start | bytes 270344 | tf_op jit(solution)/shard_map/ppermute | solution.py:299
  5.1 0.3 collective-permute-start
  5.3 3.2 %stage.1 = (bf16[16,3,256,256]{3,2,1,0:T(8,128)(2,1)S(1)}, bf16[16,64,256]{2,1,0:T(8,128)(2,1)S(1)}, bf16[16,64,64]{2,1,0:T(8,128)(2,1)S(1)}, bf16[16,64,384]{2,...) custom-call(bf16[22,8,256]{2,1,0:T(8,128)(2,1)S(1)} %get-tuple-element.18.after_any.own_ref, ...), custom_call_target="tpu_custom_call" | custom-call | tf_op jit(solution)/shard_map/stage/pallas_call | solution.py:358
  8.6 0.0 collective-permute-done.2.third_ref
  8.6 0.9 %collective-permute-done.1.second_ref = bf16[22,8,256]{2,1,0:T(8,128)(2,1)S(1)} collective-permute-done((bf16[22,8,256]{2,1,0:T(8,128)(2,1)S(1)}, bf16[22,8,256]{2,1,0:T(8,128)(2,1)S(1)}, u32[]{:S(2)}, u32[]{:S(2)}) %collective-permute-start.1) | collective-permute-done | bytes 90144 | tf_op jit(solution)/shard_map/ppermute | solution.py:299
  9.4 0.0 collective-permute-done.first_ref
  9.5 1.7 %collective-permute-start.3 = (bf16[4,22,8,256]{3,2,1,0:T(8,128)(2,1)S(1)}, bf16[4,22,8,256]{3,2,1,0:T(8,128)(2,1)S(1)}, u32[]{:S(2)}, u32[]{:S(2)}) collective-permute-start(bf16[4,22,8,256]{3,2,1,0:T(8,128)(2,1)S(1)} %get-tuple-element.20.line_ref), channel_id=1, source_target_pairs={{0,8},{1,9},{2,10},{3,11},{4,12},{5,13},{6,14},{7,15},{8,0},{9,1},... | collective-permute-start | bytes 1081352 | tf_op jit(solution)/shard_map/ppermute | solution.py:299
  11.2 6.7 %collective-permute-start.4 = (bf16[4,22,8,256]{3,2,1,0:T(8,128)(2,1)S(1)}, bf16[4,22,8,256]{3,2,1,0:T(8,128)(2,1)S(1)}, u32[]{:S(2)}, u32[]{:S(2)}) collective-permute-start(bf16[4,22,8,256]{3,2,1,0:T(8,128)(2,1)S(1)} %get-tuple-element.20.line_ref), channel_id=1, source_target_pairs={{8,16},{9,17},{10,18},{11,19},{12,20},{13,21},{14,22},{15,23},{16,... | collective-permute-start | bytes 1081352 | tf_op jit(solution)/shard_map/ppermute | solution.py:299
  18.0 0.0 collective-permute-done.3.up_ref
  18.0 2.3 %collective-permute-start.5 = (f32[8,128]{1,0:T(8,128)S(1)}, f32[8,128]{1,0:T(8,128)S(1)}, u32[]{:S(2)}, u32[]{:S(2)}) collective-permute-start(f32[8,128]{1,0:T(8,128)S(1)} %add.3), channel_id=1, source_target_pairs={{0,16},{1,17},{2,18},{3,19},{4,20},{5,21},{6,22},{7,23},{8,24},{9,... | collective-permute-start | bytes 12296 | tf_op jit(solution)/shard_map/ppermute | solution.py:299
  20.3 3.5 %collective-permute-done.4.down_ref = bf16[4,22,8,256]{3,2,1,0:T(8,128)(2,1)S(1)} collective-permute-done((bf16[4,22,8,256]{3,2,1,0:T(8,128)(2,1)S(1)}, bf16[4,22,8,256]{3,2,1,0:T(8,128)(2,1)S(1)}, u32[]{:S(2)}, u32[]{:S(2)}) %collective-permute-start.4) | collective-permute-done | bytes 360480 | tf_op jit(solution)/shard_map/ppermute | solution.py:299
  23.8 0.0 collective-permute-done.5.top
  23.8 0.1 pack.1.after_any.same_any
  23.8 3.6 %collective-permute-start.6 = (bf16[2,4,22,8,256]{4,3,2,1,0:T(8,128)(2,1)S(1)}, bf16[2,4,22,8,256]{4,3,2,1,0:T(8,128)(2,1)S(1)}, u32[]{:S(2)}, u32[]{:S(2)}) collective-permute-start(bf16[2,4,22,8,256]{4,3,2,1,0:T(8,128)(2,1)S(1)} %pack.1.after_any.same_any), channel_id=1, source_target_pairs={{0,1},{1,0},{2,3},{3,2},{4,5},{5,4},{6,7},{7,6},{8,9},{9,8},{10,11... | collective-permute-start | bytes 2162696 | tf_op jit(solution)/shard_map/ppermute | solution.py:299
  27.5 2.1 %own.1.near = f32[16,8,256]{2,1,0:T(8,128)S(1)} custom-call(f32[8,128]{1,0:T(8,128)S(1)} %get-tuple-element.17.weight_any, bf16[2,4,22,8,256]{4,3,2,1,0:T(8,128)(2,1)S(1)} %pack.1.after_any.same_any, bf16[16,8,256]{2,1,0:T(8,128)(2,1)} %vectors_any.3, bf16[16,4,256,256]{3,2,1,0:T(8,128)(2,1)} %tiles_any.3), custom_call_target="tpu_custom_call" | custom-call | tf_op jit(solution)/shard_map/own/pallas_call | solution.py:413
  29.6 0.0 collective-permute-done.6.other_any
  29.6 4.1 %final.1 = f32[16,8,256]{2,1,0:T(8,128)} custom-call(s32[16,128]{1,0:T(8,128)S(1)} %get-tuple-element.16.place_any, f32[8,128]{1,0:T(8,128)S(1)} %get-tuple-element.17.weight_any, bf16[2,4,22,8,256]{4,3,2,1,0:T(8,128)(2,1)S(1)} %pack.1.after_any.same_any, bf16[2,4,22,8,256]{4,3,2,1,0:T(8,128)(2,1)S(1)} %collective-permute-done.6.other_any, ...), custom_call_target="tpu_custom_call" | custom-call | tf_op jit(solution)/shard_map/final/pallas_call | solution.py:428
  (3 shorter events, 0.0 us)
Async XLA Ops:
  2.0 6.6 %collective-permute-start.2 = (bf16[22,8,256]{2,1,0:T(8,128)(2,1)S(1)}, bf16[22,8,256]{2,1,0:T(8,128)(2,1)S(1)}, u32[]{:S(2)}, u32[]{:S(2)}) collective-permute-start(bf16[22,8,256]{2,1,0:T(8,128)(2,1)S(1)} %get-tuple-element.18.after_any.own_ref), channel_id=1, source_target_pairs={{0,6},{1,7},{2,4},{3,5},{4,2},{5,3},{6,0},{7,1},{8,14},{9,15},{10,... | collective-permute-start | bytes 270344 | tf_op jit(solution)/shard_map/ppermute | solution.py:299
  4.6 4.9 %collective-permute-start.1 = (bf16[22,8,256]{2,1,0:T(8,128)(2,1)S(1)}, bf16[22,8,256]{2,1,0:T(8,128)(2,1)S(1)}, u32[]{:S(2)}, u32[]{:S(2)}) collective-permute-start(bf16[22,8,256]{2,1,0:T(8,128)(2,1)S(1)} %get-tuple-element.18.after_any.own_ref), channel_id=1, source_target_pairs={{0,4},{1,5},{2,6},{3,7},{4,0},{5,1},{6,2},{7,3},{8,12},{9,13},{10,... | collective-permute-start | bytes 270344 | tf_op jit(solution)/shard_map/ppermute | solution.py:299
  5.1 4.4 %collective-permute-start = (bf16[22,8,256]{2,1,0:T(8,128)(2,1)S(1)}, bf16[22,8,256]{2,1,0:T(8,128)(2,1)S(1)}, u32[]{:S(2)}, u32[]{:S(2)}) collective-permute-start(bf16[22,8,256]{2,1,0:T(8,128)(2,1)S(1)} %get-tuple-element.18.after_any.own_ref), channel_id=1, source_target_pairs={{0,2},{1,3},{2,0},{3,1},{4,6},{5,7},{6,4},{7,5},{8,10},{9,11},{10,... | collective-permute-start | bytes 270344 | tf_op jit(solution)/shard_map/ppermute | solution.py:299
  9.5 8.5 %collective-permute-start.3 = (bf16[4,22,8,256]{3,2,1,0:T(8,128)(2,1)S(1)}, bf16[4,22,8,256]{3,2,1,0:T(8,128)(2,1)S(1)}, u32[]{:S(2)}, u32[]{:S(2)}) collective-permute-start(bf16[4,22,8,256]{3,2,1,0:T(8,128)(2,1)S(1)} %get-tuple-element.20.line_ref), channel_id=1, source_target_pairs={{0,8},{1,9},{2,10},{3,11},{4,12},{5,13},{6,14},{7,15},{8,0},{9,1},... | collective-permute-start | bytes 1081352 | tf_op jit(solution)/shard_map/ppermute | solution.py:299
  11.2 12.6 %collective-permute-start.4 = (bf16[4,22,8,256]{3,2,1,0:T(8,128)(2,1)S(1)}, bf16[4,22,8,256]{3,2,1,0:T(8,128)(2,1)S(1)}, u32[]{:S(2)}, u32[]{:S(2)}) collective-permute-start(bf16[4,22,8,256]{3,2,1,0:T(8,128)(2,1)S(1)} %get-tuple-element.20.line_ref), channel_id=1, source_target_pairs={{8,16},{9,17},{10,18},{11,19},{12,20},{13,21},{14,22},{15,23},{16,... | collective-permute-start | bytes 1081352 | tf_op jit(solution)/shard_map/ppermute | solution.py:299
  18.0 5.8 %collective-permute-start.5 = (f32[8,128]{1,0:T(8,128)S(1)}, f32[8,128]{1,0:T(8,128)S(1)}, u32[]{:S(2)}, u32[]{:S(2)}) collective-permute-start(f32[8,128]{1,0:T(8,128)S(1)} %add.3), channel_id=1, source_target_pairs={{0,16},{1,17},{2,18},{3,19},{4,20},{5,21},{6,22},{7,23},{8,24},{9,... | collective-permute-start | bytes 12296 | tf_op jit(solution)/shard_map/ppermute | solution.py:299
  23.8 5.8 %collective-permute-start.6 = (bf16[2,4,22,8,256]{4,3,2,1,0:T(8,128)(2,1)S(1)}, bf16[2,4,22,8,256]{4,3,2,1,0:T(8,128)(2,1)S(1)}, u32[]{:S(2)}, u32[]{:S(2)}) collective-permute-start(bf16[2,4,22,8,256]{4,3,2,1,0:T(8,128)(2,1)S(1)} %pack.1.after_any.same_any), channel_id=1, source_target_pairs={{0,1},{1,0},{2,3},{3,2},{4,5},{5,4},{6,7},{7,6},{8,9},{9,8},{10,11... | collective-permute-start | bytes 2162696 | tf_op jit(solution)/shard_map/ppermute | solution.py:299

commit v5 on v4

--- a/solution.py
+++ b/solution.py
@@ -19,6 +19,8 @@
 Q_ROW = BOXES
 LIFT_ROW = Q_ROW + BOXES // PER_ROW
 ROWS = LIFT_ROW + 2
+Z_ROWS = CHIPS * LIFT_ROW + 1
+ALL_ROWS = CHIPS * (ROWS + LIFT_ROW)
 MIB = 1024 * 1024
 
 F32 = jnp.float32
@@ -95,7 +97,8 @@
         apart = ((box >> 4) & 1) ^ core
         beside = ((box >> 7) != line).astype(I32)
         chip = ((box >> 5) & 3) ^ home
-        place = (apart << 7) | (beside << 6) | (chip << 4) | (box & 15)
+        start = jnp.where(beside == 1, CHIPS * ROWS + LIFT_ROW * chip, ROWS * chip)
+        place = (apart << 12) | (start << 4) | (box & 15)
         place_ref[first : first + box.shape[0], 0:BOXES] = place
     used = iota((NEAR, BOXES), 0) < jnp.broadcast_to(count[...].reshape(1, BOXES), (NEAR, BOXES))
     weight_ref[0:NEAR, 0:BOXES] = jnp.where(used, scale[...], 0.0)
@@ -103,10 +106,8 @@
     copies[1].wait()
     coefficients = [nt(vectors[b], basis[b]).astype(BF16) for b in range(BOXES)]
     copies[2].wait()
-    total = jnp.zeros((RHS, RANK), F32)
-    for b in range(BOXES):
-        total = total + nn(coefficients[b], transfer[b])
-    total = total.astype(BF16)
+    joined = jnp.concatenate([q.astype(F32) for q in coefficients], axis=1).astype(BF16)
+    total = nn(joined, transfer[...].reshape(BOXES * RANK, RANK)).astype(BF16)
     copies[3].wait()
     lifted = [nn(total, up[0, k].astype(BF16)) for k in range(UP)]
     nothing = jnp.zeros((RHS, RANK), F32)
@@ -121,35 +122,42 @@
     put(LIFT_ROW + 1, [lifted[4], nothing, nothing, nothing])
 
 
-def join_kernel(ready_any, own_ref, first_ref, second_ref, third_ref, line_ref, top_ref):
-    top = jnp.zeros((RHS, 128), F32)
-    for k, ref in enumerate((own_ref, first_ref, second_ref, third_ref)):
-        line_ref[k] = ref[...]
-        top = top + ref[LIFT_ROW + 1, :, :128].astype(F32)
-    top_ref[...] = top
-
-
-def pack_kernel(me_ref, line_ref, up_ref, down_ref, third, top, out_ref):
+def join_kernel(ready_any, own_ref, first_ref, second_ref, third_ref, line_ref, z_ref):
+    refs = (own_ref, first_ref, second_ref, third_ref)
+    for k, ref in enumerate(refs):
+        line_ref[k * ROWS : (k + 1) * ROWS] = ref[...]
+        z_ref[k * LIFT_ROW : (k + 1) * LIFT_ROW] = ref[:LIFT_ROW]
+    sums = [
+        sum(ref[row, :, lanes].astype(F32) for ref in refs)
+        for row, lanes in ((LIFT_ROW, slice(128, LEAF)), (LIFT_ROW + 1, slice(0, 128)))
+    ]
+    z_ref[CHIPS * LIFT_ROW] = jnp.concatenate(sums, axis=1).astype(BF16)
+
+
+def pack_kernel(me_ref, line_ref, up_ref, down_ref, top, out_ref):
     me = me_ref[0]
     home, core = me & 7, me & 1
     prev_is_up = ((me >> 3) & 1) == 1
-    out_ref[0] = line_ref[...]
+    out_ref[: CHIPS * ROWS] = line_ref[...]
     for k in range(CHIPS):
         use_prev = (home ^ (2 * k)) > home if k else core == 1
         use_up = use_prev == prev_is_up
+        rows = slice(k * LIFT_ROW, (k + 1) * LIFT_ROW)
+        first = CHIPS * ROWS + k * LIFT_ROW
 
         @pl.when(use_up)
         def _():
-            out_ref[1, k] = up_ref[k]
+            out_ref[first : first + LIFT_ROW] = up_ref[rows]
 
         @pl.when(jnp.logical_not(use_up))
         def _():
-            out_ref[1, k] = down_ref[k]
+            out_ref[first : first + LIFT_ROW] = down_ref[rows]
 
     low = iota((RHS, 128), 1) < RANK
-    mixed = jnp.where(low, line_ref[0, LIFT_ROW, :, 128:].astype(F32), third[...])
-    out_ref[0, 0, LIFT_ROW, :, 128:] = mixed.astype(BF16)
-    out_ref[0, 0, LIFT_ROW + 1, :, :128] = top[...].astype(BF16)
+    third = up_ref[CHIPS * LIFT_ROW, :, :128].astype(F32)
+    mixed = jnp.where(low, line_ref[LIFT_ROW, :, 128:].astype(F32), third)
+    out_ref[LIFT_ROW, :, 128:] = mixed.astype(BF16)
+    out_ref[LIFT_ROW + 1, :, :128] = top[...].astype(BF16)
 
 
 def own_kernel(weight_any, after_any, vectors_any, tiles_any, near_ref, weight, vectors, mine, sems):
@@ -235,15 +243,19 @@
 
     def entry(row, b):
         at = place[row, b]
-        return at >> 7, (at >> 6) & 1, (at >> 4) & 3, at & 15
+        return at >> 12, (at >> 4) & 255, at & 15
+
+    def vectors(row, b):
+        half, start, box = entry(row, b)
+        return window[half, start + box]
 
     def levels(half, k, level):
         row, lane = LIFT_ROW + level // PER_ROW, level % PER_ROW * RANK
-        return window[half, 0, k, row].astype(F32)[:, lane : lane + RANK]
+        return window[half, k * ROWS + row].astype(F32)[:, lane : lane + RANK]
 
     for first in range(0, BOXES, 2):
         parts = [
-            [nt(window[entry(s, b)], tiles[b, s - 1]) for s in range(1, NEAR)]
+            [nt(vectors(s, b), tiles[b, s - 1]) for s in range(1, NEAR)]
             for b in range(first, first + 2)
         ]
         for b in range(first, first + 2):
@@ -267,9 +279,9 @@
     low = iota((RHS, 128), 1) < RANK
 
     def coefficient(row, b, odd):
-        half, line, k, box = entry(row, b)
+        half, start, box = entry(row, b)
         lanes = pl.ds(pl.multiple_of((box >> 3) * 128, 128), 128)
-        piece = window[half, line, k, Q_ROW + (box & 3), :, lanes].astype(F32)
+        piece = window[half, start + Q_ROW + (box & 3), :, lanes].astype(F32)
         return pltpu.roll(piece, (((box >> 2) & 1) ^ odd) * RANK, 1)
 
     leaves = []
@@ -379,11 +391,14 @@
         off(level_coupling),
     )
 
-    line, tops = pl.pallas_call(
+    first, third, second = [
+        pairwise(block, lambda i, k=k: i ^ (CORES * k)) for k in (1, 3, 2)
+    ]
+    line, z_line = pl.pallas_call(
         join_kernel,
         out_shape=(
-            shape_of((CHIPS, ROWS, RHS, LEAF), BF16),
-            shape_of((RHS, 128), F32),
+            shape_of((CHIPS * ROWS, RHS, LEAF), BF16),
+            shape_of((Z_ROWS, RHS, LEAF), BF16),
         ),
         in_specs=[ANY] + [VMEM] * CHIPS,
         out_specs=(VMEM, VMEM),
@@ -392,22 +407,23 @@
     )(
         ready,
         block,
-        *[pairwise(block, lambda i, k=k: i ^ (CORES * k)) for k in range(1, CHIPS)],
-    )
-
-    up = pairwise(line, lambda i: LINE * partner_up(i // LINE) + i % LINE)
-    down = pairwise(line, lambda i: LINE * partner_down(i // LINE) + i % LINE)
-    third = up[:, LIFT_ROW, :, 128:].astype(F32).sum(axis=0)
-    tops = tops + up[:, LIFT_ROW + 1, :, :128].astype(F32).sum(axis=0)
+        first,
+        second,
+        third,
+    )
+
+    up = pairwise(z_line, lambda i: LINE * partner_up(i // LINE) + i % LINE)
+    down = pairwise(z_line, lambda i: LINE * partner_down(i // LINE) + i % LINE)
+    tops = z_line[-1, :, 128:].astype(F32) + up[-1, :, 128:].astype(F32)
     top = pairwise(tops, lambda i: i ^ (2 * LINE))
     same = pl.pallas_call(
         pack_kernel,
-        out_shape=shape_of((2, CHIPS, ROWS, RHS, LEAF), BF16),
-        in_specs=[SMEM] + [VMEM] * 5,
+        out_shape=shape_of((ALL_ROWS, RHS, LEAF), BF16),
+        in_specs=[SMEM] + [VMEM] * 4,
         out_specs=VMEM,
         compiler_params=pltpu.CompilerParams(vmem_limit_bytes=4 * MIB),
         name="pack",
-    )(me, line, up, down, third, top)
+    )(me, line, up, down, top)
     other = pairwise(same, lambda i: i ^ 1)
 
     near = pl.pallas_call(
@@ -431,7 +447,7 @@
         in_specs=[ANY] * 4 + [VMEM] * 6,
         out_specs=ANY,
         scratch_shapes=[
-            pltpu.VMEM((CORES, 2, CHIPS, ROWS, RHS, LEAF), BF16),
+            pltpu.VMEM((CORES, ALL_ROWS, RHS, LEAF), BF16),
             pltpu.SMEM((BOXES, 128), I32),
             pltpu.SMEM((8, 128), F32),
             pltpu.VMEM((BOXES, RHS, LEAF), F32),

time: 33.8 us -> 32.9 us (0.973)
  starting transfers between devices: 17.7 us -> 17 us
    ppermute x7, starting transfers between devices: 17.7 us -> 17 us  [pairwise(): return lax.ppermute(block, 'pts', route)]
where the time goes in v5:
time: 32.9 us; the launch traced here: 32.8 us
  starting transfers between devices  17 us (52%)
  Pallas kernels  11.2 us (34%)
  waiting for transfers between devices  4.44 us (13%)
    ppermute x7, starting transfers between devices, pairwise(): return lax.ppermute(block, 'pts', route)  17 us
    ppermute x7, waiting for transfers between devices, pairwise(): return lax.ppermute(block, 'pts', route)  4.44 us
    pallas_call x1, Pallas kernels, per_device(): pl.pallas_call(final_kernel, out_shape=shape_of((BOXES, RHS, LEAF), F32),...  3.86 us
    pallas_call x1, Pallas kernels, per_device(): pl.pallas_call(stage_kernel, out_shape=(pltpu.VMEM((BOXES, NEAR - 1, LEAF...  3.22 us
    pallas_call x1, Pallas kernels, per_device(): pl.pallas_call(own_kernel, out_shape=shape_of((BOXES, RHS, LEAF), F32), i...  2.14 us
    pallas_call x1, Pallas kernels, per_device(): pl.pallas_call(front_kernel, out_shape=(shape_of((ROWS, RHS, LEAF), BF16)...  1.88 us
  transfers between devices with their start and end apart: 7, of which 2 were waited for; matrix products, arithmetic and copies ran while one was open for 0% of the time, Pallas kernels for 16%

profile of v5, /device:TPU:25, one launch (start us, length us, event | category | flops | bytes accessed | tf_op | source)
XLA Modules:
  0.0 32.8 jit_solution(6249671807321628604)
XLA Ops:
  0.0 1.9 %front.1 = (bf16[22,8,256]{2,1,0:T(8,128)(2,1)S(1)}, s32[16,128]{1,0:T(8,128)S(1)}, f32[8,128]{1,0:T(8,128)S(1)}) custom-call(s32[1]{0:T(128)} %bitcast.me_ref, s32[4,16]{1,0:T(4,128)} %bitcast.7, s32[6,16]{1,0:T(8,128)} %bitcast.6, s32[16]{0:T(128)} %count_any.1, f32[4,16]{1,0:T(4,128)} %bitcast.8, bf16[16,8,256]{2,1,0:T(8,128)(2,1)} %vectors_any.3, ...), custom_call_target="tpu_custom_call" | custom-call | tf_op jit(solution)/shard_map/front/pallas_call | solution.py:336
  1.9 2.6 %collective-permute-start.2 = (bf16[22,8,256]{2,1,0:T(8,128)(2,1)S(1)}, bf16[22,8,256]{2,1,0:T(8,128)(2,1)S(1)}, u32[]{:S(2)}, u32[]{:S(2)}) collective-permute-start(bf16[22,8,256]{2,1,0:T(8,128)(2,1)S(1)} %get-tuple-element.18.after_any.own_ref), channel_id=1, source_target_pairs={{0,6},{1,7},{2,4},{3,5},{4,2},{5,3},{6,0},{7,1},{8,14},{9,15},{10,... | collective-permute-start | bytes 270344 | tf_op jit(solution)/shard_map/ppermute | solution.py:311
  4.5 0.5 %collective-permute-start.1 = (bf16[22,8,256]{2,1,0:T(8,128)(2,1)S(1)}, bf16[22,8,256]{2,1,0:T(8,128)(2,1)S(1)}, u32[]{:S(2)}, u32[]{:S(2)}) collective-permute-start(bf16[22,8,256]{2,1,0:T(8,128)(2,1)S(1)} %get-tuple-element.18.after_any.own_ref), channel_id=1, source_target_pairs={{0,4},{1,5},{2,6},{3,7},{4,0},{5,1},{6,2},{7,3},{8,12},{9,13},{10,... | collective-permute-start | bytes 270344 | tf_op jit(solution)/shard_map/ppermute | solution.py:311
  5.0 0.3 collective-permute-start
  5.2 3.2 %stage.1 = (bf16[16,3,256,256]{3,2,1,0:T(8,128)(2,1)S(1)}, bf16[16,64,256]{2,1,0:T(8,128)(2,1)S(1)}, bf16[16,64,64]{2,1,0:T(8,128)(2,1)S(1)}, bf16[16,64,384]{2,...) custom-call(bf16[22,8,256]{2,1,0:T(8,128)(2,1)S(1)} %get-tuple-element.18.after_any.own_ref, ...), custom_call_target="tpu_custom_call" | custom-call | tf_op jit(solution)/shard_map/stage/pallas_call | solution.py:370
  8.5 0.0 collective-permute-done.2.third_ref
  8.5 0.9 %collective-permute-done.1.second_ref = bf16[22,8,256]{2,1,0:T(8,128)(2,1)S(1)} collective-permute-done((bf16[22,8,256]{2,1,0:T(8,128)(2,1)S(1)}, bf16[22,8,256]{2,1,0:T(8,128)(2,1)S(1)}, u32[]{:S(2)}, u32[]{:S(2)}) %collective-permute-start.1) | collective-permute-done | bytes 90144 | tf_op jit(solution)/shard_map/ppermute | solution.py:311
  9.3 0.0 collective-permute-done.first_ref
  9.4 1.7 %collective-permute-start.3 = (bf16[81,8,256]{2,1,0:T(8,128)(2,1)S(1)}, bf16[81,8,256]{2,1,0:T(8,128)(2,1)S(1)}, u32[]{:S(2)}, u32[]{:S(2)}) collective-permute-start(bf16[81,8,256]{2,1,0:T(8,128)(2,1)S(1)} %get-tuple-element.21), channel_id=1, source_target_pairs={{0,8},{1,9},{2,10},{3,11},{4,12},{5,13},{6,14},{7,15},{8,0},{9,1},... | collective-permute-start | bytes 995336 | tf_op jit(solution)/shard_map/ppermute | solution.py:311
  11.1 6.7 %collective-permute-start.4 = (bf16[81,8,256]{2,1,0:T(8,128)(2,1)S(1)}, bf16[81,8,256]{2,1,0:T(8,128)(2,1)S(1)}, u32[]{:S(2)}, u32[]{:S(2)}) collective-permute-start(bf16[81,8,256]{2,1,0:T(8,128)(2,1)S(1)} %get-tuple-element.21), channel_id=1, source_target_pairs={{8,16},{9,17},{10,18},{11,19},{12,20},{13,21},{14,22},{15,23},{16,... | collective-permute-start | bytes 995336 | tf_op jit(solution)/shard_map/ppermute | solution.py:311
  17.9 0.0 collective-permute-done.3.up_ref
  17.9 1.6 %collective-permute-start.5 = (f32[8,128]{1,0:T(8,128)S(1)}, f32[8,128]{1,0:T(8,128)S(1)}, u32[]{:S(2)}, u32[]{:S(2)}) collective-permute-start(f32[8,128]{1,0:T(8,128)S(1)} %add_bitcast_fusion), channel_id=1, source_target_pairs={{0,16},{1,17},{2,18},{3,19},{4,20},{5,21},{6,22},{7,23},{8,24},{9,... | collective-permute-start | bytes 12296 | tf_op jit(solution)/shard_map/ppermute | solution.py:311
  19.5 3.6 %collective-permute-done.4.down_ref = bf16[81,8,256]{2,1,0:T(8,128)(2,1)S(1)} collective-permute-done((bf16[81,8,256]{2,1,0:T(8,128)(2,1)S(1)}, bf16[81,8,256]{2,1,0:T(8,128)(2,1)S(1)}, u32[]{:S(2)}, u32[]{:S(2)}) %collective-permute-start.4) | collective-permute-done | bytes 331808 | tf_op jit(solution)/shard_map/ppermute | solution.py:311
  23.1 0.0 collective-permute-done.5.top
  23.1 0.1 pack.1.after_any.same_any
  23.1 3.6 %collective-permute-start.6 = (bf16[168,8,256]{2,1,0:T(8,128)(2,1)S(1)}, bf16[168,8,256]{2,1,0:T(8,128)(2,1)S(1)}, u32[]{:S(2)}, u32[]{:S(2)}) collective-permute-start(bf16[168,8,256]{2,1,0:T(8,128)(2,1)S(1)} %pack.1.after_any.same_any), channel_id=1, source_target_pairs={{0,1},{1,0},{2,3},{3,2},{4,5},{5,4},{6,7},{7,6},{8,9},{9,8},{10,11... | collective-permute-start | bytes 2064392 | tf_op jit(solution)/shard_map/ppermute | solution.py:311
  26.8 2.1 %own.1.near = f32[16,8,256]{2,1,0:T(8,128)S(1)} custom-call(f32[8,128]{1,0:T(8,128)S(1)} %get-tuple-element.17.weight_any, bf16[168,8,256]{2,1,0:T(8,128)(2,1)S(1)} %pack.1.after_any.same_any, bf16[16,8,256]{2,1,0:T(8,128)(2,1)} %vectors_any.3, bf16[16,4,256,256]{3,2,1,0:T(8,128)(2,1)} %tiles_any.3), custom_call_target="tpu_custom_call" | custom-call | tf_op jit(solution)/shard_map/own/pallas_call | solution.py:429
  28.9 0.0 collective-permute-done.6.other_any
  28.9 3.9 %final.1 = f32[16,8,256]{2,1,0:T(8,128)} custom-call(s32[16,128]{1,0:T(8,128)S(1)} %get-tuple-element.16.place_any, f32[8,128]{1,0:T(8,128)S(1)} %get-tuple-element.17.weight_any, bf16[168,8,256]{2,1,0:T(8,128)(2,1)S(1)} %pack.1.after_any.same_any, bf16[168,8,256]{2,1,0:T(8,128)(2,1)S(1)} %collective-permute-done.6.other_any, f32[16,8,256]{2,1,0:T(8,128)S(1)} %own.1.near, ...), custom_call_target="tpu_custom_call" | custom-call | tf_op jit(solution)/shard_map/final/pallas_call | solution.py:444
  (2 shorter events, 0.1 us)
Async XLA Ops:
  1.9 6.6 %collective-permute-start.2 = (bf16[22,8,256]{2,1,0:T(8,128)(2,1)S(1)}, bf16[22,8,256]{2,1,0:T(8,128)(2,1)S(1)}, u32[]{:S(2)}, u32[]{:S(2)}) collective-permute-start(bf16[22,8,256]{2,1,0:T(8,128)(2,1)S(1)} %get-tuple-element.18.after_any.own_ref), channel_id=1, source_target_pairs={{0,6},{1,7},{2,4},{3,5},{4,2},{5,3},{6,0},{7,1},{8,14},{9,15},{10,... | collective-permute-start | bytes 270344 | tf_op jit(solution)/shard_map/ppermute | solution.py:311
  4.5 4.9 %collective-permute-start.1 = (bf16[22,8,256]{2,1,0:T(8,128)(2,1)S(1)}, bf16[22,8,256]{2,1,0:T(8,128)(2,1)S(1)}, u32[]{:S(2)}, u32[]{:S(2)}) collective-permute-start(bf16[22,8,256]{2,1,0:T(8,128)(2,1)S(1)} %get-tuple-element.18.after_any.own_ref), channel_id=1, source_target_pairs={{0,4},{1,5},{2,6},{3,7},{4,0},{5,1},{6,2},{7,3},{8,12},{9,13},{10,... | collective-permute-start | bytes 270344 | tf_op jit(solution)/shard_map/ppermute | solution.py:311
  5.0 4.4 %collective-permute-start = (bf16[22,8,256]{2,1,0:T(8,128)(2,1)S(1)}, bf16[22,8,256]{2,1,0:T(8,128)(2,1)S(1)}, u32[]{:S(2)}, u32[]{:S(2)}) collective-permute-start(bf16[22,8,256]{2,1,0:T(8,128)(2,1)S(1)} %get-tuple-element.18.after_any.own_ref), channel_id=1, source_target_pairs={{0,2},{1,3},{2,0},{3,1},{4,6},{5,7},{6,4},{7,5},{8,10},{9,11},{10,... | collective-permute-start | bytes 270344 | tf_op jit(solution)/shard_map/ppermute | solution.py:311
  9.4 8.5 %collective-permute-start.3 = (bf16[81,8,256]{2,1,0:T(8,128)(2,1)S(1)}, bf16[81,8,256]{2,1,0:T(8,128)(2,1)S(1)}, u32[]{:S(2)}, u32[]{:S(2)}) collective-permute-start(bf16[81,8,256]{2,1,0:T(8,128)(2,1)S(1)} %get-tuple-element.21), channel_id=1, source_target_pairs={{0,8},{1,9},{2,10},{3,11},{4,12},{5,13},{6,14},{7,15},{8,0},{9,1},... | collective-permute-start | bytes 995336 | tf_op jit(solution)/shard_map/ppermute | solution.py:311
  11.1 11.9 %collective-permute-start.4 = (bf16[81,8,256]{2,1,0:T(8,128)(2,1)S(1)}, bf16[81,8,256]{2,1,0:T(8,128)(2,1)S(1)}, u32[]{:S(2)}, u32[]{:S(2)}) collective-permute-start(bf16[81,8,256]{2,1,0:T(8,128)(2,1)S(1)} %get-tuple-element.21), channel_id=1, source_target_pairs={{8,16},{9,17},{10,18},{11,19},{12,20},{13,21},{14,22},{15,23},{16,... | collective-permute-start | bytes 995336 | tf_op jit(solution)/shard_map/ppermute | solution.py:311
  17.9 5.2 %collective-permute-start.5 = (f32[8,128]{1,0:T(8,128)S(1)}, f32[8,128]{1,0:T(8,128)S(1)}, u32[]{:S(2)}, u32[]{:S(2)}) collective-permute-start(f32[8,128]{1,0:T(8,128)S(1)} %add_bitcast_fusion), channel_id=1, source_target_pairs={{0,16},{1,17},{2,18},{3,19},{4,20},{5,21},{6,22},{7,23},{8,24},{9,... | collective-permute-start | bytes 12296 | tf_op jit(solution)/shard_map/ppermute | solution.py:311
  23.1 5.8 %collective-permute-start.6 = (bf16[168,8,256]{2,1,0:T(8,128)(2,1)S(1)}, bf16[168,8,256]{2,1,0:T(8,128)(2,1)S(1)}, u32[]{:S(2)}, u32[]{:S(2)}) collective-permute-start(bf16[168,8,256]{2,1,0:T(8,128)(2,1)S(1)} %pack.1.after_any.same_any), channel_id=1, source_target_pairs={{0,1},{1,0},{2,3},{3,2},{4,5},{5,4},{6,7},{7,6},{8,9},{9,8},{10,11... | collective-permute-start | bytes 2064392 | tf_op jit(solution)/shard_map/ppermute | solution.py:311

commit v6 on v5

--- a/solution.py
+++ b/solution.py
@@ -18,9 +18,10 @@
 PER_ROW = LEAF // RANK
 Q_ROW = BOXES
 LIFT_ROW = Q_ROW + BOXES // PER_ROW
-ROWS = LIFT_ROW + 2
+ROWS = LIFT_ROW + 1
 Z_ROWS = CHIPS * LIFT_ROW + 1
-ALL_ROWS = CHIPS * (ROWS + LIFT_ROW)
+SUM_ROW = CHIPS * ROWS
+ALL_ROWS = SUM_ROW + 1 + CHIPS * LIFT_ROW
 MIB = 1024 * 1024
 
 F32 = jnp.float32
@@ -64,6 +65,7 @@
     block_ref,
     place_ref,
     weight_ref,
+    zero_ref,
     near,
     far,
     count,
@@ -97,7 +99,7 @@
         apart = ((box >> 4) & 1) ^ core
         beside = ((box >> 7) != line).astype(I32)
         chip = ((box >> 5) & 3) ^ home
-        start = jnp.where(beside == 1, CHIPS * ROWS + LIFT_ROW * chip, ROWS * chip)
+        start = jnp.where(beside == 1, SUM_ROW + 1 + LIFT_ROW * chip, ROWS * chip)
         place = (apart << 12) | (start << 4) | (box & 15)
         place_ref[first : first + box.shape[0], 0:BOXES] = place
     used = iota((NEAR, BOXES), 0) < jnp.broadcast_to(count[...].reshape(1, BOXES), (NEAR, BOXES))
@@ -118,8 +120,8 @@
 
     for j in range(PER_ROW):
         put(Q_ROW + j, [coefficients[PER_ROW * g + j].astype(F32) for g in range(PER_ROW)])
-    put(LIFT_ROW, lifted[:4])
-    put(LIFT_ROW + 1, [lifted[4], nothing, nothing, nothing])
+    put(LIFT_ROW, lifted[1:])
+    zero_ref[...] = jnp.concatenate([lifted[0], nothing], axis=1)
 
 
 def join_kernel(ready_any, own_ref, first_ref, second_ref, third_ref, line_ref, z_ref):
@@ -127,23 +129,20 @@
     for k, ref in enumerate(refs):
         line_ref[k * ROWS : (k + 1) * ROWS] = ref[...]
         z_ref[k * LIFT_ROW : (k + 1) * LIFT_ROW] = ref[:LIFT_ROW]
-    sums = [
-        sum(ref[row, :, lanes].astype(F32) for ref in refs)
-        for row, lanes in ((LIFT_ROW, slice(128, LEAF)), (LIFT_ROW + 1, slice(0, 128)))
-    ]
-    z_ref[CHIPS * LIFT_ROW] = jnp.concatenate(sums, axis=1).astype(BF16)
-
-
-def pack_kernel(me_ref, line_ref, up_ref, down_ref, top, out_ref):
+    sums = sum(ref[LIFT_ROW, :, 128:].astype(F32) for ref in refs)
+    z_ref[CHIPS * LIFT_ROW] = jnp.concatenate([sums, jnp.zeros_like(sums)], axis=1).astype(BF16)
+
+
+def pack_kernel(me_ref, line_ref, up_ref, down_ref, top, zero, out_ref):
     me = me_ref[0]
     home, core = me & 7, me & 1
     prev_is_up = ((me >> 3) & 1) == 1
-    out_ref[: CHIPS * ROWS] = line_ref[...]
+    out_ref[:SUM_ROW] = line_ref[...]
     for k in range(CHIPS):
         use_prev = (home ^ (2 * k)) > home if k else core == 1
         use_up = use_prev == prev_is_up
         rows = slice(k * LIFT_ROW, (k + 1) * LIFT_ROW)
-        first = CHIPS * ROWS + k * LIFT_ROW
+        first = SUM_ROW + 1 + k * LIFT_ROW
 
         @pl.when(use_up)
         def _():
@@ -154,10 +153,8 @@
             out_ref[first : first + LIFT_ROW] = down_ref[rows]
 
     low = iota((RHS, 128), 1) < RANK
-    third = up_ref[CHIPS * LIFT_ROW, :, :128].astype(F32)
-    mixed = jnp.where(low, line_ref[LIFT_ROW, :, 128:].astype(F32), third)
-    out_ref[LIFT_ROW, :, 128:] = mixed.astype(BF16)
-    out_ref[LIFT_ROW + 1, :, :128] = top[...].astype(BF16)
+    sums = jnp.where(low, up_ref[CHIPS * LIFT_ROW, :, :128].astype(F32), top[...])
+    out_ref[SUM_ROW] = jnp.concatenate([sums, zero[...]], axis=1).astype(BF16)
 
 
 def own_kernel(weight_any, after_any, vectors_any, tiles_any, near_ref, weight, vectors, mine, sems):
@@ -249,27 +246,29 @@
         half, start, box = entry(row, b)
         return window[half, start + box]
 
-    def levels(half, k, level):
-        row, lane = LIFT_ROW + level // PER_ROW, level % PER_ROW * RANK
-        return window[half, k * ROWS + row].astype(F32)[:, lane : lane + RANK]
-
-    for first in range(0, BOXES, 2):
+    def levels(half, row, lane):
+        return window[half, row].astype(F32)[:, lane * RANK : (lane + 1) * RANK]
+
+    def lifts(half, k, level):
+        return levels(half, k * ROWS + LIFT_ROW, level - 1)
+
+    for first in range(0, BOXES, 4):
         parts = [
             [nt(vectors(s, b), tiles[b, s - 1]) for s in range(1, NEAR)]
-            for b in range(first, first + 2)
+            for b in range(first, first + 4)
         ]
-        for b in range(first, first + 2):
+        for b in range(first, first + 4):
             total = near[b]
             for s in range(1, NEAR):
                 total = total + weight[s, b] * parts[b - first][s - 1]
             out[b] = total
 
     groups = [
-        levels(1, 0, 0),
-        levels(0, 1, 1) + levels(1, 1, 1),
-        levels(0, 2, 2) + levels(1, 2, 2) + levels(0, 3, 2) + levels(1, 3, 2),
-        levels(0, 0, 3) + levels(1, 0, 3),
-        levels(0, 0, 4) + levels(1, 0, 4),
+        levels(1, SUM_ROW, 2),
+        lifts(0, 1, 1) + lifts(1, 1, 1),
+        lifts(0, 2, 2) + lifts(1, 2, 2) + lifts(0, 3, 2) + lifts(1, 3, 2),
+        levels(0, SUM_ROW, 0) + levels(1, SUM_ROW, 0),
+        levels(0, SUM_ROW, 1) + levels(1, SUM_ROW, 1),
     ]
     far_field = jnp.zeros((RHS, RANK), F32)
     for k in range(UP):
@@ -295,10 +294,10 @@
     outs = []
     for b in range(BOXES):
         out[b] = out[b] + nn(leaves[b], basis[b])
-        if b % 8 == 7:
-            rows = pl.ds(b - 7, 8)
+        if b % 4 == 3:
+            rows = pl.ds(b - 3, 4)
             outs.append(
-                pltpu.make_async_copy(out.at[rows], out_any.at[rows], out_sems.at[b // 8])
+                pltpu.make_async_copy(out.at[rows], out_any.at[rows], out_sems.at[b // 4])
             )
             outs[-1].start()
     for copy in outs:
@@ -333,15 +332,16 @@
     def off(x):
         return pltpu.with_memory_space_constraint(x, pltpu.HBM)
 
-    block, place, weight = pl.pallas_call(
+    block, place, weight, zero = pl.pallas_call(
         front_kernel,
         out_shape=(
             shape_of((ROWS, RHS, LEAF), BF16),
             shape_of((BOXES, 128), I32),
             shape_of((8, 128), F32),
+            shape_of((RHS, 128), F32),
         ),
         in_specs=[SMEM] + [ANY] * 8,
-        out_specs=(VMEM,) * 3,
+        out_specs=(VMEM,) * 4,
         scratch_shapes=[
             pltpu.VMEM((NEAR, BOXES), I32),
             pltpu.VMEM((FAR, BOXES), I32),
@@ -414,16 +414,16 @@
 
     up = pairwise(z_line, lambda i: LINE * partner_up(i // LINE) + i % LINE)
     down = pairwise(z_line, lambda i: LINE * partner_down(i // LINE) + i % LINE)
-    tops = z_line[-1, :, 128:].astype(F32) + up[-1, :, 128:].astype(F32)
+    tops = z_line[-1, :, :128].astype(F32) + up[-1, :, :128].astype(F32)
     top = pairwise(tops, lambda i: i ^ (2 * LINE))
     same = pl.pallas_call(
         pack_kernel,
         out_shape=shape_of((ALL_ROWS, RHS, LEAF), BF16),
-        in_specs=[SMEM] + [VMEM] * 4,
+        in_specs=[SMEM] + [VMEM] * 5,
         out_specs=VMEM,
         compiler_params=pltpu.CompilerParams(vmem_limit_bytes=4 * MIB),
         name="pack",
-    )(me, line, up, down, top)
+    )(me, line, up, down, top, zero)
     other = pairwise(same, lambda i: i ^ 1)
 
     near = pl.pallas_call(
@@ -452,7 +452,7 @@
             pltpu.SMEM((8, 128), F32),
             pltpu.VMEM((BOXES, RHS, LEAF), F32),
             pltpu.SemaphoreType.DMA((4,)),
-            pltpu.SemaphoreType.DMA((2,)),
+            pltpu.SemaphoreType.DMA((4,)),
         ],
         compiler_params=pltpu.CompilerParams(vmem_limit_bytes=16 * MIB),
         name="final",

time: 32.9 us -> 32.9 us (level)
  no operation moved by 1% of the time
where the time goes in v6:
time: 32.9 us; the launch traced here: 32.8 us
  starting transfers between devices  17 us (52%)
  Pallas kernels  11.3 us (34%)
  waiting for transfers between devices  4.41 us (13%)
    ppermute x7, starting transfers between devices, pairwise(): return lax.ppermute(block, 'pts', route)  17 us
    ppermute x7, waiting for transfers between devices, pairwise(): return lax.ppermute(block, 'pts', route)  4.41 us
    pallas_call x1, Pallas kernels, per_device(): pl.pallas_call(final_kernel, out_shape=shape_of((BOXES, RHS, LEAF), F32),...  3.89 us
    pallas_call x1, Pallas kernels, per_device(): pl.pallas_call(stage_kernel, out_shape=(pltpu.VMEM((BOXES, NEAR - 1, LEAF...  3.22 us
    pallas_call x1, Pallas kernels, per_device(): pl.pallas_call(own_kernel, out_shape=shape_of((BOXES, RHS, LEAF), F32), i...  2.14 us
    pallas_call x1, Pallas kernels, per_device(): pl.pallas_call(front_kernel, out_shape=(shape_of((ROWS, RHS, LEAF), BF16)...  1.89 us
  transfers between devices with their start and end apart: 7, of which 2 were waited for; matrix products, arithmetic and copies ran while one was open for 0% of the time, Pallas kernels for 16%

profile of v6, /device:TPU:25, one launch (start us, length us, event | category | flops | bytes accessed | tf_op | source)
XLA Modules:
  0.0 32.8 jit_solution(2317611485667441303)
XLA Ops:
  0.0 1.9 %front.1 = (bf16[21,8,256]{2,1,0:T(8,128)(2,1)S(1)}, s32[16,128]{1,0:T(8,128)S(1)}, f32[8,128]{1,0:T(8,128)S(1)}, f32[8,128]{1,0:T(8,128)S(1)}) custom-call(s32[1]{0:T(128)} %bitcast.me_ref, s32[4,16]{1,0:T(4,128)} %bitcast.7, s32[6,16]{1,0:T(8,128)} %bitcast.6, s32[16]{0:T(128)} %count_any.1, f32[4,16]{1,0:T(4,128)} %bitcast.8, ...), custom_call_target="tpu_custom_call" | custom-call | tf_op jit(solution)/shard_map/front/pallas_call | solution.py:335
  1.9 2.6 %collective-permute-start.2 = (bf16[21,8,256]{2,1,0:T(8,128)(2,1)S(1)}, bf16[21,8,256]{2,1,0:T(8,128)(2,1)S(1)}, u32[]{:S(2)}, u32[]{:S(2)}) collective-permute-start(bf16[21,8,256]{2,1,0:T(8,128)(2,1)S(1)} %get-tuple-element.19.after_any.own_ref), channel_id=1, source_target_pairs={{0,6},{1,7},{2,4},{3,5},{4,2},{5,3},{6,0},{7,1},{8,14},{9,15},{10,... | collective-permute-start | bytes 258056 | tf_op jit(solution)/shard_map/ppermute | solution.py:310
  4.5 0.5 %collective-permute-start.1 = (bf16[21,8,256]{2,1,0:T(8,128)(2,1)S(1)}, bf16[21,8,256]{2,1,0:T(8,128)(2,1)S(1)}, u32[]{:S(2)}, u32[]{:S(2)}) collective-permute-start(bf16[21,8,256]{2,1,0:T(8,128)(2,1)S(1)} %get-tuple-element.19.after_any.own_ref), channel_id=1, source_target_pairs={{0,4},{1,5},{2,6},{3,7},{4,0},{5,1},{6,2},{7,3},{8,12},{9,13},{10,... | collective-permute-start | bytes 258056 | tf_op jit(solution)/shard_map/ppermute | solution.py:310
  5.0 0.2 collective-permute-start
  5.2 3.2 %stage.1 = (bf16[16,3,256,256]{3,2,1,0:T(8,128)(2,1)S(1)}, bf16[16,64,256]{2,1,0:T(8,128)(2,1)S(1)}, bf16[16,64,64]{2,1,0:T(8,128)(2,1)S(1)}, bf16[16,64,384]{2,...) custom-call(bf16[21,8,256]{2,1,0:T(8,128)(2,1)S(1)} %get-tuple-element.19.after_any.own_ref, ...), custom_call_target="tpu_custom_call" | custom-call | tf_op jit(solution)/shard_map/stage/pallas_call | solution.py:370
  8.5 0.0 collective-permute-done.2.third_ref
  8.5 0.8 %collective-permute-done.1.second_ref = bf16[21,8,256]{2,1,0:T(8,128)(2,1)S(1)} collective-permute-done((bf16[21,8,256]{2,1,0:T(8,128)(2,1)S(1)}, bf16[21,8,256]{2,1,0:T(8,128)(2,1)S(1)}, u32[]{:S(2)}, u32[]{:S(2)}) %collective-permute-start.1) | collective-permute-done | bytes 86048 | tf_op jit(solution)/shard_map/ppermute | solution.py:310
  9.3 0.0 collective-permute-done.first_ref
  9.4 1.7 %collective-permute-start.3 = (bf16[81,8,256]{2,1,0:T(8,128)(2,1)S(1)}, bf16[81,8,256]{2,1,0:T(8,128)(2,1)S(1)}, u32[]{:S(2)}, u32[]{:S(2)}) collective-permute-start(bf16[81,8,256]{2,1,0:T(8,128)(2,1)S(1)} %get-tuple-element.22), channel_id=1, source_target_pairs={{0,8},{1,9},{2,10},{3,11},{4,12},{5,13},{6,14},{7,15},{8,0},{9,1},... | collective-permute-start | bytes 995336 | tf_op jit(solution)/shard_map/ppermute | solution.py:310
  11.1 6.7 %collective-permute-start.4 = (bf16[81,8,256]{2,1,0:T(8,128)(2,1)S(1)}, bf16[81,8,256]{2,1,0:T(8,128)(2,1)S(1)}, u32[]{:S(2)}, u32[]{:S(2)}) collective-permute-start(bf16[81,8,256]{2,1,0:T(8,128)(2,1)S(1)} %get-tuple-element.22), channel_id=1, source_target_pairs={{8,16},{9,17},{10,18},{11,19},{12,20},{13,21},{14,22},{15,23},{16,... | collective-permute-start | bytes 995336 | tf_op jit(solution)/shard_map/ppermute | solution.py:310
  17.8 0.0 collective-permute-done.3.up_ref
  17.9 1.7 %collective-permute-start.5 = (f32[8,128]{1,0:T(8,128)S(1)}, f32[8,128]{1,0:T(8,128)S(1)}, u32[]{:S(2)}, u32[]{:S(2)}) collective-permute-start(f32[8,128]{1,0:T(8,128)S(1)} %add_bitcast_fusion), channel_id=1, source_target_pairs={{0,16},{1,17},{2,18},{3,19},{4,20},{5,21},{6,22},{7,23},{8,24},{9,... | collective-permute-start | bytes 12296 | tf_op jit(solution)/shard_map/ppermute | solution.py:310
  19.5 3.6 %collective-permute-done.4.down_ref = bf16[81,8,256]{2,1,0:T(8,128)(2,1)S(1)} collective-permute-done((bf16[81,8,256]{2,1,0:T(8,128)(2,1)S(1)}, bf16[81,8,256]{2,1,0:T(8,128)(2,1)S(1)}, u32[]{:S(2)}, u32[]{:S(2)}) %collective-permute-start.4) | collective-permute-done | bytes 331808 | tf_op jit(solution)/shard_map/ppermute | solution.py:310
  23.1 0.0 collective-permute-done.5.top
  23.1 0.1 pack.1.after_any.same_any
  23.2 3.5 %collective-permute-start.6 = (bf16[165,8,256]{2,1,0:T(8,128)(2,1)S(1)}, bf16[165,8,256]{2,1,0:T(8,128)(2,1)S(1)}, u32[]{:S(2)}, u32[]{:S(2)}) collective-permute-start(bf16[165,8,256]{2,1,0:T(8,128)(2,1)S(1)} %pack.1.after_any.same_any), channel_id=1, source_target_pairs={{0,1},{1,0},{2,3},{3,2},{4,5},{5,4},{6,7},{7,6},{8,9},{9,8},{10,11... | collective-permute-start | bytes 2027528 | tf_op jit(solution)/shard_map/ppermute | solution.py:310
  26.7 2.1 %own.1.near = f32[16,8,256]{2,1,0:T(8,128)S(1)} custom-call(f32[8,128]{1,0:T(8,128)S(1)} %get-tuple-element.18.weight_any, bf16[165,8,256]{2,1,0:T(8,128)(2,1)S(1)} %pack.1.after_any.same_any, bf16[16,8,256]{2,1,0:T(8,128)(2,1)} %vectors_any.3, bf16[16,4,256,256]{3,2,1,0:T(8,128)(2,1)} %tiles_any.3), custom_call_target="tpu_custom_call" | custom-call | tf_op jit(solution)/shard_map/own/pallas_call | solution.py:429
  28.9 0.0 collective-permute-done.6.other_any
  28.9 3.9 %final.1 = f32[16,8,256]{2,1,0:T(8,128)} custom-call(s32[16,128]{1,0:T(8,128)S(1)} %get-tuple-element.17.place_any, f32[8,128]{1,0:T(8,128)S(1)} %get-tuple-element.18.weight_any, bf16[165,8,256]{2,1,0:T(8,128)(2,1)S(1)} %pack.1.after_any.same_any, bf16[165,8,256]{2,1,0:T(8,128)(2,1)S(1)} %collective-permute-done.6.other_any, f32[16,8,256]{2,1,0:T(8,128)S(1)} %own.1.near, ...), custom_call_target="tpu_custom_call" | custom-call | tf_op jit(solution)/shard_map/final/pallas_call | solution.py:444
  (2 shorter events, 0.1 us)
Async XLA Ops:
  1.9 6.6 %collective-permute-start.2 = (bf16[21,8,256]{2,1,0:T(8,128)(2,1)S(1)}, bf16[21,8,256]{2,1,0:T(8,128)(2,1)S(1)}, u32[]{:S(2)}, u32[]{:S(2)}) collective-permute-start(bf16[21,8,256]{2,1,0:T(8,128)(2,1)S(1)} %get-tuple-element.19.after_any.own_ref), channel_id=1, source_target_pairs={{0,6},{1,7},{2,4},{3,5},{4,2},{5,3},{6,0},{7,1},{8,14},{9,15},{10,... | collective-permute-start | bytes 258056 | tf_op jit(solution)/shard_map/ppermute | solution.py:310
  4.5 4.8 %collective-permute-start.1 = (bf16[21,8,256]{2,1,0:T(8,128)(2,1)S(1)}, bf16[21,8,256]{2,1,0:T(8,128)(2,1)S(1)}, u32[]{:S(2)}, u32[]{:S(2)}) collective-permute-start(bf16[21,8,256]{2,1,0:T(8,128)(2,1)S(1)} %get-tuple-element.19.after_any.own_ref), channel_id=1, source_target_pairs={{0,4},{1,5},{2,6},{3,7},{4,0},{5,1},{6,2},{7,3},{8,12},{9,13},{10,... | collective-permute-start | bytes 258056 | tf_op jit(solution)/shard_map/ppermute | solution.py:310
  5.0 4.3 %collective-permute-start = (bf16[21,8,256]{2,1,0:T(8,128)(2,1)S(1)}, bf16[21,8,256]{2,1,0:T(8,128)(2,1)S(1)}, u32[]{:S(2)}, u32[]{:S(2)}) collective-permute-start(bf16[21,8,256]{2,1,0:T(8,128)(2,1)S(1)} %get-tuple-element.19.after_any.own_ref), channel_id=1, source_target_pairs={{0,2},{1,3},{2,0},{3,1},{4,6},{5,7},{6,4},{7,5},{8,10},{9,11},{10,... | collective-permute-start | bytes 258056 | tf_op jit(solution)/shard_map/ppermute | solution.py:310
  9.4 8.5 %collective-permute-start.3 = (bf16[81,8,256]{2,1,0:T(8,128)(2,1)S(1)}, bf16[81,8,256]{2,1,0:T(8,128)(2,1)S(1)}, u32[]{:S(2)}, u32[]{:S(2)}) collective-permute-start(bf16[81,8,256]{2,1,0:T(8,128)(2,1)S(1)} %get-tuple-element.22), channel_id=1, source_target_pairs={{0,8},{1,9},{2,10},{3,11},{4,12},{5,13},{6,14},{7,15},{8,0},{9,1},... | collective-permute-start | bytes 995336 | tf_op jit(solution)/shard_map/ppermute | solution.py:310
  11.1 12.0 %collective-permute-start.4 = (bf16[81,8,256]{2,1,0:T(8,128)(2,1)S(1)}, bf16[81,8,256]{2,1,0:T(8,128)(2,1)S(1)}, u32[]{:S(2)}, u32[]{:S(2)}) collective-permute-start(bf16[81,8,256]{2,1,0:T(8,128)(2,1)S(1)} %get-tuple-element.22), channel_id=1, source_target_pairs={{8,16},{9,17},{10,18},{11,19},{12,20},{13,21},{14,22},{15,23},{16,... | collective-permute-start | bytes 995336 | tf_op jit(solution)/shard_map/ppermute | solution.py:310
  17.9 5.3 %collective-permute-start.5 = (f32[8,128]{1,0:T(8,128)S(1)}, f32[8,128]{1,0:T(8,128)S(1)}, u32[]{:S(2)}, u32[]{:S(2)}) collective-permute-start(f32[8,128]{1,0:T(8,128)S(1)} %add_bitcast_fusion), channel_id=1, source_target_pairs={{0,16},{1,17},{2,18},{3,19},{4,20},{5,21},{6,22},{7,23},{8,24},{9,... | collective-permute-start | bytes 12296 | tf_op jit(solution)/shard_map/ppermute | solution.py:310
  23.2 5.7 %collective-permute-start.6 = (bf16[165,8,256]{2,1,0:T(8,128)(2,1)S(1)}, bf16[165,8,256]{2,1,0:T(8,128)(2,1)S(1)}, u32[]{:S(2)}, u32[]{:S(2)}) collective-permute-start(bf16[165,8,256]{2,1,0:T(8,128)(2,1)S(1)} %pack.1.after_any.same_any), channel_id=1, source_target_pairs={{0,1},{1,0},{2,3},{3,2},{4,5},{5,4},{6,7},{7,6},{8,9},{9,8},{10,11... | collective-permute-start | bytes 2027528 | tf_op jit(solution)/shard_map/ppermute | solution.py:310
